TPU v7x, 32 devices: a whole 2x2x4 slice. The times are simulated.
32 devices in a mesh: dp: 4 (over y, core), fsdp: 8 (over z, x).
Axes of the slice: x: 2, y: 2, z: 4, core: 2. Of those that a mesh axis runs over, the one named last changes fastest.
Arguments:
- acts: bfloat16 [4096, 8192], P(('dp', 'fsdp')), may hold values from -3 to 3
- out_grads: bfloat16 [4096, 8192], P(('dp', 'fsdp')), may hold values from -6 to 6
- token_counts: int32 [4], replicated, may hold values from 512 to 1024, as said below
- k_factor: float32 [32, 256, 512], P('fsdp'), may hold values from -0.1875 to 2.44
- c_factor: float32 [32, 256, 512], P('fsdp'), may hold values from -0.1875 to 2.44
- k_moment: float32 [32, 256, 512], P('fsdp'), may hold values from -0.046875 to 0.946875
- c_moment: float32 [32, 256, 512], P('fsdp'), may hold values from -0.046875 to 0.946875
- grad_weight: bfloat16 [8192, 8192], P('dp', 'fsdp'), may hold values from -6 to 6
Outputs:
- k_factor_new: float32 [32, 256, 512], P('fsdp')
- c_factor_new: float32 [32, 256, 512], P('fsdp')
- k_moment_new: float32 [32, 256, 512], P('fsdp')
- c_moment_new: float32 [32, 256, 512], P('fsdp')
- precond: bfloat16 [8192, 8192], P('dp', 'fsdp')
Inputs may be any that keep to these rules, and one draw needn't show every extreme that they name: `token_counts`: some data group has all 1024 slots valid and some other has exactly 512.
All inputs are finite; a program needn't handle non-finite values.
Results may differ from a plain program's by a relative error of at most 0.0081.
Values may be sent and summed in bfloat16 or wider, within the bound.
No kernel may reach another device: no remote copies, remote signals or barrier semaphores. Data moves between devices by JAX's collectives and lax.ppermute only.
A program may use at most 128 MiB of HBM per device.

v0:
```python
import jax
import jax.numpy as jnp
from jax import lax
from jax.sharding import PartitionSpec as P

damping = 0.1
momentum_rate = 0.5
step_rate = 0.2
highest = lax.Precision.HIGHEST


def spread(value, axis, source):
    kept = jnp.where(lax.axis_index(axis) == source, value, 0).astype(value.dtype)
    return lax.psum(kept, axis)


def owner_image(columns, lead_columns, diag_half, side_half):
    row_count = columns.shape[0]
    block_count = diag_half.shape[0]
    block_size = diag_half.shape[1]
    blocked = columns.reshape(row_count, block_count, block_size)
    image_sum = jnp.einsum("tnk,nkj->tnj", blocked, diag_half, preferred_element_type=jnp.float32)
    image_sum = image_sum + jnp.einsum(
        "tk,nkj->tnj", lead_columns, side_half, preferred_element_type=jnp.float32
    )
    return image_sum.astype(jnp.bfloat16).reshape(row_count, block_count * block_size)


def to_owners(pair):
    return (
        lax.all_to_all(pair[0], "fsdp", split_axis=1, concat_axis=0, tiled=True),
        lax.all_to_all(pair[1], "fsdp", split_axis=1, concat_axis=0, tiled=True),
    )


def fetch_lead(before):
    return (
        lax.all_gather(before[0], "fsdp", axis=0, tiled=True),
        lax.all_gather(before[1], "fsdp", axis=0, tiled=True),
    )


def block_stats(owned, lead_image, block_count, block_size):
    blocked = owned.reshape(owned.shape[0], block_count, block_size)
    own_sum = jnp.einsum("tni,tnj->nij", blocked, blocked, preferred_element_type=jnp.float32)
    cross_sum = jnp.einsum("ti,tnj->nij", lead_image, blocked, preferred_element_type=jnp.float32)
    return (own_sum, cross_sum)


def gram_trace(factor, border_keep):
    block_size = factor.shape[1]
    diag_part = factor[:, :, :block_size]
    side_part = factor[:, :, block_size:] * border_keep
    return jnp.sum(diag_part * diag_part) + jnp.sum(side_part * side_part)


def advance(factor, moment, own_sum, cross_sum, lead_block, border_keep, other_h, other_g, width):
    block_size = factor.shape[1]
    diag_part = factor[:, :, :block_size]
    side_part = factor[:, :, block_size:] * border_keep
    gram_diag = jnp.einsum("nki,nkj->nij", diag_part, diag_part, precision=highest)
    gram_diag = gram_diag + jnp.einsum("nki,nkj->nij", side_part, side_part, precision=highest)
    gram_side = jnp.einsum("ki,nkj->nij", lead_block, side_part, precision=highest)
    identity = jnp.eye(block_size, dtype=jnp.float32)
    fresh_diag = (other_h * own_sum + damping * other_g * gram_diag - width * identity) / (
        2.0 * width
    )
    fresh_side = (other_h * cross_sum + damping * other_g * gram_side) * border_keep / (2.0 * width)
    moment_diag = momentum_rate * moment[:, :, :block_size] + fresh_diag
    moment_side = (momentum_rate * moment[:, :, block_size:] + fresh_side) * border_keep
    new_diag = diag_part - step_rate * jnp.einsum(
        "nik,nkj->nij", diag_part, moment_diag, precision=highest
    )
    side_change = jnp.einsum("ik,nkj->nij", lead_block, moment_side, precision=highest)
    side_change = side_change + jnp.einsum(
        "nik,nkj->nij", side_part, moment_diag, precision=highest
    )
    new_side = (side_part - step_rate * side_change) * border_keep
    return (
        jnp.concatenate([new_diag, new_side], axis=-1),
        jnp.concatenate([moment_diag, moment_side], axis=-1),
    )


def per_device(acts, out_grads, token_counts, k_factor, c_factor, k_moment, c_moment, grad_weight):
    tok_dev, width = acts.shape
    blocks_dev = k_factor.shape[0]
    block_size = k_factor.shape[1]
    group_count = lax.axis_size("dp")
    shard_count = lax.axis_size("fsdp")
    group_id = lax.axis_index("dp")
    shard_id = lax.axis_index("fsdp")
    token_total = jnp.sum(token_counts).astype(jnp.float32)
    valid_limit = jnp.sum(jnp.where(lax.iota(jnp.int32, group_count) == group_id, token_counts, 0))
    positions = shard_id * tok_dev + lax.iota(jnp.int32, tok_dev)
    row_keep = (positions < valid_limit).astype(jnp.bfloat16)[:, None]
    masked_acts = acts * row_keep
    masked_grads = out_grads * row_keep
    block_ids = shard_id * blocks_dev + lax.iota(jnp.int32, blocks_dev)
    border_keep = (block_ids > 0).astype(jnp.float32)[:, None, None]
    lead_k, lead_c = (
        spread(k_factor[0, :, :block_size], "fsdp", 0),
        spread(c_factor[0, :, :block_size], "fsdp", 0),
    )
    raw_acts, raw_grads = to_owners((masked_acts, masked_grads))
    lead_raw_acts, lead_raw_grads = fetch_lead(
        (masked_acts[:, :block_size], masked_grads[:, :block_size])
    )
    k_diag_half = k_factor[:, :, :block_size].astype(jnp.bfloat16)
    k_side_half = (k_factor[:, :, block_size:] * border_keep).astype(jnp.bfloat16)
    c_diag_half = c_factor[:, :, :block_size].astype(jnp.bfloat16)
    c_side_half = (c_factor[:, :, block_size:] * border_keep).astype(jnp.bfloat16)
    owned_acts = owner_image(raw_acts, lead_raw_acts, k_diag_half, k_side_half)
    owned_grads = owner_image(raw_grads, lead_raw_grads, c_diag_half, c_side_half)
    lead_acts = jnp.dot(
        lead_raw_acts, lead_k.astype(jnp.bfloat16), preferred_element_type=jnp.float32
    ).astype(jnp.bfloat16)
    lead_grads = jnp.dot(
        lead_raw_grads, lead_c.astype(jnp.bfloat16), preferred_element_type=jnp.float32
    ).astype(jnp.bfloat16)
    own_k, cross_k = block_stats(owned_acts, lead_acts, blocks_dev, block_size)
    own_c, cross_c = block_stats(owned_grads, lead_grads, blocks_dev, block_size)
    summed = lax.psum((own_k, cross_k, own_c, cross_c), "dp")
    gram_k = gram_trace(k_factor, border_keep)
    gram_c = gram_trace(c_factor, border_keep)
    local_traces = jnp.stack(
        [
            jnp.sum(jnp.trace(summed[0], axis1=1, axis2=2)),
            jnp.sum(jnp.trace(summed[2], axis1=1, axis2=2)),
            gram_k,
            gram_c,
        ]
    )
    totals = lax.psum(local_traces, "fsdp")
    trace_hk = totals[0] / token_total
    trace_hc = totals[1] / token_total
    scale_width = float(width)
    k_factor_new, k_moment_new = advance(
        k_factor,
        k_moment,
        summed[0] / token_total,
        summed[1] / token_total,
        lead_k,
        border_keep,
        trace_hc,
        totals[3],
        scale_width,
    )
    c_factor_new, c_moment_new = advance(
        c_factor,
        c_moment,
        summed[2] / token_total,
        summed[3] / token_total,
        lead_c,
        border_keep,
        trace_hk,
        totals[2],
        scale_width,
    )
    grad_rows = grad_weight.shape[0]
    grad_lead = spread(grad_weight[:, :block_size], "fsdp", 0)
    k_diag = k_factor_new[:, :, :block_size].astype(jnp.bfloat16)
    k_side = k_factor_new[:, :, block_size:].astype(jnp.bfloat16)
    grad_blocked = grad_weight.reshape(grad_rows, blocks_dev, block_size)
    first_sum = jnp.einsum("rnk,nkj->rnj", grad_blocked, k_diag, preferred_element_type=jnp.float32)
    first_sum = first_sum + jnp.einsum(
        "rk,nkj->rnj", grad_lead, k_side, preferred_element_type=jnp.float32
    )
    first_product = first_sum.astype(jnp.bfloat16)
    own_second = jnp.einsum(
        "rnk,njk->rnj", first_product, k_diag, preferred_element_type=jnp.float32
    )
    lead_term = jnp.einsum("rnk,njk->rj", first_product, k_side, preferred_element_type=jnp.float32)
    lead_sum = lax.psum(lead_term, "fsdp")
    lead_mask = (block_ids == 0).astype(jnp.float32)[None, :, None]
    second_product = (own_second + lead_mask * lead_sum[:, None, :]).astype(jnp.bfloat16)
    row_blocks = grad_rows // block_size
    owner_count = shard_count // group_count
    c_half = c_factor_new.astype(jnp.bfloat16)
    fetched = []
    for owner_step in range(owner_count):
        fetched.append(spread(c_half, "fsdp", group_id * owner_count + owner_step))
    row_factor = jnp.concatenate(fetched, axis=0)
    c_diag = row_factor[:, :, :block_size]
    c_side = row_factor[:, :, block_size:]
    by_rows = second_product.reshape(row_blocks, block_size, blocks_dev * block_size)
    lead_rows = spread(by_rows[0], "dp", 0)
    third_sum = jnp.einsum("nki,nkc->nic", c_diag, by_rows, preferred_element_type=jnp.float32)
    third_sum = third_sum + jnp.einsum(
        "nki,kc->nic", c_side, lead_rows, preferred_element_type=jnp.float32
    )
    third_product = third_sum.astype(jnp.bfloat16)
    own_fourth = jnp.einsum(
        "nik,nkc->nic", c_diag, third_product, preferred_element_type=jnp.float32
    )
    row_term = jnp.einsum("nik,nkc->ic", c_side, third_product, preferred_element_type=jnp.float32)
    row_sum = lax.psum(row_term, "dp")
    row_ids = group_id * row_blocks + lax.iota(jnp.int32, row_blocks)
    row_mask = (row_ids == 0).astype(jnp.float32)[:, None, None]
    precond = (
        (own_fourth + row_mask * row_sum[None, :, :])
        .astype(jnp.bfloat16)
        .reshape(grad_rows, blocks_dev * block_size)
    )
    return (k_factor_new, c_factor_new, k_moment_new, c_moment_new, precond)


def solution(mesh):
    in_specs = (
        P(("dp", "fsdp"), None),
        P(("dp", "fsdp"), None),
        P(),
        P("fsdp", None, None),
        P("fsdp", None, None),
        P("fsdp", None, None),
        P("fsdp", None, None),
        P("dp", "fsdp"),
    )
    out_specs = (
        P("fsdp", None, None),
        P("fsdp", None, None),
        P("fsdp", None, None),
        P("fsdp", None, None),
        P("dp", "fsdp"),
    )
    return jax.shard_map(
        per_device, mesh=mesh, in_specs=in_specs, out_specs=out_specs, check_vma=False
    )
```

profile of v0, /device:TPU:17, one launch (start us, length us, event | category | flops | bytes accessed | tf_op | source)
XLA Modules:
  0.0 739.3 jit_solution(4585320828865927913)
XLA Ops:
  13.0 4.4 copy.205
  17.4 5.6 all-to-all-start.1
  25.4 42.0 %all-to-all-done.1 = bf16[128,8,1024]{0,2,1:T(8,128)(2,1)} async-done(((bf16[128,8,1024]{0,2,1:T(8,128)(2,1)}), bf16[128,8,1024]{0,2,1:T(8,128)(2,1)}, u32[]{:S(2)}, u32[]{:S(2)}) %all-to-all-start.1) | async-done | bytes 2097184 | tf_op jit(solution)/shard_map/all_to_all | solution.py:32
  67.4 7.9 %all-to-all-start = ((bf16[128,8,1024]{0,2,1:T(8,128)(2,1)}), bf16[128,8,1024]{0,2,1:T(8,128)(2,1)}, u32[]{:S(2)}, u32[]{:S(2)}) async-start(bf16[128,8,1024]{0,2,1:T(8,128)(2,1)} %bitcast.137), calls=%async_computation | async-start | bytes 4194304 | tf_op jit(solution)/shard_map/all_to_all | solution.py:31
  82.2 59.3 %all_gather.6 = bf16[1024,256]{1,0:T(8,128)(2,1)S(1)} all-gather(bf16[128,256]{1,0:T(8,128)(2,1)S(1)} %slice.89), channel_id=1, replica_groups=mesh['dp'=4,'fsdp'=8] {'fsdp'}, dimensions={0}, use_global_device_ids=true | all-gather | bytes 589824 | tf_op jit(solution)/shard_map/all_gather | solution.py:38
  141.6 25.9 %all_gather.7 = bf16[1024,256]{1,0:T(8,128)(2,1)S(1)} all-gather(bf16[128,256]{1,0:T(8,128)(2,1)S(1)} %slice.90), channel_id=1, replica_groups=mesh['dp'=4,'fsdp'=8] {'fsdp'}, dimensions={0}, use_global_device_ids=true | all-gather | bytes 589824 | tf_op jit(solution)/shard_map/all_gather | solution.py:39
  178.3 4.3 copy.117
  182.6 4.3 reshape.82
  202.6 10.7 %all-reduce.22.cloned.1.call-start = ((), (), s32[]{:S(2)}) async-start(), calls=%async_computation.7 | async-start | bytes 4718592 | tf_op jit(solution)/shard_map/psum | solution.py:14
  222.3 59.0 %all-reduce.24.cloned.1.call-done = (f32[4,256,256]{2,1,0:T(8,128)}, f32[4,256,256]{1,2,0:T(8,128)}, f32[4,256,256]{1,2,0:T(8,128)}) async-done(((f32[4,256,256]{2,1,0:T(8,128)}, f32[4,256,256]{1,2,0:T(8,128)}, f32[4,256,256]{1,2,0:T(8,128)}), (f32[4,256,256]{2,1,0:T(8,128)}, f32[4,256,256]{1,2,0:T(8,128)}, f32[4,256,256]{1,2,0:T(8,128)})) %all-reduce.24.cloned.1.call-update) | async-done | bytes 3145744 | tf_op jit(solution)/shard_map/psum | solution.py:123
  285.6 12.8 %psum.93 = f32[4]{0:T(128)S(1)} all-reduce(f32[4]{0:T(128)S(1)} %pad_maximum_fusion.4), channel_id=1, replica_groups=mesh['dp'=4,'fsdp'=8] {'fsdp'}, use_global_device_ids=true, to_apply=%region_9.10 | all-reduce | flops 4 | bytes 32 | tf_op jit(solution)/shard_map/psum | solution.py:134
  319.0 4.7 fusion.2
  323.7 38.9 %all-reduce.16.cloned.1.call-done = bf16[2048,256]{1,0:T(8,128)(2,1)} async-done(((bf16[2048,256]{1,0:T(8,128)(2,1)}), bf16[2048,256]{1,0:T(8,128)(2,1)}) %all-reduce.16.cloned.1.call-update) | async-done | bytes 1048592 | tf_op jit(solution)/shard_map/psum | solution.py:14
  362.6 5.0 fusion.1
  372.9 4.5 fusion.41
  383.5 99.0 %all-reduce.22.cloned.1.call-done = (f32[256,256]{1,0:T(8,128)}, f32[2048,256]{1,0:T(8,128)}) async-done(((f32[256,256]{1,0:T(8,128)}, f32[2048,256]{1,0:T(8,128)}), (f32[256,256]{1,0:T(8,128)}, f32[2048,256]{1,0:T(8,128)})) %all-reduce.22.cloned.1.call-update) | async-done | bytes 2359312 | tf_op jit(solution)/shard_map/psum | solution.py:14
  493.1 28.9 %all-reduce.14.cloned.1.call-done = f32[4,256,256]{1,2,0:T(8,128)} async-done(((f32[4,256,256]{1,2,0:T(8,128)}), f32[4,256,256]{1,2,0:T(8,128)}) %all-reduce.14.cloned.1.call-update) | async-done | bytes 1048592 | tf_op jit(solution)/shard_map/psum | solution.py:123
  552.5 5.7 copy.211
  558.3 86.9 %all-reduce.26.cloned.1.call-done = (bf16[4,256,512]{2,1,0:T(8,128)(2,1)}, bf16[4,256,512]{2,1,0:T(8,128)(2,1)}) async-done(((bf16[4,256,512]{2,1,0:T(8,128)(2,1)}, bf16[4,256,512]{2,1,0:T(8,128)(2,1)}), (bf16[4,256,512]{2,1,0:T(8,128)(2,1)}, bf16[4,256,512]{2,1,0:T(8,128)(2,1)})) %all-reduce.26.cloned.1.call-update) | async-done | bytes 2097168 | tf_op jit(solution)/shard_map/psum | solution.py:14
  649.3 5.1 fusion.7
  654.4 25.9 %all-reduce.18.cloned.1.call-done = bf16[256,1024]{1,0:T(8,128)(2,1)} async-done(((bf16[256,1024]{1,0:T(8,128)(2,1)}), bf16[256,1024]{1,0:T(8,128)(2,1)}) %all-reduce.18.cloned.1.call-update) | async-done | bytes 524304 | tf_op jit(solution)/shard_map/psum | solution.py:14
  680.3 5.3 add_convert_fusion.1
  695.4 31.1 %all-reduce.20.cloned.1.call-done = f32[256,1024]{1,0:T(8,128)} async-done(((f32[256,1024]{1,0:T(8,128)}), f32[256,1024]{1,0:T(8,128)}) %all-reduce.20.cloned.1.call-update) | async-done | bytes 1048592 | tf_op jit(solution)/shard_map/psum | solution.py:197
  726.5 5.8 add_convert_fusion
  (153 shorter events, 136.1 us)
Async XLA Ops:
  13.0 10.0 %copy-start.19 = (bf16[128,8192]{1,0:T(8,128)(2,1)}, bf16[128,8192]{1,0:T(8,128)(2,1)S(1)}, u32[]{:S(2)}) copy-start(bf16[128,8192]{1,0:T(8,128)(2,1)S(1)} %get-tuple-element.29) | copy-start | bytes 6291460
  17.4 50.0 %all-to-all-start.1 = ((bf16[128,8,1024]{0,2,1:T(8,128)(2,1)}), bf16[128,8,1024]{0,2,1:T(8,128)(2,1)}, u32[]{:S(2)}, u32[]{:S(2)}) async-start(bf16[128,8,1024]{0,2,1:T(8,128)(2,1)} %bitcast.138), calls=%async_computation.1 | async-start | bytes 4194304 | tf_op jit(solution)/shard_map/all_to_all | solution.py:32
  67.4 7.9 %copy-start.13 = (f32[4,256,512]{2,1,0:T(8,128)S(1)}, f32[4,256,512]{2,1,0:T(8,128)}, u32[]{:S(2)}) copy-start(f32[4,256,512]{2,1,0:T(8,128)} %param.11) | copy-start | bytes 6291460
  67.4 110.9 %all-to-all-start = ((bf16[128,8,1024]{0,2,1:T(8,128)(2,1)}), bf16[128,8,1024]{0,2,1:T(8,128)(2,1)}, u32[]{:S(2)}, u32[]{:S(2)}) async-start(bf16[128,8,1024]{0,2,1:T(8,128)(2,1)} %bitcast.137), calls=%async_computation | async-start | bytes 4194304 | tf_op jit(solution)/shard_map/all_to_all | solution.py:31
  75.3 121.8 %all-reduce.12.cloned.1.call-start = ((), (), s32[]{:S(2)}) async-start(), calls=%async_computation.2 | async-start | bytes 524288 | tf_op jit(solution)/shard_map/psum | solution.py:14
  76.0 205.2 %all-reduce.24.cloned.1.call-start = ((), (), s32[]{:S(2)}) async-start(), calls=%async_computation.8 | async-start | bytes 6291456 | tf_op jit(solution)/shard_map/psum | solution.py:123
  79.1 91.2 %copy-start.5 = (f32[4,256,256]{1,2,0:T(8,128)}, f32[4,256,256]{1,2,0:T(8,128)S(1)}, u32[]{:S(2)}) copy-start(f32[4,256,256]{1,2,0:T(8,128)S(1)} %copy.206) | copy-start | bytes 3145732
  141.6 28.7 %copy-start.30 = (bf16[1024,256]{1,0:T(8,128)(2,1)}, bf16[1024,256]{1,0:T(8,128)(2,1)S(1)}, u32[]{:S(2)}) copy-start(bf16[1024,256]{1,0:T(8,128)(2,1)S(1)} %all_gather.6) | copy-start | bytes 1572868
  186.9 5.8 copy-start.14
  186.9 5.8 copy-start.21
  200.3 162.4 %all-reduce.16.cloned.1.call-start = ((), (), s32[]{:S(2)}) async-start(), calls=%async_computation.4 | async-start | bytes 2097152 | tf_op jit(solution)/shard_map/psum | solution.py:14
  202.6 16.0 %copy-start.6 = (f32[4,256,256]{1,2,0:T(8,128)S(1)}, f32[4,256,256]{1,2,0:T(8,128)}, u32[]{:S(2)}) copy-start(f32[4,256,256]{1,2,0:T(8,128)} %copy-done.5) | copy-start | bytes 3145732
  202.6 279.9 %all-reduce.22.cloned.1.call-start = ((), (), s32[]{:S(2)}) async-start(), calls=%async_computation.7 | async-start | bytes 4718592 | tf_op jit(solution)/shard_map/psum | solution.py:14
  307.1 5.1 copy-start.10
  314.7 4.3 copy-start.25
  372.8 149.3 %all-reduce.14.cloned.1.call-start = ((), (), s32[]{:S(2)}) async-start(), calls=%async_computation.3 | async-start | bytes 2097152 | tf_op jit(solution)/shard_map/psum | solution.py:123
  486.3 158.8 %all-reduce.26.cloned.1.call-start = ((), (), s32[]{:S(2)}) async-start(), calls=%async_computation.9 | async-start | bytes 4194304 | tf_op jit(solution)/shard_map/psum | solution.py:14
  486.4 4.5 copy-start.16
  490.9 31.1 %copy-start.33 = (f32[256,256]{1,0:T(8,128)S(1)}, f32[256,256]{1,0:T(8,128)}, u32[]{:S(2)}) copy-start(f32[256,256]{1,0:T(8,128)} %get-tuple-element.11) | copy-start | bytes 786436
  527.8 4.6 copy-start.8
  542.1 138.2 %all-reduce.18.cloned.1.call-start = ((), (), s32[]{:S(2)}) async-start(), calls=%async_computation.5 | async-start | bytes 1048576 | tf_op jit(solution)/shard_map/psum | solution.py:14
  558.2 168.3 %all-reduce.20.cloned.1.call-start = ((), (), s32[]{:S(2)}) async-start(), calls=%async_computation.6 | async-start | bytes 2097152 | tf_op jit(solution)/shard_map/psum | solution.py:197
  680.3 7.2 copy-start.23
  693.8 32.7 %copy-start.24 = (bf16[8,256,512]{2,1,0:T(8,128)(2,1)S(1)}, bf16[8,256,512]{2,1,0:T(8,128)(2,1)}, u32[]{:S(2)}) copy-start(bf16[8,256,512]{2,1,0:T(8,128)(2,1)} %copy-done.22) | copy-start | bytes 6291460
  (21 other events, 47.0 us)
Sparse Core Ops, SparseCore 0:
  79.5 91.6 all-reduce.11
  200.4 80.8 all-reduce.23
  285.8 76.7 all-reduce.15
  372.9 109.5 all-reduce.21
  486.5 35.5 all-reduce.13
  542.3 102.7 all-reduce.25
  648.0 32.2 all-reduce.17
  689.9 36.5 all-reduce.19
where the time goes:
time: 746 us; the launch traced here: 739 us
  waiting for transfers between devices  412 us (55%)
  blocking collectives  98 us (13%)
  matrix products  90.7 us (12%)
  local copies, waits for them, and re-layouts  60.6 us (8%)
  other arithmetic  33.2 us (4%)
  starting transfers between devices  24.6 us (3%)
  between operations  20.3 us (3%)
    psum x5, waiting for transfers between devices, spread(): return lax.psum(kept, axis)  251 us
    psum x2, waiting for transfers between devices, per_device(): summed = lax.psum((own_k, cross_k, own_c, cross_c), 'dp')  87.9 us
    all_gather x1, blocking collectives, fetch_lead(): lax.all_gather(before[0], 'fsdp', axis=0, tiled=True)  59.3 us
    all_to_all x1, waiting for transfers between devices, to_owners(): lax.all_to_all(pair[1], 'fsdp', split_axis=1, concat_axis=0, tiled=True)  42 us
    psum x1, waiting for transfers between devices, per_device(): row_sum = lax.psum(row_term, 'dp')  31.1 us
    all_gather x1, blocking collectives, fetch_lead(): lax.all_gather(before[1], 'fsdp', axis=0, tiled=True)  25.9 us
    unnamed x74, local copies, waits for them, and re-layouts  23.7 us
  transfers between devices with their start and end apart: 10, of which 8 were waited for; matrix products, arithmetic and copies ran while one was open for 15% of the time, Pallas kernels for 0%

commit v1 on v0

--- a/solution.py
+++ b/solution.py
@@ -1,12 +1,475 @@
+import functools
+
 import jax
 import jax.numpy as jnp
 from jax import lax
+from jax.experimental import pallas as pl
+from jax.experimental.pallas import tpu as pltpu
 from jax.sharding import PartitionSpec as P
 
 damping = 0.1
 momentum_rate = 0.5
 step_rate = 0.2
 highest = lax.Precision.HIGHEST
+both = ("dp", "fsdp")
+f32 = jnp.float32
+bf16 = jnp.bfloat16
+vmem_cap = 48 * 1024 * 1024
+
+
+def params(*semantics):
+    return pltpu.CompilerParams(dimension_semantics=semantics, vmem_limit_bytes=vmem_cap)
+
+
+def dot(a, b, dims=((1,), (0,)), precision=None):
+    return lax.dot_general(a, b, (dims, ((), ())), precision=precision, preferred_element_type=f32)
+
+
+nn = ((1,), (0,))
+tn = ((0,), (0,))
+nt = ((1,), (1,))
+
+
+def pack_body(zs, xs, ds, bs, tile, lim_ref, a_ref, o_ref):
+    rows = pl.program_id(0) * tile + lax.broadcasted_iota(jnp.int32, (tile, bs), 0)
+    keep = jnp.where(rows < lim_ref[0], 1.0, 0.0).astype(bf16)
+    lead = a_ref[:, :bs] * keep
+    for d in range(ds):
+        for x in range(xs):
+            for z in range(zs):
+                n = (z * xs + x) * ds + d
+                o_ref[d * xs + x, z] = a_ref[:, n * bs : (n + 1) * bs] * keep
+            o_ref[d * xs + x, zs] = lead
+
+
+def pack(limit, tokens, zs, xs, ds, bs):
+    count, width = tokens.shape
+    tile = 32
+    return pl.pallas_call(
+        functools.partial(pack_body, zs, xs, ds, bs, tile),
+        grid=(count // tile,),
+        in_specs=[
+            pl.BlockSpec(memory_space=pltpu.SMEM),
+            pl.BlockSpec((tile, width), lambda i: (i, 0)),
+        ],
+        out_specs=pl.BlockSpec((ds * xs, zs + 1, tile, bs), lambda i: (0, 0, i, 0)),
+        out_shape=jax.ShapeDtypeStruct((ds * xs, zs + 1, count, bs), bf16),
+        compiler_params=params("arbitrary"),
+        name="pack_tokens",
+    )(limit, tokens)
+
+
+def moments_body(ids_ref, x_ref, l_ref, o_ref):
+    groups, _, count, bs = x_ref.shape
+    cols = x_ref[:, 0].reshape(groups * count, bs)
+    lead = l_ref[:, 0].reshape(groups * count, bs)
+    o_ref[0, 0] = dot(cols, cols, tn).astype(bf16)
+    o_ref[0, 1] = dot(lead, cols, tn).astype(bf16)
+    o_ref[0, 2] = dot(lead, lead, tn).astype(bf16)
+
+
+def raw_moments(ids, owned):
+    groups, slots, count, bs = owned.shape
+    zs = slots - 1
+    return pl.pallas_call(
+        moments_body,
+        grid_spec=pltpu.PrefetchScalarGridSpec(
+            num_scalar_prefetch=1,
+            grid=(zs,),
+            in_specs=[
+                pl.BlockSpec((groups, 1, count, bs), lambda k, ids: (0, ids[0] ^ k, 0, 0)),
+                pl.BlockSpec((groups, 1, count, bs), lambda k, ids: (0, zs, 0, 0)),
+            ],
+            out_specs=pl.BlockSpec((1, 3, bs, bs), lambda k, ids: (k, 0, 0, 0)),
+        ),
+        out_shape=jax.ShapeDtypeStruct((zs, 3, bs, bs), bf16),
+        compiler_params=params("arbitrary"),
+        name="raw_moments",
+    )(ids, owned, owned)
+
+
+def image_stats_body(count, ids_ref, sc_ref, *refs):
+    parts = refs[:count]
+    fac_ref, lead_ref, h_ref, hb_ref, tr_ref = refs[count:]
+    bs = lead_ref.shape[0]
+    keep = sc_ref[1]
+    total = parts[0][...].astype(f32)
+    for part in parts[1:]:
+        total = total + part[...].astype(f32)
+    fac = fac_ref[0]
+    diag = fac[:, :bs]
+    side = fac[:, bs:] * keep
+    gram = jnp.sum(diag * diag) + jnp.sum(side * side)
+    bn = diag.astype(bf16).astype(f32)
+    pn = side.astype(bf16).astype(f32)
+    b0 = lead_ref[...].astype(f32)
+    mm = functools.partial(dot, precision=highest)
+    t1 = mm(total[0], bn) + mm(total[1], pn, tn)
+    t0 = mm(total[1], bn) + mm(total[2], pn)
+    own = (mm(bn, t1, tn) + mm(pn, t0, tn)) * sc_ref[0]
+    cross = mm(b0, t0, tn) * sc_ref[0]
+    h_ref[0] = own
+    h_ref[1] = cross
+    hb_ref[0] = own.astype(bf16)
+    hb_ref[1] = cross.astype(bf16)
+    row = lax.broadcasted_iota(jnp.int32, (bs, bs), 0)
+    col = lax.broadcasted_iota(jnp.int32, (bs, bs), 1)
+    trace = jnp.sum(jnp.where(row == col, own, 0.0))
+    top = lax.broadcasted_iota(jnp.int32, (8, 128), 0)
+    tr_ref[...] = jnp.where(top == 0, trace, gram)
+
+
+def image_stats(ids, scalars, parts, factor, lead):
+    bs = lead.shape[0]
+    whole = lambda shape: pl.BlockSpec(shape, lambda i, ids: (0,) * len(shape))
+    return pl.pallas_call(
+        functools.partial(image_stats_body, len(parts)),
+        grid_spec=pltpu.PrefetchScalarGridSpec(
+            num_scalar_prefetch=1,
+            grid=(1,),
+            in_specs=[pl.BlockSpec(memory_space=pltpu.SMEM)]
+            + [whole((3, bs, bs)) for _ in parts]
+            + [pl.BlockSpec((1, bs, 2 * bs), lambda i, ids: (ids[1], 0, 0)), whole((bs, bs))],
+            out_specs=[whole((2, bs, bs)), whole((2, bs, bs)), whole((8, 128))],
+        ),
+        out_shape=[
+            jax.ShapeDtypeStruct((2, bs, bs), f32),
+            jax.ShapeDtypeStruct((2, bs, bs), bf16),
+            jax.ShapeDtypeStruct((8, 128), f32),
+        ],
+        compiler_params=params("arbitrary"),
+        name="image_stats",
+    )(ids, scalars, *parts, factor, lead)
+
+
+def advance_block(width, own, cross, fac, mom, b0, other_h, other_g, keep):
+    bs = fac.shape[0]
+    diag = fac[:, :bs]
+    side = fac[:, bs:] * keep
+    db = diag.astype(bf16)
+    sb = side.astype(bf16)
+    gram_d = dot(db, db, tn) + dot(sb, sb, tn)
+    gram_s = dot(b0, sb, tn)
+    row = lax.broadcasted_iota(jnp.int32, (bs, bs), 0)
+    col = lax.broadcasted_iota(jnp.int32, (bs, bs), 1)
+    ident = jnp.where(row == col, width, 0.0)
+    scale = 1.0 / (2.0 * width)
+    md = momentum_rate * mom[:, :bs] + (other_h * own + damping * other_g * gram_d - ident) * scale
+    ms = momentum_rate * mom[:, bs:] + (other_h * cross + damping * other_g * gram_s) * scale
+    ms = ms * keep
+    mdb = md.astype(bf16)
+    new_d = diag - step_rate * dot(db, mdb)
+    new_s = side - step_rate * (dot(b0, ms.astype(bf16)) + dot(sb, mdb)) * keep
+    return md, ms, new_d, new_s
+
+
+def order_of(ids, m):
+    return ids[1] ^ ((m & 1) * 2 + (m >> 1))
+
+
+def advance_body(width, ids_ref, sc_ref, h_ref, fac_ref, mom_ref, lead_ref, fn_ref, mn_ref, fb_ref):
+    blocks = lead_ref.shape[0]
+    bs = lead_ref.shape[0]
+    j = order_of(ids_ref, pl.program_id(0))
+    keep = jnp.where(ids_ref[2] + j > 0, 1.0, 0.0)
+    md, ms, new_d, new_s = advance_block(
+        width,
+        h_ref[0, 0].astype(f32),
+        h_ref[0, 1].astype(f32),
+        fac_ref[0],
+        mom_ref[0],
+        lead_ref[...],
+        sc_ref[0],
+        sc_ref[1],
+        keep,
+    )
+    fn_ref[0, :, :bs] = new_d
+    fn_ref[0, :, bs:] = new_s
+    mn_ref[0, :, :bs] = md
+    mn_ref[0, :, bs:] = ms
+    fb_ref[0, :, :bs] = new_d.astype(bf16)
+    fb_ref[0, :, bs:] = new_s.astype(bf16)
+
+
+def advance_all(width, ids, scalars, stats, factor, moment, lead):
+    blocks, bs, wide = factor.shape
+    spec = pl.BlockSpec((1, bs, wide), lambda m, ids: (order_of(ids, m), 0, 0))
+    return pl.pallas_call(
+        functools.partial(advance_body, width),
+        grid_spec=pltpu.PrefetchScalarGridSpec(
+            num_scalar_prefetch=1,
+            grid=(blocks,),
+            in_specs=[
+                pl.BlockSpec(memory_space=pltpu.SMEM),
+                pl.BlockSpec((1, 2, bs, bs), lambda m, ids: (m, 0, 0, 0)),
+                spec,
+                spec,
+                pl.BlockSpec((bs, bs), lambda m, ids: (0, 0)),
+            ],
+            out_specs=[spec, spec, spec],
+        ),
+        out_shape=[
+            jax.ShapeDtypeStruct(factor.shape, f32),
+            jax.ShapeDtypeStruct(factor.shape, f32),
+            jax.ShapeDtypeStruct(factor.shape, bf16),
+        ],
+        compiler_params=params("arbitrary"),
+        name="advance_all",
+    )(ids, scalars, stats, factor, moment, lead)
+
+
+def advance_one_body(width, ids_ref, sc_ref, h_ref, fac_ref, mom_ref, lead_ref, fb_ref):
+    bs = lead_ref.shape[0]
+    keep = jnp.where(ids_ref[2] + ids_ref[1] > 0, 1.0, 0.0)
+    _, _, new_d, new_s = advance_block(
+        width, h_ref[0], h_ref[1], fac_ref[0], mom_ref[0], lead_ref[...], sc_ref[0], sc_ref[1], keep
+    )
+    fb_ref[:, :bs] = new_d.astype(bf16)
+    fb_ref[:, bs:] = new_s.astype(bf16)
+
+
+def advance_one(width, ids, scalars, stats, factor, moment, lead):
+    blocks, bs, wide = factor.shape
+    spec = pl.BlockSpec((1, bs, wide), lambda i, ids: (ids[1], 0, 0))
+    return pl.pallas_call(
+        functools.partial(advance_one_body, width),
+        grid_spec=pltpu.PrefetchScalarGridSpec(
+            num_scalar_prefetch=1,
+            grid=(1,),
+            in_specs=[
+                pl.BlockSpec(memory_space=pltpu.SMEM),
+                pl.BlockSpec((2, bs, bs), lambda i, ids: (0, 0, 0)),
+                spec,
+                spec,
+                pl.BlockSpec((bs, bs), lambda i, ids: (0, 0)),
+            ],
+            out_specs=pl.BlockSpec((bs, wide), lambda i, ids: (0, 0)),
+        ),
+        out_shape=jax.ShapeDtypeStruct((bs, wide), bf16),
+        compiler_params=params("arbitrary"),
+        name="advance_one",
+    )(ids, scalars, stats, factor, moment, lead)
+
+
+def columns_body(ids_ref, g_ref, l_ref, k_ref, s_ref, t_ref):
+    blocks, bs, _ = k_ref.shape
+    lead = l_ref[...]
+    term = None
+    for n in range(blocks):
+        kd = k_ref[n, :, :bs]
+        ks = k_ref[n, :, bs:]
+        first = (dot(g_ref[:, n * bs : (n + 1) * bs], kd) + dot(lead, ks)).astype(bf16)
+        second = dot(first, kd, nt)
+        s_ref[:, n * bs : (n + 1) * bs] = second.astype(bf16)
+        part = dot(first, ks, nt)
+        if n == 0:
+            part = part + second * jnp.where(ids_ref[2] == 0, 1.0, 0.0)
+        term = part if term is None else term + part
+    t_ref[...] = term.astype(bf16)
+
+
+def columns(ids, grad, lead, kb):
+    rows, wide = grad.shape
+    blocks, bs, _ = kb.shape
+    tile = 512
+    return pl.pallas_call(
+        columns_body,
+        grid_spec=pltpu.PrefetchScalarGridSpec(
+            num_scalar_prefetch=1,
+            grid=(rows // tile,),
+            in_specs=[
+                pl.BlockSpec((tile, wide), lambda i, ids: (i, 0)),
+                pl.BlockSpec((tile, bs), lambda i, ids: (i, 0)),
+                pl.BlockSpec(kb.shape, lambda i, ids: (0, 0, 0)),
+            ],
+            out_specs=[
+                pl.BlockSpec((tile, wide), lambda i, ids: (i, 0)),
+                pl.BlockSpec((tile, bs), lambda i, ids: (i, 0)),
+            ],
+        ),
+        out_shape=[
+            jax.ShapeDtypeStruct((rows, wide), bf16),
+            jax.ShapeDtypeStruct((rows, bs), bf16),
+        ],
+        compiler_params=params("arbitrary"),
+        name="column_products",
+    )(ids, grad, lead, kb)
+
+
+def row_of(ids, k):
+    q = ids[3] ^ k
+    return (q & 1) * ids[4] + (q >> 1)
+
+
+def rows_body(ids_ref, s_ref, l_ref, c_ref, p_ref, u_ref, acc_ref):
+    k = pl.program_id(0)
+    bs = l_ref.shape[0]
+    cd = c_ref[0, :, :bs]
+    cs = c_ref[0, :, bs:]
+    third = (dot(cd, s_ref[...], tn) + dot(cs, l_ref[...], tn)).astype(bf16)
+    fourth = dot(cd, third)
+    p_ref[...] = fourth.astype(bf16)
+    is_first = (ids_ref[5] == 0) & (row_of(ids_ref, k) == 0)
+    term = dot(cs, third) + fourth * jnp.where(is_first, 1.0, 0.0)
+
+    @pl.when(k == 0)
+    def _():
+        acc_ref[...] = term
+
+    @pl.when(k > 0)
+    def _():
+        acc_ref[...] = acc_ref[...] + term
+
+    @pl.when(k == pl.num_programs(0) - 1)
+    def _():
+        u_ref[...] = acc_ref[...].astype(bf16)
+
+
+def rows(ids, second, lead, cb):
+    count, wide = second.shape
+    blocks, bs, _ = cb.shape
+    spec = pl.BlockSpec((bs, wide), lambda k, ids: (row_of(ids, k), 0))
+    whole = pl.BlockSpec((bs, wide), lambda k, ids: (0, 0))
+    return pl.pallas_call(
+        rows_body,
+        grid_spec=pltpu.PrefetchScalarGridSpec(
+            num_scalar_prefetch=1,
+            grid=(blocks,),
+            in_specs=[spec, whole, pl.BlockSpec((1, bs, 2 * bs), lambda k, ids: (k, 0, 0))],
+            out_specs=[spec, whole],
+            scratch_shapes=[pltpu.VMEM((bs, wide), f32)],
+        ),
+        out_shape=[
+            jax.ShapeDtypeStruct((count, wide), bf16),
+            jax.ShapeDtypeStruct((bs, wide), bf16),
+        ],
+        compiler_params=params("arbitrary"),
+        name="row_products",
+    )(ids, second, lead, cb)
+
+
+def planned(acts, out_grads, token_counts, k_factor, c_factor, k_moment, c_moment, grad_weight):
+    tok_dev, width = acts.shape
+    ds, bs, _ = k_factor.shape
+    shards = lax.axis_size("fsdp")
+    xs = 2
+    zs = shards // xs
+    d = lax.axis_index("dp")
+    s = lax.axis_index("fsdp")
+    x = s % xs
+    z = s // xs
+    flat = lambda dd, ss: dd * shards + ss
+    plane = [[flat(dd, zz * xs + xx) for dd in range(ds) for xx in range(xs)] for zz in range(zs)]
+    ids = jnp.stack([z, d, s * ds, s, jnp.int32(ds), d]).astype(jnp.int32)
+    token_total = jnp.sum(token_counts).astype(f32)
+    valid = jnp.sum(jnp.where(lax.iota(jnp.int32, ds) == d, token_counts, 0))
+    limit = (valid - s * tok_dev).reshape(1).astype(jnp.int32)
+    keep = jnp.where(s * ds + d > 0, 1.0, 0.0)
+    stat_scalars = jnp.stack([1.0 / token_total, keep]).astype(f32)
+
+    def to_all_shards(value):
+        over_x = lax.ppermute(value, "fsdp", [(0, 1)])
+        value = jnp.where(s == 0, value, over_x)
+        got = [
+            lax.ppermute(value, "fsdp", [(xx, zz * xs + xx) for xx in range(xs)])
+            for zz in range(1, zs)
+        ]
+        out = got[0]
+        for g in got[1:]:
+            out = out + g
+        return jnp.where(z == 0, value, out)
+
+    leads = jnp.stack([k_factor[0, :, :bs], c_factor[0, :, :bs]]).astype(bf16)
+    leads = to_all_shards(leads)
+    lead_k, lead_c = leads[0], leads[1]
+
+    def grad_lead_all():
+        value = grad_weight[:, :bs]
+        half = value.shape[0] // xs
+        over_x = lax.ppermute(value[half:], "fsdp", [(0, 1)])
+        mine = jnp.where(s == 0, value[:half], over_x)
+        got = [
+            lax.ppermute(mine, "fsdp", [(xx, zz * xs + xx) for xx in range(xs)])
+            for zz in range(1, zs)
+        ]
+        out = got[0]
+        for g in got[1:]:
+            out = out + g
+        mine = jnp.where(z == 0, mine, out)
+        other = lax.ppermute(mine, "fsdp", [(i, i ^ 1) for i in range(shards)])
+        low = jnp.where(x == 0, mine, other)
+        high = jnp.where(x == 0, other, mine)
+        return jnp.concatenate([low, high], axis=0)
+
+    grad_lead = grad_lead_all()
+
+    def side(tokens, factor, lead):
+        packed = pack(limit, tokens, zs, xs, ds, bs)
+        owned = lax.all_to_all(packed, both, 0, 0, tiled=True, axis_index_groups=plane)
+        raw = raw_moments(ids, owned)
+        parts = [raw[0]]
+        for k in range(1, zs):
+            pairs = [(zz * xs + xx, (zz ^ k) * xs + xx) for zz in range(zs) for xx in range(xs)]
+            parts.append(lax.ppermute(raw[k], "fsdp", pairs))
+        return image_stats(ids, stat_scalars, parts, factor, lead)
+
+    def totals(traces):
+        spread = jnp.broadcast_to(traces[None], (ds * shards,) + traces.shape)
+        got = lax.all_to_all(spread, both, 0, 0, tiled=True)
+        summed = jnp.sum(got, axis=0)
+        return summed[:2, 0]
+
+    def over_dp(value):
+        pair = jnp.stack([value, lax.ppermute(value, "dp", [(i, i ^ 2) for i in range(ds)])])
+        other = lax.ppermute(pair, "dp", [(i, i ^ 1) for i in range(ds)])
+        return jnp.concatenate([pair, other], axis=0)
+
+    scale_width = float(width)
+    stat_k, stat_kb, trace_k = side(acts, k_factor, lead_k)
+    total_k = totals(trace_k)
+    all_k = over_dp(stat_kb)
+    stat_c, stat_cb, trace_c = side(out_grads, c_factor, lead_c)
+
+    c_block = advance_one(scale_width, ids, total_k, stat_c, c_factor, c_moment, lead_c)
+    fetched = []
+    for k in range(shards):
+        pairs = [
+            (flat(dd, zz * xs + xx), flat(zz, (dd * xs + xx) ^ k))
+            for dd in range(ds)
+            for zz in range(zs)
+            for xx in range(xs)
+        ]
+        fetched.append(lax.ppermute(c_block, both, pairs))
+    c_rows = jnp.stack(fetched)
+
+    total_c = totals(trace_c)
+    k_factor_new, k_moment_new, kb = advance_all(
+        scale_width, ids, total_c, all_k, k_factor, k_moment, lead_k
+    )
+    second, term = columns(ids, grad_weight, grad_lead, kb)
+    count = grad_weight.shape[0]
+    by_shard = term.reshape(shards, count // shards, bs)
+    got = lax.all_to_all(by_shard, "fsdp", 0, 0, tiled=True)
+    block_sum = jnp.sum(got.astype(f32), axis=0).astype(bf16)
+    blocks = [block_sum] + [lax.ppermute(block_sum, "fsdp", [(k, 0)]) for k in range(1, shards)]
+    lead_cols = jnp.where(s == 0, jnp.concatenate(blocks, axis=0), second[:, :bs])
+    second = jnp.concatenate([lead_cols, second[:, bs:]], axis=1)
+    top = second[:bs]
+    lead_rows = jnp.where(d == 0, top, 0).astype(bf16)
+    for k in range(1, ds):
+        lead_rows = lead_rows + lax.ppermute(top, "dp", [(0, k)])
+
+    all_c = over_dp(stat_cb)
+    c_factor_new, c_moment_new, _ = advance_all(
+        scale_width, ids, total_k, all_c, c_factor, c_moment, lead_c
+    )
+    precond, up = rows(ids, second, lead_rows, c_rows)
+    over_y = lax.ppermute(up, "dp", [(2, 0), (3, 1)])
+    up_sum = up.astype(f32) + over_y.astype(f32)
+    over_core = lax.ppermute(up_sum.astype(bf16), "dp", [(1, 0)])
+    up_sum = (up_sum + over_core.astype(f32)).astype(bf16)
+    precond = precond.at[:bs].set(jnp.where(d == 0, up_sum, precond[:bs]))
+    return (k_factor_new, c_factor_new, k_moment_new, c_moment_new, precond)
 
 
 def spread(value, axis, source):
@@ -82,7 +545,7 @@
     )
 
 
-def per_device(acts, out_grads, token_counts, k_factor, c_factor, k_moment, c_moment, grad_weight):
+def general(acts, out_grads, token_counts, k_factor, c_factor, k_moment, c_moment, grad_weight):
     tok_dev, width = acts.shape
     blocks_dev = k_factor.shape[0]
     block_size = k_factor.shape[1]
@@ -205,6 +668,13 @@
     return (k_factor_new, c_factor_new, k_moment_new, c_moment_new, precond)
 
 
+def per_device(*args):
+    blocks = args[3].shape[0]
+    groups, shards = lax.axis_size("dp"), lax.axis_size("fsdp")
+    fits = blocks == 4 and groups == 4 and shards == 8
+    return (planned if fits else general)(*args)
+
+
 def solution(mesh):
     in_specs = (
         P(("dp", "fsdp"), None),

time: 746 us -> 430 us (0.58)
  the two profiles are of different devices: /device:TPU:17 before, /device:TPU:1 now
where the time goes in v1:
time: 430 us; the launch traced here: 428 us
  waiting for transfers between devices  178 us (41%)
  starting transfers between devices  148 us (34%)
  Pallas kernels  49.6 us (12%)
  local copies, waits for them, and re-layouts  30.5 us (7%)
  other arithmetic  20.1 us (5%)
    ppermute x8, starting transfers between devices, planned(): fetched.append(lax.ppermute(c_block, both, pairs))  50.4 us
    ppermute x1, waiting for transfers between devices, to_all_shards(): over_x = lax.ppermute(value, 'fsdp', [(0, 1)])  35.3 us
    ppermute x6, waiting for transfers between devices, side(): parts.append(lax.ppermute(raw[k], 'fsdp', pairs))  30 us
    all_to_all x2, waiting for transfers between devices, side(): lax.all_to_all(packed, both, 0, 0, tiled=True, axis_index_groups=plane)  27.5 us
    ppermute x3, waiting for transfers between devices, grad_lead_all(): lax.ppermute(mine, 'fsdp', [(xx, zz * xs + xx) for xx in range(xs)])  24.3 us
    all_to_all x2, starting transfers between devices, totals(): got = lax.all_to_all(spread, both, 0, 0, tiled=True)  21.3 us
    unnamed x52, local copies, waits for them, and re-layouts  19.1 us
    ppermute x2, waiting for transfers between devices, over_dp(): lax.ppermute(value, 'dp', [(i, i ^ 2) for i in range(ds)])  16.9 us
  transfers between devices with their start and end apart: 44, of which 17 were waited for; matrix products, arithmetic and copies ran while one was open for 8% of the time, Pallas kernels for 9%

profile of v1, /device:TPU:1, one launch (start us, length us, event | category | flops | bytes accessed | tf_op | source)
XLA Modules:
  0.0 428.5 jit_solution(10642421581315088633)
XLA Ops:
  6.1 5.2 %all-to-all-start.2 = ((bf16[8,5,128,256]{3,2,1,0:T(8,128)(2,1)}), bf16[8,5,128,256]{3,2,1,0:T(8,128)(2,1)S(1)}, u32[]{:S(2)}, u32[]{:S(2)}) async-start(bf16[8,5,128,256]{3,2,1,0:T(8,128)(2,1)} %copy-done.4), calls=%async_computation.2 | async-start | bytes 5242880 | tf_op jit(solution)/shard_map/all_to_all | solution.py:408
  14.9 27.5 %all-to-all-done.2.x_ref.l_ref = bf16[8,5,128,256]{3,2,1,0:T(8,128)(2,1)S(1)} async-done(((bf16[8,5,128,256]{3,2,1,0:T(8,128)(2,1)}), bf16[8,5,128,256]{3,2,1,0:T(8,128)(2,1)S(1)}, u32[]{:S(2)}, u32[]{:S(2)}) %all-to-all-start.2) | async-done | bytes 2621472 | tf_op jit(solution)/shard_map/all_to_all | solution.py:408
  58.2 35.3 %collective-permute-done.3 = bf16[2,256,256]{2,1,0:T(8,128)(2,1)S(1)} collective-permute-done((bf16[2,256,256]{2,1,0:T(8,128)(2,1)S(1)}, bf16[2,256,256]{2,1,0:T(8,128)(2,1)S(1)}, u32[]{:S(2)}, u32[]{:S(2)}) %collective-permute-start.3) | collective-permute-done | bytes 262176 | tf_op jit(solution)/shard_map/ppermute | solution.py:371
  105.9 5.6 %collective-permute-done.6 = bf16[2,256,256]{2,1,0:T(8,128)(2,1)S(1)} collective-permute-done((bf16[2,256,256]{2,1,0:T(8,128)(2,1)S(1)}, bf16[2,256,256]{2,1,0:T(8,128)(2,1)S(1)}, u32[]{:S(2)}, u32[]{:S(2)}) %collective-permute-start.6) | collective-permute-done | bytes 262176 | tf_op jit(solution)/shard_map/ppermute | solution.py:374
  122.7 11.3 %collective-permute-done.16 = bf16[1024,256]{1,0:T(8,128)(2,1)S(1)} collective-permute-done((bf16[1024,256]{1,0:T(8,128)(2,1)S(1)}, bf16[1024,256]{1,0:T(8,128)(2,1)S(1)}, u32[]{:S(2)}, u32[]{:S(2)}) %collective-permute-start.16) | collective-permute-done | bytes 524320 | tf_op jit(solution)/shard_map/ppermute | solution.py:392
  134.0 11.2 %collective-permute-done.17 = bf16[1024,256]{1,0:T(8,128)(2,1)S(1)} collective-permute-done((bf16[1024,256]{1,0:T(8,128)(2,1)S(1)}, bf16[1024,256]{1,0:T(8,128)(2,1)S(1)}, u32[]{:S(2)}, u32[]{:S(2)}) %collective-permute-start.17) | collective-permute-done | bytes 524320 | tf_op jit(solution)/shard_map/ppermute | solution.py:392
  148.3 7.7 %collective-permute-start.9 = (bf16[3,256,256]{2,1,0:T(8,128)(2,1)}, bf16[3,256,256]{2,1,0:T(8,128)(2,1)}, u32[]{:S(2)}, u32[]{:S(2)}) collective-permute-start(bf16[3,256,256]{2,1,0:T(8,128)(2,1)} %get-tuple-element.47), channel_id=1, source_target_pairs={{0,6},{1,7},{2,4},{3,5},{4,2},{5,3},{6,0},{7,1},{8,14},{9,15},{10,... | collective-permute-start | bytes 1179656 | tf_op jit(solution)/shard_map/ppermute | solution.py:413
  164.7 6.0 %collective-permute-done.9.refs_3_ = bf16[3,256,256]{2,1,0:T(8,128)(2,1)} collective-permute-done((bf16[3,256,256]{2,1,0:T(8,128)(2,1)}, bf16[3,256,256]{2,1,0:T(8,128)(2,1)}, u32[]{:S(2)}, u32[]{:S(2)}) %collective-permute-start.9) | collective-permute-done | bytes 393248 | tf_op jit(solution)/shard_map/ppermute | solution.py:413
  179.1 22.3 %collective-permute-done.1.refs_2_ = bf16[3,256,256]{2,1,0:T(8,128)(2,1)} collective-permute-done((bf16[3,256,256]{2,1,0:T(8,128)(2,1)}, bf16[3,256,256]{2,1,0:T(8,128)(2,1)}, u32[]{:S(2)}, u32[]{:S(2)}) %collective-permute-start.1) | collective-permute-done | bytes 393248 | tf_op jit(solution)/shard_map/ppermute | solution.py:413
  207.2 18.7 %all-to-all-start.1 = ((f32[32,8,128]{2,1,0:T(8,128)}), f32[32,8,128]{2,1,0:T(8,128)S(1)}, u32[]{:S(2)}, u32[]{:S(2)}) async-start(f32[32,8,128]{2,1,0:T(8,128)} %broadcast_in_dim.21), calls=%async_computation.1 | async-start | bytes 262144 | tf_op jit(solution)/shard_map/all_to_all | solution.py:418
  240.9 5.6 %advance_all.2 = (f32[4,256,512]{2,1,0:T(8,128)}, f32[4,256,512]{2,1,0:T(8,128)}, bf16[4,256,512]{2,1,0:T(8,128)(2,1)S(1)}) custom-call(s32[6]{0:T(128)S(1)} %stack.78.ids_ref, f32[2]{0:T(128)S(1)} %slice_reduce_fusion.1.sc_ref, bf16[4,2,256,256]{3,2,1,0:T(8,128)(2,1)S(1)} %pad_maximum_fusion.1.h_ref, f32[4,256,512]{2,1,0:T(8,128)S(1)} %copy-done.6, ...), custom_call_target="tpu_custom_call" | custom-call | tf_op jit(solution)/shard_map/advance_all/pallas_call | solution.py:197
  246.6 8.7 %column_products.1 = (bf16[2048,1024]{1,0:T(8,128)(2,1)}, bf16[2048,256]{1,0:T(8,128)(2,1)S(1)}) custom-call(s32[6]{0:T(128)S(1)} %stack.78.ids_ref, bf16[2048,1024]{1,0:T(8,128)(2,1)} %g_ref.1, bf16[2048,256]{1,0:T(8,128)(2,1)S(1)} %pad_maximum_fusion.3.l_ref, bf16[4,256,512]{2,1,0:T(8,128)(2,1)S(1)} %get-tuple-element.39.k_ref), custom_call_target="tpu_custom_call" | custom-call | tf_op jit(solution)/shard_map/column_products/pallas_call | solution.py:275
  256.2 5.7 %all-to-all-start.4 = ((bf16[8,256,256]{2,1,0:T(8,128)(2,1)}), bf16[8,256,256]{2,1,0:T(8,128)(2,1)}, u32[]{:S(2)}, u32[]{:S(2)}) async-start(bf16[8,256,256]{2,1,0:T(8,128)(2,1)} %bitcast.48), calls=%async_computation.4 | async-start | bytes 2097152 | tf_op jit(solution)/shard_map/all_to_all | solution.py:452
  276.7 8.3 %collective-permute-done.29 = bf16[256,512]{1,0:T(8,128)(2,1)S(1)} collective-permute-done((bf16[256,512]{1,0:T(8,128)(2,1)S(1)}, bf16[256,512]{1,0:T(8,128)(2,1)S(1)}, u32[]{:S(2)}, u32[]{:S(2)}) %collective-permute-start.29) | collective-permute-done | bytes 262176 | tf_op jit(solution)/shard_map/ppermute | solution.py:442
  285.0 5.7 %collective-permute-start.34 = (bf16[256,512]{1,0:T(8,128)(2,1)S(1)}, bf16[256,512]{1,0:T(8,128)(2,1)S(1)}, u32[]{:S(2)}, u32[]{:S(2)}) collective-permute-start(bf16[256,512]{1,0:T(8,128)(2,1)S(1)} %advance_one.1), channel_id=1, source_target_pairs={{0,5},{1,4},{2,13},{3,12},{4,21},{5,20},{6,29},{7,28},{8,7},{9,6},... | collective-permute-start | bytes 786440 | tf_op jit(solution)/shard_map/ppermute | solution.py:442
  291.4 6.9 %collective-permute-done.30 = bf16[256,512]{1,0:T(8,128)(2,1)} collective-permute-done((bf16[256,512]{1,0:T(8,128)(2,1)S(1)}, bf16[256,512]{1,0:T(8,128)(2,1)}, u32[]{:S(2)}, u32[]{:S(2)}) %collective-permute-start.30) | collective-permute-done | bytes 262176 | tf_op jit(solution)/shard_map/ppermute | solution.py:442
  298.3 27.6 %collective-permute-start.35 = (bf16[256,512]{1,0:T(8,128)(2,1)S(1)}, bf16[256,512]{1,0:T(8,128)(2,1)S(1)}, u32[]{:S(2)}, u32[]{:S(2)}) collective-permute-start(bf16[256,512]{1,0:T(8,128)(2,1)S(1)} %advance_one.1), channel_id=1, source_target_pairs={{0,6},{1,7},{2,14},{3,15},{4,22},{5,23},{6,30},{7,31},{8,4},{9,5},... | collective-permute-start | bytes 786440 | tf_op jit(solution)/shard_map/ppermute | solution.py:442
  327.5 5.7 %collective-permute-start.36 = (bf16[256,512]{1,0:T(8,128)(2,1)S(1)}, bf16[256,512]{1,0:T(8,128)(2,1)}, u32[]{:S(2)}, u32[]{:S(2)}) collective-permute-start(bf16[256,512]{1,0:T(8,128)(2,1)S(1)} %advance_one.1), channel_id=1, source_target_pairs={{0,7},{1,6},{2,15},{3,14},{4,23},{5,22},{6,31},{7,30},{8,5},{9,4},... | collective-permute-start | bytes 786440 | tf_op jit(solution)/shard_map/ppermute | solution.py:442
  346.9 9.1 %collective-permute-done.20 = bf16[256,256]{1,0:T(8,128)(2,1)S(1)} collective-permute-done((bf16[256,256]{1,0:T(8,128)(2,1)S(1)}, bf16[256,256]{1,0:T(8,128)(2,1)S(1)}, u32[]{:S(2)}, u32[]{:S(2)}) %collective-permute-start.20) | collective-permute-done | bytes 131104 | tf_op jit(solution)/shard_map/ppermute | solution.py:454
  358.7 5.6 %collective-permute-done.24 = bf16[256,256]{1,0:T(8,128)(2,1)S(1)} collective-permute-done((bf16[256,256]{1,0:T(8,128)(2,1)S(1)}, bf16[256,256]{1,0:T(8,128)(2,1)S(1)}, u32[]{:S(2)}, u32[]{:S(2)}) %collective-permute-start.24) | collective-permute-done | bytes 131104 | tf_op jit(solution)/shard_map/ppermute | solution.py:454
  375.1 11.2 %row_products.1 = (bf16[2048,1024]{1,0:T(8,128)(2,1)}, bf16[256,1024]{1,0:T(8,128)(2,1)S(1)}) custom-call(s32[6]{0:T(128)S(1)} %stack.78.ids_ref, bf16[2048,1024]{1,0:T(8,128)(2,1)} %pad_maximum_fusion.s_ref, bf16[256,1024]{1,0:T(8,128)(2,1)S(1)} %add_add_fusion.l_ref, bf16[8,256,512]{2,1,0:T(8,128)(2,1)} %bitcast_dynamic-update-slice_fusion.c_ref), custom_call_target="tpu_custom_call" | custom-call | tf_op jit(solution)/shard_map/row_products/pallas_call | solution.py:333
  387.6 12.1 %collective-permute-start.12 = (bf16[2,256,256]{2,1,0:T(8,128)(2,1)S(1)}, bf16[2,256,256]{2,1,0:T(8,128)(2,1)S(1)}, u32[]{:S(2)}, u32[]{:S(2)}) collective-permute-start(bf16[2,256,256]{2,1,0:T(8,128)(2,1)S(1)} %copy-done.12), channel_id=1, source_target_pairs={{0,16},{8,24},{16,0},{24,8},{1,17},{9,25},{17,1},{25,9},{2,18},{10... | collective-permute-start | bytes 786440 | tf_op jit(solution)/shard_map/ppermute | solution.py:423
  399.7 16.9 %collective-permute-done.12 = bf16[2,256,256]{2,1,0:T(8,128)(2,1)S(1)} collective-permute-done((bf16[2,256,256]{2,1,0:T(8,128)(2,1)S(1)}, bf16[2,256,256]{2,1,0:T(8,128)(2,1)S(1)}, u32[]{:S(2)}, u32[]{:S(2)}) %collective-permute-start.12) | collective-permute-done | bytes 262176 | tf_op jit(solution)/shard_map/ppermute | solution.py:423
  420.4 5.8 %advance_all.3 = (f32[4,256,512]{2,1,0:T(8,128)}, f32[4,256,512]{2,1,0:T(8,128)}, bf16[4,256,512]{2,1,0:T(8,128)(2,1)}) custom-call(s32[6]{0:T(128)S(1)} %stack.78.ids_ref, f32[2]{0:T(128)S(1)} %slice_reduce_fusion.sc_ref, bf16[4,2,256,256]{3,2,1,0:T(8,128)(2,1)S(1)} %pad_maximum_fusion.2.h_ref, f32[4,256,512]{2,1,0:T(8,128)S(1)} %copy-done.2, ...), custom_call_target="tpu_custom_call" | custom-call | tf_op jit(solution)/shard_map/advance_all/pallas_call | solution.py:197
  (163 shorter events, 140.2 us)
Async XLA Ops:
  6.1 36.2 %all-to-all-start.2 = ((bf16[8,5,128,256]{3,2,1,0:T(8,128)(2,1)}), bf16[8,5,128,256]{3,2,1,0:T(8,128)(2,1)S(1)}, u32[]{:S(2)}, u32[]{:S(2)}) async-start(bf16[8,5,128,256]{3,2,1,0:T(8,128)(2,1)} %copy-done.4), calls=%async_computation.2 | async-start | bytes 5242880 | tf_op jit(solution)/shard_map/all_to_all | solution.py:408
  43.8 112.2 %all-to-all-start = ((bf16[8,5,128,256]{3,2,1,0:T(8,128)(2,1)}), bf16[8,5,128,256]{3,2,1,0:T(8,128)(2,1)S(1)}, u32[]{:S(2)}, u32[]{:S(2)}) async-start(bf16[8,5,128,256]{3,2,1,0:T(8,128)(2,1)} %copy-done.3), calls=%async_computation | async-start | bytes 5242880 | tf_op jit(solution)/shard_map/all_to_all | solution.py:408
  50.0 47.5 %collective-permute-start.14 = (bf16[1024,256]{1,0:T(8,128)(2,1)}, bf16[1024,256]{1,0:T(8,128)(2,1)}, u32[]{:S(2)}, u32[]{:S(2)}) collective-permute-start(bf16[1024,256]{1,0:T(8,128)(2,1)} %slice.97), channel_id=1, source_target_pairs={{0,1},{8,9},{16,17},{24,25}} | collective-permute-start | bytes 1572872 | tf_op jit(solution)/shard_map/ppermute | solution.py:389
  56.1 37.5 %collective-permute-start.3 = (bf16[2,256,256]{2,1,0:T(8,128)(2,1)S(1)}, bf16[2,256,256]{2,1,0:T(8,128)(2,1)S(1)}, u32[]{:S(2)}, u32[]{:S(2)}) collective-permute-start(bf16[2,256,256]{2,1,0:T(8,128)(2,1)S(1)} %pad_maximum_fusion.6), channel_id=1, source_target_pairs={{0,1},{8,9},{16,17},{24,25}} | collective-permute-start | bytes 786440 | tf_op jit(solution)/shard_map/ppermute | solution.py:371
  98.7 24.0 %collective-permute-start.15 = (bf16[1024,256]{1,0:T(8,128)(2,1)S(1)}, bf16[1024,256]{1,0:T(8,128)(2,1)S(1)}, u32[]{:S(2)}, u32[]{:S(2)}) collective-permute-start(bf16[1024,256]{1,0:T(8,128)(2,1)S(1)} %slice_select_fusion.1), channel_id=1, source_target_pairs={{0,2},{1,3},{8,10},{9,11},{16,18},{17,19},{24,26},{25,27}} | collective-permute-start | bytes 1572872 | tf_op jit(solution)/shard_map/ppermute | solution.py:392
  100.0 34.0 %collective-permute-start.16 = (bf16[1024,256]{1,0:T(8,128)(2,1)S(1)}, bf16[1024,256]{1,0:T(8,128)(2,1)S(1)}, u32[]{:S(2)}, u32[]{:S(2)}) collective-permute-start(bf16[1024,256]{1,0:T(8,128)(2,1)S(1)} %slice_select_fusion.1), channel_id=1, source_target_pairs={{0,4},{1,5},{8,12},{9,13},{16,20},{17,21},{24,28},{25,29}} | collective-permute-start | bytes 1572872 | tf_op jit(solution)/shard_map/ppermute | solution.py:392
  101.3 43.9 %collective-permute-start.17 = (bf16[1024,256]{1,0:T(8,128)(2,1)S(1)}, bf16[1024,256]{1,0:T(8,128)(2,1)S(1)}, u32[]{:S(2)}, u32[]{:S(2)}) collective-permute-start(bf16[1024,256]{1,0:T(8,128)(2,1)S(1)} %slice_select_fusion.1), channel_id=1, source_target_pairs={{0,6},{1,7},{8,14},{9,15},{16,22},{17,23},{24,30},{25,31}} | collective-permute-start | bytes 1572872 | tf_op jit(solution)/shard_map/ppermute | solution.py:392
  116.6 45.1 %collective-permute-start.7 = (bf16[3,256,256]{2,1,0:T(8,128)(2,1)}, bf16[3,256,256]{2,1,0:T(8,128)(2,1)S(1)}, u32[]{:S(2)}, u32[]{:S(2)}) collective-permute-start(bf16[3,256,256]{2,1,0:T(8,128)(2,1)} %get-tuple-element.49), channel_id=1, source_target_pairs={{0,2},{1,3},{2,0},{3,1},{4,6},{5,7},{6,4},{7,5},{8,10},{9,11},{10,... | collective-permute-start | bytes 1179656 | tf_op jit(solution)/shard_map/ppermute | solution.py:413
  116.6 48.0 %collective-permute-start.8 = (bf16[3,256,256]{2,1,0:T(8,128)(2,1)}, bf16[3,256,256]{2,1,0:T(8,128)(2,1)}, u32[]{:S(2)}, u32[]{:S(2)}) collective-permute-start(bf16[3,256,256]{2,1,0:T(8,128)(2,1)} %get-tuple-element.48), channel_id=1, source_target_pairs={{0,4},{1,5},{2,6},{3,7},{4,0},{5,1},{6,2},{7,3},{8,12},{9,13},{10,... | collective-permute-start | bytes 1179656 | tf_op jit(solution)/shard_map/ppermute | solution.py:413
  146.1 81.9 %collective-permute-start.18 = (bf16[1024,256]{1,0:T(8,128)(2,1)}, bf16[1024,256]{1,0:T(8,128)(2,1)}, u32[]{:S(2)}, u32[]{:S(2)}) collective-permute-start(bf16[1024,256]{1,0:T(8,128)(2,1)} %add_select_fusion), channel_id=1, source_target_pairs={{0,1},{1,0},{2,3},{3,2},{4,5},{5,4},{6,7},{7,6},{8,9},{9,8},{10,11... | collective-permute-start | bytes 1572872 | tf_op jit(solution)/shard_map/ppermute | solution.py:399
  162.5 39.0 %collective-permute-start.1 = (bf16[3,256,256]{2,1,0:T(8,128)(2,1)}, bf16[3,256,256]{2,1,0:T(8,128)(2,1)}, u32[]{:S(2)}, u32[]{:S(2)}) collective-permute-start(bf16[3,256,256]{2,1,0:T(8,128)(2,1)} %get-tuple-element.52), channel_id=1, source_target_pairs={{0,4},{1,5},{2,6},{3,7},{4,0},{5,1},{6,2},{7,3},{8,12},{9,13},{10,... | collective-permute-start | bytes 1179656 | tf_op jit(solution)/shard_map/ppermute | solution.py:413
  164.7 36.8 %collective-permute-start.2 = (bf16[3,256,256]{2,1,0:T(8,128)(2,1)}, bf16[3,256,256]{2,1,0:T(8,128)(2,1)}, u32[]{:S(2)}, u32[]{:S(2)}) collective-permute-start(bf16[3,256,256]{2,1,0:T(8,128)(2,1)} %get-tuple-element.51), channel_id=1, source_target_pairs={{0,6},{1,7},{2,4},{3,5},{4,2},{5,3},{6,0},{7,1},{8,14},{9,15},{10,... | collective-permute-start | bytes 1179656 | tf_op jit(solution)/shard_map/ppermute | solution.py:413
  176.6 49.3 %collective-permute-start.10 = (bf16[2,256,256]{2,1,0:T(8,128)(2,1)}, bf16[2,256,256]{2,1,0:T(8,128)(2,1)}, u32[]{:S(2)}, u32[]{:S(2)}) collective-permute-start(bf16[2,256,256]{2,1,0:T(8,128)(2,1)} %get-tuple-element.32), channel_id=1, source_target_pairs={{0,16},{8,24},{16,0},{24,8},{1,17},{9,25},{17,1},{25,9},{2,18},{10... | collective-permute-start | bytes 786440 | tf_op jit(solution)/shard_map/ppermute | solution.py:423
  207.2 26.3 %all-to-all-start.1 = ((f32[32,8,128]{2,1,0:T(8,128)}), f32[32,8,128]{2,1,0:T(8,128)S(1)}, u32[]{:S(2)}, u32[]{:S(2)}) async-start(f32[32,8,128]{2,1,0:T(8,128)} %broadcast_in_dim.21), calls=%async_computation.1 | async-start | bytes 262144 | tf_op jit(solution)/shard_map/all_to_all | solution.py:418
  256.2 79.9 %all-to-all-start.4 = ((bf16[8,256,256]{2,1,0:T(8,128)(2,1)}), bf16[8,256,256]{2,1,0:T(8,128)(2,1)}, u32[]{:S(2)}, u32[]{:S(2)}) async-start(bf16[8,256,256]{2,1,0:T(8,128)(2,1)} %bitcast.48), calls=%async_computation.4 | async-start | bytes 2097152 | tf_op jit(solution)/shard_map/all_to_all | solution.py:452
  269.5 28.8 %collective-permute-start.30 = (bf16[256,512]{1,0:T(8,128)(2,1)S(1)}, bf16[256,512]{1,0:T(8,128)(2,1)}, u32[]{:S(2)}, u32[]{:S(2)}) collective-permute-start(bf16[256,512]{1,0:T(8,128)(2,1)S(1)} %advance_one.1), channel_id=1, source_target_pairs={{0,1},{1,0},{2,9},{3,8},{4,17},{5,16},{6,25},{7,24},{8,3},{9,2},{1... | collective-permute-start | bytes 786440 | tf_op jit(solution)/shard_map/ppermute | solution.py:442
  270.5 57.1 %collective-permute-start.31 = (bf16[256,512]{1,0:T(8,128)(2,1)S(1)}, bf16[256,512]{1,0:T(8,128)(2,1)S(1)}, u32[]{:S(2)}, u32[]{:S(2)}) collective-permute-start(bf16[256,512]{1,0:T(8,128)(2,1)S(1)} %advance_one.1), channel_id=1, source_target_pairs={{0,2},{1,3},{2,10},{3,11},{4,18},{5,19},{6,26},{7,27},{8,0},{9,1},... | collective-permute-start | bytes 786440 | tf_op jit(solution)/shard_map/ppermute | solution.py:442
  270.5 63.5 %collective-permute-start.32 = (bf16[256,512]{1,0:T(8,128)(2,1)S(1)}, bf16[256,512]{1,0:T(8,128)(2,1)S(1)}, u32[]{:S(2)}, u32[]{:S(2)}) collective-permute-start(bf16[256,512]{1,0:T(8,128)(2,1)S(1)} %advance_one.1), channel_id=1, source_target_pairs={{0,3},{1,2},{2,11},{3,10},{4,19},{5,18},{6,27},{7,26},{8,1},{9,0},... | collective-permute-start | bytes 786440 | tf_op jit(solution)/shard_map/ppermute | solution.py:442
  272.8 61.9 %collective-permute-start.33 = (bf16[256,512]{1,0:T(8,128)(2,1)S(1)}, bf16[256,512]{1,0:T(8,128)(2,1)S(1)}, u32[]{:S(2)}, u32[]{:S(2)}) collective-permute-start(bf16[256,512]{1,0:T(8,128)(2,1)S(1)} %advance_one.1), channel_id=1, source_target_pairs={{0,4},{1,5},{2,12},{3,13},{4,20},{5,21},{6,28},{7,29},{8,6},{9,7},... | collective-permute-start | bytes 786440 | tf_op jit(solution)/shard_map/ppermute | solution.py:442
  285.0 50.4 %collective-permute-start.34 = (bf16[256,512]{1,0:T(8,128)(2,1)S(1)}, bf16[256,512]{1,0:T(8,128)(2,1)S(1)}, u32[]{:S(2)}, u32[]{:S(2)}) collective-permute-start(bf16[256,512]{1,0:T(8,128)(2,1)S(1)} %advance_one.1), channel_id=1, source_target_pairs={{0,5},{1,4},{2,13},{3,12},{4,21},{5,20},{6,29},{7,28},{8,7},{9,6},... | collective-permute-start | bytes 786440 | tf_op jit(solution)/shard_map/ppermute | solution.py:442
  298.3 40.5 %collective-permute-start.35 = (bf16[256,512]{1,0:T(8,128)(2,1)S(1)}, bf16[256,512]{1,0:T(8,128)(2,1)S(1)}, u32[]{:S(2)}, u32[]{:S(2)}) collective-permute-start(bf16[256,512]{1,0:T(8,128)(2,1)S(1)} %advance_one.1), channel_id=1, source_target_pairs={{0,6},{1,7},{2,14},{3,15},{4,22},{5,23},{6,30},{7,31},{8,4},{9,5},... | collective-permute-start | bytes 786440 | tf_op jit(solution)/shard_map/ppermute | solution.py:442
  327.5 43.1 %collective-permute-start.36 = (bf16[256,512]{1,0:T(8,128)(2,1)S(1)}, bf16[256,512]{1,0:T(8,128)(2,1)}, u32[]{:S(2)}, u32[]{:S(2)}) collective-permute-start(bf16[256,512]{1,0:T(8,128)(2,1)S(1)} %advance_one.1), channel_id=1, source_target_pairs={{0,7},{1,6},{2,15},{3,14},{4,23},{5,22},{6,31},{7,30},{8,5},{9,4},... | collective-permute-start | bytes 786440 | tf_op jit(solution)/shard_map/ppermute | solution.py:442
  386.3 31.9 %collective-permute-start.37 = (bf16[256,1024]{1,0:T(8,128)(2,1)S(1)}, bf16[256,1024]{1,0:T(8,128)(2,1)S(1)}, u32[]{:S(2)}, u32[]{:S(2)}) collective-permute-start(bf16[256,1024]{1,0:T(8,128)(2,1)S(1)} %get-tuple-element.44), channel_id=1, source_target_pairs={{16,0},{24,8},{17,1},{25,9},{18,2},{26,10},{19,3},{27,11},{20,4},{... | collective-permute-start | bytes 1572872 | tf_op jit(solution)/shard_map/ppermute | solution.py:467
  387.6 29.0 %collective-permute-start.12 = (bf16[2,256,256]{2,1,0:T(8,128)(2,1)S(1)}, bf16[2,256,256]{2,1,0:T(8,128)(2,1)S(1)}, u32[]{:S(2)}, u32[]{:S(2)}) collective-permute-start(bf16[2,256,256]{2,1,0:T(8,128)(2,1)S(1)} %copy-done.12), channel_id=1, source_target_pairs={{0,16},{8,24},{16,0},{24,8},{1,17},{9,25},{17,1},{25,9},{2,18},{10... | collective-permute-start | bytes 786440 | tf_op jit(solution)/shard_map/ppermute | solution.py:423
  (39 other events, 413.3 us)

commit v2 on v1

--- a/solution.py
+++ b/solution.py
@@ -59,87 +59,55 @@
     )(limit, tokens)
 
 
-def moments_body(ids_ref, x_ref, l_ref, o_ref):
+def stats_body(x_ref, l_ref, f_ref, b_ref, o_ref, t_ref, lead_image):
     groups, _, count, bs = x_ref.shape
+    k = pl.program_id(0)
     cols = x_ref[:, 0].reshape(groups * count, bs)
     lead = l_ref[:, 0].reshape(groups * count, bs)
-    o_ref[0, 0] = dot(cols, cols, tn).astype(bf16)
-    o_ref[0, 1] = dot(lead, cols, tn).astype(bf16)
-    o_ref[0, 2] = dot(lead, lead, tn).astype(bf16)
-
-
-def raw_moments(ids, owned):
+
+    @pl.when(k == 0)
+    def _():
+        lead_image[...] = dot(lead, b_ref[...]).astype(bf16)
+        t_ref[...] = jnp.zeros_like(t_ref)
+
+    image = (dot(cols, f_ref[0, :, :bs]) + dot(lead, f_ref[0, :, bs:])).astype(bf16)
+    o_ref[0, 0] = dot(image, image, tn).astype(bf16)
+    o_ref[0, 1] = dot(lead_image[...], image, tn).astype(bf16)
+    wide = image.astype(f32)
+    t_ref[...] = t_ref[...] + jnp.sum(wide * wide)
+
+
+def stats(ids, owned, blocks, lead):
     groups, slots, count, bs = owned.shape
     zs = slots - 1
+
+    def body(ids_ref, *refs):
+        stats_body(*refs)
+
     return pl.pallas_call(
-        moments_body,
+        body,
         grid_spec=pltpu.PrefetchScalarGridSpec(
             num_scalar_prefetch=1,
             grid=(zs,),
             in_specs=[
                 pl.BlockSpec((groups, 1, count, bs), lambda k, ids: (0, ids[0] ^ k, 0, 0)),
                 pl.BlockSpec((groups, 1, count, bs), lambda k, ids: (0, zs, 0, 0)),
+                pl.BlockSpec((1, bs, 2 * bs), lambda k, ids: (k, 0, 0)),
+                pl.BlockSpec((bs, bs), lambda k, ids: (0, 0)),
             ],
-            out_specs=pl.BlockSpec((1, 3, bs, bs), lambda k, ids: (k, 0, 0, 0)),
-        ),
-        out_shape=jax.ShapeDtypeStruct((zs, 3, bs, bs), bf16),
-        compiler_params=params("arbitrary"),
-        name="raw_moments",
-    )(ids, owned, owned)
-
-
-def image_stats_body(count, ids_ref, sc_ref, *refs):
-    parts = refs[:count]
-    fac_ref, lead_ref, h_ref, hb_ref, tr_ref = refs[count:]
-    bs = lead_ref.shape[0]
-    keep = sc_ref[1]
-    total = parts[0][...].astype(f32)
-    for part in parts[1:]:
-        total = total + part[...].astype(f32)
-    fac = fac_ref[0]
-    diag = fac[:, :bs]
-    side = fac[:, bs:] * keep
-    gram = jnp.sum(diag * diag) + jnp.sum(side * side)
-    bn = diag.astype(bf16).astype(f32)
-    pn = side.astype(bf16).astype(f32)
-    b0 = lead_ref[...].astype(f32)
-    mm = functools.partial(dot, precision=highest)
-    t1 = mm(total[0], bn) + mm(total[1], pn, tn)
-    t0 = mm(total[1], bn) + mm(total[2], pn)
-    own = (mm(bn, t1, tn) + mm(pn, t0, tn)) * sc_ref[0]
-    cross = mm(b0, t0, tn) * sc_ref[0]
-    h_ref[0] = own
-    h_ref[1] = cross
-    hb_ref[0] = own.astype(bf16)
-    hb_ref[1] = cross.astype(bf16)
-    row = lax.broadcasted_iota(jnp.int32, (bs, bs), 0)
-    col = lax.broadcasted_iota(jnp.int32, (bs, bs), 1)
-    trace = jnp.sum(jnp.where(row == col, own, 0.0))
-    top = lax.broadcasted_iota(jnp.int32, (8, 128), 0)
-    tr_ref[...] = jnp.where(top == 0, trace, gram)
-
-
-def image_stats(ids, scalars, parts, factor, lead):
-    bs = lead.shape[0]
-    whole = lambda shape: pl.BlockSpec(shape, lambda i, ids: (0,) * len(shape))
-    return pl.pallas_call(
-        functools.partial(image_stats_body, len(parts)),
-        grid_spec=pltpu.PrefetchScalarGridSpec(
-            num_scalar_prefetch=1,
-            grid=(1,),
-            in_specs=[pl.BlockSpec(memory_space=pltpu.SMEM)]
-            + [whole((3, bs, bs)) for _ in parts]
-            + [pl.BlockSpec((1, bs, 2 * bs), lambda i, ids: (ids[1], 0, 0)), whole((bs, bs))],
-            out_specs=[whole((2, bs, bs)), whole((2, bs, bs)), whole((8, 128))],
+            out_specs=[
+                pl.BlockSpec((1, 2, bs, bs), lambda k, ids: (k, 0, 0, 0)),
+                pl.BlockSpec((8, 128), lambda k, ids: (0, 0)),
+            ],
+            scratch_shapes=[pltpu.VMEM((groups * count, bs), bf16)],
         ),
         out_shape=[
-            jax.ShapeDtypeStruct((2, bs, bs), f32),
-            jax.ShapeDtypeStruct((2, bs, bs), bf16),
+            jax.ShapeDtypeStruct((zs, 2, bs, bs), bf16),
             jax.ShapeDtypeStruct((8, 128), f32),
         ],
         compiler_params=params("arbitrary"),
-        name="image_stats",
-    )(ids, scalars, *parts, factor, lead)
+        name="plane_stats",
+    )(ids, owned, owned, blocks, lead)
 
 
 def advance_block(width, own, cross, fac, mom, b0, other_h, other_g, keep):
@@ -168,7 +136,6 @@
 
 
 def advance_body(width, ids_ref, sc_ref, h_ref, fac_ref, mom_ref, lead_ref, fn_ref, mn_ref, fb_ref):
-    blocks = lead_ref.shape[0]
     bs = lead_ref.shape[0]
     j = order_of(ids_ref, pl.program_id(0))
     keep = jnp.where(ids_ref[2] + j > 0, 1.0, 0.0)
@@ -215,39 +182,6 @@
         ],
         compiler_params=params("arbitrary"),
         name="advance_all",
-    )(ids, scalars, stats, factor, moment, lead)
-
-
-def advance_one_body(width, ids_ref, sc_ref, h_ref, fac_ref, mom_ref, lead_ref, fb_ref):
-    bs = lead_ref.shape[0]
-    keep = jnp.where(ids_ref[2] + ids_ref[1] > 0, 1.0, 0.0)
-    _, _, new_d, new_s = advance_block(
-        width, h_ref[0], h_ref[1], fac_ref[0], mom_ref[0], lead_ref[...], sc_ref[0], sc_ref[1], keep
-    )
-    fb_ref[:, :bs] = new_d.astype(bf16)
-    fb_ref[:, bs:] = new_s.astype(bf16)
-
-
-def advance_one(width, ids, scalars, stats, factor, moment, lead):
-    blocks, bs, wide = factor.shape
-    spec = pl.BlockSpec((1, bs, wide), lambda i, ids: (ids[1], 0, 0))
-    return pl.pallas_call(
-        functools.partial(advance_one_body, width),
-        grid_spec=pltpu.PrefetchScalarGridSpec(
-            num_scalar_prefetch=1,
-            grid=(1,),
-            in_specs=[
-                pl.BlockSpec(memory_space=pltpu.SMEM),
-                pl.BlockSpec((2, bs, bs), lambda i, ids: (0, 0, 0)),
-                spec,
-                spec,
-                pl.BlockSpec((bs, bs), lambda i, ids: (0, 0)),
-            ],
-            out_specs=pl.BlockSpec((bs, wide), lambda i, ids: (0, 0)),
-        ),
-        out_shape=jax.ShapeDtypeStruct((bs, wide), bf16),
-        compiler_params=params("arbitrary"),
-        name="advance_one",
     )(ids, scalars, stats, factor, moment, lead)
 
 
@@ -297,19 +231,21 @@
 
 
 def row_of(ids, k):
-    q = ids[3] ^ k
-    return (q & 1) * ids[4] + (q >> 1)
-
-
-def rows_body(ids_ref, s_ref, l_ref, c_ref, p_ref, u_ref, acc_ref):
+    per = ids[4]
+    return ((ids[3] & 1) ^ (k // per)) * per + k % per
+
+
+def rows_body(ids_ref, s_ref, g_ref, l_ref, c_ref, p_ref, u_ref, acc_ref):
     k = pl.program_id(0)
     bs = l_ref.shape[0]
     cd = c_ref[0, :, :bs]
     cs = c_ref[0, :, bs:]
-    third = (dot(cd, s_ref[...], tn) + dot(cs, l_ref[...], tn)).astype(bf16)
+    lead = jnp.where(ids_ref[3] == 0, g_ref[...], s_ref[:, :bs])
+    second = jnp.concatenate([lead, s_ref[:, bs:]], axis=1)
+    third = (dot(cd, second, tn) + dot(cs, l_ref[...], tn)).astype(bf16)
     fourth = dot(cd, third)
     p_ref[...] = fourth.astype(bf16)
-    is_first = (ids_ref[5] == 0) & (row_of(ids_ref, k) == 0)
+    is_first = (ids_ref[1] == 0) & (row_of(ids_ref, k) == 0)
     term = dot(cs, third) + fourth * jnp.where(is_first, 1.0, 0.0)
 
     @pl.when(k == 0)
@@ -325,7 +261,7 @@
         u_ref[...] = acc_ref[...].astype(bf16)
 
 
-def rows(ids, second, lead, cb):
+def rows(ids, second, gathered, lead, cb):
     count, wide = second.shape
     blocks, bs, _ = cb.shape
     spec = pl.BlockSpec((bs, wide), lambda k, ids: (row_of(ids, k), 0))
@@ -335,7 +271,12 @@
         grid_spec=pltpu.PrefetchScalarGridSpec(
             num_scalar_prefetch=1,
             grid=(blocks,),
-            in_specs=[spec, whole, pl.BlockSpec((1, bs, 2 * bs), lambda k, ids: (k, 0, 0))],
+            in_specs=[
+                spec,
+                pl.BlockSpec((bs, bs), lambda k, ids: (row_of(ids, k), 0)),
+                whole,
+                pl.BlockSpec((1, bs, 2 * bs), lambda k, ids: (k, 0, 0)),
+            ],
             out_specs=[spec, whole],
             scratch_shapes=[pltpu.VMEM((bs, wide), f32)],
         ),
@@ -345,7 +286,41 @@
         ],
         compiler_params=params("arbitrary"),
         name="row_products",
-    )(ids, second, lead, cb)
+    )(ids, second, gathered, lead, cb)
+
+
+def put_top_body(ids_ref, p_ref, low_ref, high_ref, o_ref):
+    half = low_ref.shape[0]
+    first = ids_ref[1] == 0
+
+    @pl.when(first)
+    def _():
+        o_ref[:half] = low_ref[...]
+        o_ref[half:] = high_ref[...]
+
+    @pl.when(jnp.logical_not(first))
+    def _():
+        o_ref[...] = p_ref[...]
+
+
+def put_top(ids, tile, low, high):
+    half, wide = low.shape
+    top = pl.BlockSpec((2 * half, wide), lambda i, ids: (0, 0))
+    part = pl.BlockSpec((half, wide), lambda i, ids: (0, 0))
+    return pl.pallas_call(
+        put_top_body,
+        grid_spec=pltpu.PrefetchScalarGridSpec(
+            num_scalar_prefetch=1, grid=(1,), in_specs=[top, part, part], out_specs=top
+        ),
+        out_shape=jax.ShapeDtypeStruct(tile.shape, tile.dtype),
+        input_output_aliases={1: 0},
+        compiler_params=params("arbitrary"),
+        name="put_top",
+    )(ids, tile, low, high)
+
+
+def after(value, *earlier):
+    return lax.optimization_barrier((value,) + earlier)[0]
 
 
 def planned(acts, out_grads, token_counts, k_factor, c_factor, k_moment, c_moment, grad_weight):
@@ -360,16 +335,17 @@
     z = s // xs
     flat = lambda dd, ss: dd * shards + ss
     plane = [[flat(dd, zz * xs + xx) for dd in range(ds) for xx in range(xs)] for zz in range(zs)]
-    ids = jnp.stack([z, d, s * ds, s, jnp.int32(ds), d]).astype(jnp.int32)
+    flip_x = [(i, i ^ 1) for i in range(shards)]
+    ids = jnp.stack([z, d, s * ds, s, jnp.int32(ds)]).astype(jnp.int32)
     token_total = jnp.sum(token_counts).astype(f32)
     valid = jnp.sum(jnp.where(lax.iota(jnp.int32, ds) == d, token_counts, 0))
     limit = (valid - s * tok_dev).reshape(1).astype(jnp.int32)
-    keep = jnp.where(s * ds + d > 0, 1.0, 0.0)
-    stat_scalars = jnp.stack([1.0 / token_total, keep]).astype(f32)
-
-    def to_all_shards(value):
-        over_x = lax.ppermute(value, "fsdp", [(0, 1)])
-        value = jnp.where(s == 0, value, over_x)
+
+    def along_z(value, k):
+        pairs = [(zz * xs + xx, (zz ^ k) * xs + xx) for zz in range(zs) for xx in range(xs)]
+        return lax.ppermute(value, "fsdp", pairs)
+
+    def from_plane_0(value):
         got = [
             lax.ppermute(value, "fsdp", [(xx, zz * xs + xx) for xx in range(xs)])
             for zz in range(1, zs)
@@ -379,96 +355,117 @@
             out = out + g
         return jnp.where(z == 0, value, out)
 
-    leads = jnp.stack([k_factor[0, :, :bs], c_factor[0, :, :bs]]).astype(bf16)
-    leads = to_all_shards(leads)
-    lead_k, lead_c = leads[0], leads[1]
-
-    def grad_lead_all():
-        value = grad_weight[:, :bs]
-        half = value.shape[0] // xs
-        over_x = lax.ppermute(value[half:], "fsdp", [(0, 1)])
-        mine = jnp.where(s == 0, value[:half], over_x)
-        got = [
-            lax.ppermute(mine, "fsdp", [(xx, zz * xs + xx) for xx in range(xs)])
-            for zz in range(1, zs)
-        ]
-        out = got[0]
-        for g in got[1:]:
-            out = out + g
-        mine = jnp.where(z == 0, mine, out)
-        other = lax.ppermute(mine, "fsdp", [(i, i ^ 1) for i in range(shards)])
-        low = jnp.where(x == 0, mine, other)
-        high = jnp.where(x == 0, other, mine)
-        return jnp.concatenate([low, high], axis=0)
-
-    grad_lead = grad_lead_all()
-
-    def side(tokens, factor, lead):
-        packed = pack(limit, tokens, zs, xs, ds, bs)
-        owned = lax.all_to_all(packed, both, 0, 0, tiled=True, axis_index_groups=plane)
-        raw = raw_moments(ids, owned)
-        parts = [raw[0]]
+    def block_along_z(factor, *earlier):
+        own = lax.dynamic_index_in_dim(factor, d, 0, keepdims=False)
+        side_keep = jnp.where(s * ds + d > 0, 1.0, 0.0)
+        own = jnp.concatenate([own[:, :bs], own[:, bs:] * side_keep], axis=1).astype(bf16)
+        own = after(own, *earlier)
+        return jnp.stack([own] + [along_z(own, k) for k in range(1, zs)])
+
+    def sum_along_z(partial):
+        total = partial[0].astype(f32)
         for k in range(1, zs):
-            pairs = [(zz * xs + xx, (zz ^ k) * xs + xx) for zz in range(zs) for xx in range(xs)]
-            parts.append(lax.ppermute(raw[k], "fsdp", pairs))
-        return image_stats(ids, stat_scalars, parts, factor, lead)
-
-    def totals(traces):
-        spread = jnp.broadcast_to(traces[None], (ds * shards,) + traces.shape)
-        got = lax.all_to_all(spread, both, 0, 0, tiled=True)
-        summed = jnp.sum(got, axis=0)
-        return summed[:2, 0]
+            total = total + along_z(partial[k], k).astype(f32)
+        return (total / token_total).astype(bf16)
 
     def over_dp(value):
         pair = jnp.stack([value, lax.ppermute(value, "dp", [(i, i ^ 2) for i in range(ds)])])
         other = lax.ppermute(pair, "dp", [(i, i ^ 1) for i in range(ds)])
         return jnp.concatenate([pair, other], axis=0)
 
+    def gram_part(factor):
+        block_ids = s * ds + lax.iota(jnp.int32, ds)
+        keep = (block_ids > 0).astype(f32)[:, None, None]
+        side = factor[:, :, bs:] * keep
+        return (jnp.sum(factor[:, :, :bs] ** 2) + jnp.sum(side * side)) / ds
+
+    def exchange(packed):
+        return lax.all_to_all(packed, both, 0, 0, tiled=True, axis_index_groups=plane)
+
+    leads = jnp.stack([k_factor[0, :, :bs], c_factor[0, :, :bs]]).astype(bf16)
+    leads = jnp.where(s == 0, leads, lax.ppermute(leads, "fsdp", [(0, 1)]))
+    leads = from_plane_0(leads)
+    lead_k, lead_c = leads[0], leads[1]
+    grad_half = grad_weight.shape[0] // xs
+    grad_low = grad_weight[:grad_half, :bs]
+    grad_high = lax.ppermute(grad_weight[grad_half:, :bs], "fsdp", [(0, 1)])
+    grad_mine = jnp.where(s == 0, grad_low, grad_high)
+
+    owned_k = exchange(pack(limit, acts, zs, xs, ds, bs))
+    blocks_k = block_along_z(k_factor)
+    packed_c = after(pack(limit, out_grads, zs, xs, ds, bs), owned_k)
+    owned_c = exchange(packed_c)
+    partial_k, square_k = stats(ids, owned_k, blocks_k, lead_k)
+    blocks_c = block_along_z(c_factor, owned_k)
+    stat_k = sum_along_z(partial_k)
+    grad_mine = from_plane_0(after(grad_mine, partial_k))
+    all_k = over_dp(stat_k)
+    gram_k = gram_part(k_factor)
+    gram_c = gram_part(c_factor)
+
+    partial_c, square_c = stats(ids, owned_c, blocks_c, lead_c)
+    rows8 = lax.broadcasted_iota(jnp.int32, (8, 128), 0)
+    sums = jnp.where(
+        rows8 == 0,
+        square_k,
+        jnp.where(rows8 == 1, square_c, jnp.where(rows8 == 2, gram_k, gram_c)),
+    )
+    sums = jnp.broadcast_to(sums[None], (ds * shards, 8, 128))
+    totals = jnp.sum(lax.all_to_all(sums, both, 0, 0, tiled=True), axis=0)[:, 0]
+    for_k = jnp.stack([totals[1] / token_total, totals[3]])
+    for_c = jnp.stack([totals[0] / token_total, totals[2]])
+    stat_c = sum_along_z(partial_c)
+
+    grad_other = lax.ppermute(after(grad_mine, owned_c), "fsdp", flip_x)
+    grad_lead = jnp.concatenate(
+        [jnp.where(x == 0, grad_mine, grad_other), jnp.where(x == 0, grad_other, grad_mine)], axis=0
+    )
     scale_width = float(width)
-    stat_k, stat_kb, trace_k = side(acts, k_factor, lead_k)
-    total_k = totals(trace_k)
-    all_k = over_dp(stat_kb)
-    stat_c, stat_cb, trace_c = side(out_grads, c_factor, lead_c)
-
-    c_block = advance_one(scale_width, ids, total_k, stat_c, c_factor, c_moment, lead_c)
-    fetched = []
-    for k in range(shards):
-        pairs = [
-            (flat(dd, zz * xs + xx), flat(zz, (dd * xs + xx) ^ k))
-            for dd in range(ds)
-            for zz in range(zs)
-            for xx in range(xs)
-        ]
-        fetched.append(lax.ppermute(c_block, both, pairs))
-    c_rows = jnp.stack(fetched)
-
-    total_c = totals(trace_c)
     k_factor_new, k_moment_new, kb = advance_all(
-        scale_width, ids, total_c, all_k, k_factor, k_moment, lead_k
+        scale_width, ids, for_k, all_k, k_factor, k_moment, lead_k
     )
     second, term = columns(ids, grad_weight, grad_lead, kb)
     count = grad_weight.shape[0]
     by_shard = term.reshape(shards, count // shards, bs)
     got = lax.all_to_all(by_shard, "fsdp", 0, 0, tiled=True)
     block_sum = jnp.sum(got.astype(f32), axis=0).astype(bf16)
-    blocks = [block_sum] + [lax.ppermute(block_sum, "fsdp", [(k, 0)]) for k in range(1, shards)]
-    lead_cols = jnp.where(s == 0, jnp.concatenate(blocks, axis=0), second[:, :bs])
-    second = jnp.concatenate([lead_cols, second[:, bs:]], axis=1)
-    top = second[:bs]
-    lead_rows = jnp.where(d == 0, top, 0).astype(bf16)
-    for k in range(1, ds):
-        lead_rows = lead_rows + lax.ppermute(top, "dp", [(0, k)])
-
-    all_c = over_dp(stat_cb)
-    c_factor_new, c_moment_new, _ = advance_all(
-        scale_width, ids, total_k, all_c, c_factor, c_moment, lead_c
-    )
-    precond, up = rows(ids, second, lead_rows, c_rows)
-    over_y = lax.ppermute(up, "dp", [(2, 0), (3, 1)])
-    up_sum = up.astype(f32) + over_y.astype(f32)
-    over_core = lax.ppermute(up_sum.astype(bf16), "dp", [(1, 0)])
-    up_sum = (up_sum + over_core.astype(f32)).astype(bf16)
-    precond = precond.at[:bs].set(jnp.where(d == 0, up_sum, precond[:bs]))
+
+    all_c = over_dp(stat_c)
+    c_factor_new, c_moment_new, cb = advance_all(
+        scale_width, ids, for_c, all_c, c_factor, c_moment, lead_c
+    )
+    halves = []
+    for h in range(2):
+        turn = 2 * h
+        pairs = [
+            (flat(r ^ turn, zz * xs + xx), flat(zz, r * xs + xx))
+            for r in range(ds)
+            for zz in range(zs)
+            for xx in range(xs)
+        ]
+        halves.append(lax.ppermute(cb[h * (ds // 2) : (h + 1) * (ds // 2)], both, pairs))
+    others = [lax.ppermute(h, "fsdp", flip_x) for h in halves]
+    c_rows = jnp.concatenate(halves + others, axis=0)
+
+    pair = jnp.stack([block_sum, lax.ppermute(block_sum, "fsdp", [(2 * k + 1, 2 * k) for k in range(zs)])])
+    gathered = [pair] + [lax.ppermute(pair, "fsdp", [(xs * k, 0)]) for k in range(1, zs)]
+    gathered = jnp.concatenate(gathered, axis=0).reshape(count, bs)
+    top = jnp.concatenate([jnp.where(s == 0, block_sum, second[:bs, :bs]), second[:bs, bs:]], axis=1)
+    over_y = lax.ppermute(top, "dp", [(0, 2)])
+    top = jnp.where(d == 0, top, over_y)
+    over_core = lax.ppermute(top, "dp", [(0, 1), (2, 3)])
+    lead_rows = jnp.where(d % 2 == 0, top, over_core)
+
+    precond, up = rows(ids, second, gathered, lead_rows, c_rows)
+    half = bs // 2
+    core = d % 2
+    mine = jnp.where(core == 0, up[:half], up[half:])
+    theirs = jnp.where(core == 0, up[half:], up[:half])
+    mine = mine.astype(f32) + lax.ppermute(theirs, "dp", [(i, i ^ 1) for i in range(ds)])
+    low = mine.astype(bf16)
+    mine = (mine + lax.ppermute(low, "dp", [(2, 0), (3, 1)])).astype(bf16)
+    high = lax.ppermute(mine, "dp", [(1, 0)])
+    precond = put_top(ids, precond, mine, high)
     return (k_factor_new, c_factor_new, k_moment_new, c_moment_new, precond)
 
 

time: 430 us -> 335 us (0.78)
  the two profiles are of different devices: /device:TPU:1 before, /device:TPU:0 now
where the time goes in v2:
time: 335 us; the launch traced here: 333 us
  waiting for transfers between devices  139 us (41%)
  starting transfers between devices  96.3 us (29%)
  Pallas kernels  47.7 us (14%)
  other arithmetic  26 us (8%)
  local copies, waits for them, and re-layouts  17.6 us (5%)
  between operations  6.37 us (2%)
    ppermute x6, waiting for transfers between devices, from_plane_0(): lax.ppermute(value, 'fsdp', [(xx, zz * xs + xx) for xx in range(xs)])  23.9 us
    ppermute x1, waiting for transfers between devices, planned(): grad_high = lax.ppermute(grad_weight[grad_half:, :bs], 'fsdp', [(0, 1)])  22.5 us
    ppermute x3, waiting for transfers between devices, planned(): lax.ppermute(pair, 'fsdp', [(xs * k, 0)])  17.5 us
    ppermute x1, waiting for transfers between devices, planned(): leads = jnp.where(s == 0, leads, lax.ppermute(leads, 'fsdp', [(0, 1)]))  16.2 us
    ppermute x12, waiting for transfers between devices, along_z(): return lax.ppermute(value, 'fsdp', pairs)  15.9 us
    ppermute x6, starting transfers between devices, from_plane_0(): lax.ppermute(value, 'fsdp', [(xx, zz * xs + xx) for xx in range(xs)])  15.6 us
    ppermute x1, starting transfers between devices, planned(): over_y = lax.ppermute(top, 'dp', [(0, 2)])  15.5 us
    ppermute x2, waiting for transfers between devices, planned(): lax.ppermute(cb[h * (ds // 2):(h + 1) * (ds // 2)], both, pairs)  13.7 us
  transfers between devices with their start and end apart: 42, of which 19 were waited for; matrix products, arithmetic and copies ran while one was open for 10% of the time, Pallas kernels for 10%

profile of v2, /device:TPU:0, one launch (start us, length us, event | category | flops | bytes accessed | tf_op | source)
XLA Modules:
  0.0 332.7 jit_solution(9573530333184687242)
XLA Ops:
  6.1 5.2 %all-to-all-start = ((bf16[8,5,128,256]{3,2,1,0:T(8,128)(2,1)}), bf16[8,5,128,256]{3,2,1,0:T(8,128)(2,1)S(1)}, u32[]{:S(2)}, u32[]{:S(2)}) async-start(bf16[8,5,128,256]{3,2,1,0:T(8,128)(2,1)} %copy-done.3), calls=%async_computation | async-start | bytes 5242880 | tf_op jit(solution)/shard_map/all_to_all | solution.py:383
  22.1 4.6 %collective-permute-start.3 = (bf16[2,256,256]{2,1,0:T(8,128)(2,1)}, bf16[2,256,256]{2,1,0:T(8,128)(2,1)}, u32[]{:S(2)}, u32[]{:S(2)}) collective-permute-start(bf16[2,256,256]{2,1,0:T(8,128)(2,1)} %pad_maximum_fusion.10), channel_id=1, source_target_pairs={{0,1},{8,9},{16,17},{24,25}} | collective-permute-start | bytes 786440 | tf_op jit(solution)/shard_map/ppermute | solution.py:386
  30.0 16.2 %collective-permute-done.3 = bf16[2,256,256]{2,1,0:T(8,128)(2,1)} collective-permute-done((bf16[2,256,256]{2,1,0:T(8,128)(2,1)}, bf16[2,256,256]{2,1,0:T(8,128)(2,1)}, u32[]{:S(2)}, u32[]{:S(2)}) %collective-permute-start.3) | collective-permute-done | bytes 262176 | tf_op jit(solution)/shard_map/ppermute | solution.py:386
  62.1 5.9 %all-to-all-start.1 = ((bf16[8,5,128,256]{3,2,1,0:T(8,128)(2,1)}), bf16[8,5,128,256]{3,2,1,0:T(8,128)(2,1)}, u32[]{:S(2)}, u32[]{:S(2)}) async-start(bf16[8,5,128,256]{3,2,1,0:T(8,128)(2,1)} %copy-done.2), calls=%async_computation.1 | async-start | bytes 5242880 | tf_op jit(solution)/shard_map/all_to_all | solution.py:383
  75.5 6.1 %plane_stats.2 = (bf16[4,2,256,256]{3,2,1,0:T(8,128)(2,1)S(1)}, f32[8,128]{1,0:T(8,128)S(1)}) custom-call(s32[5]{0:T(128)S(1)} %stack.92.ids_ref, bf16[8,5,128,256]{3,2,1,0:T(8,128)(2,1)S(1)} %all-to-all-done.refs_0_.refs_1_, bf16[8,5,128,256]{3,2,1,0:T(8,128)(2,1)S(1)} %all-to-all-done.refs_0_.refs_1_, bf16[4,256,512]{2,1,0:T(8,128)(2,1)S(1)} %pad_maximum_fusion.1.refs_2_, ...), custom_call_target="tpu_custom_call" | custom-call | tf_op jit(solution)/shard_map/plane_stats/pallas_call | solution.py:87
  81.6 4.4 %collective-permute-start.10 = (bf16[2,256,256]{2,1,0:T(8,128)(2,1)S(1)}, bf16[2,256,256]{2,1,0:T(8,128)(2,1)S(1)}, u32[]{:S(2)}, u32[]{:S(2)}) collective-permute-start(bf16[2,256,256]{2,1,0:T(8,128)(2,1)S(1)} %get-tuple-element.56), channel_id=1, source_target_pairs={{0,2},{1,3},{2,0},{3,1},{4,6},{5,7},{6,4},{7,5},{8,10},{9,11},{10,... | collective-permute-start | bytes 786440 | tf_op jit(solution)/shard_map/ppermute | solution.py:346
  86.1 22.5 %collective-permute-done.20 = bf16[1024,256]{1,0:T(8,128)(2,1)S(1)} collective-permute-done((bf16[1024,256]{1,0:T(8,128)(2,1)}, bf16[1024,256]{1,0:T(8,128)(2,1)S(1)}, u32[]{:S(2)}, u32[]{:S(2)}) %collective-permute-start.20) | collective-permute-done | bytes 524320 | tf_op jit(solution)/shard_map/ppermute | solution.py:391
  109.8 6.3 %collective-permute-start.23 = (bf16[1024,256]{1,0:T(8,128)(2,1)S(1)}, bf16[1024,256]{1,0:T(8,128)(2,1)S(1)}, u32[]{:S(2)}, u32[]{:S(2)}) collective-permute-start(bf16[1024,256]{1,0:T(8,128)(2,1)S(1)} %slice_select_fusion), channel_id=1, source_target_pairs={{0,6},{1,7},{8,14},{9,15},{16,22},{17,23},{24,30},{25,31}} | collective-permute-start | bytes 1572872 | tf_op jit(solution)/shard_map/ppermute | solution.py:350
  132.1 11.2 %collective-permute-done.22 = bf16[1024,256]{1,0:T(8,128)(2,1)S(1)} collective-permute-done((bf16[1024,256]{1,0:T(8,128)(2,1)S(1)}, bf16[1024,256]{1,0:T(8,128)(2,1)S(1)}, u32[]{:S(2)}, u32[]{:S(2)}) %collective-permute-start.22) | collective-permute-done | bytes 524320 | tf_op jit(solution)/shard_map/ppermute | solution.py:350
  143.4 10.5 %collective-permute-done.21 = bf16[1024,256]{1,0:T(8,128)(2,1)} collective-permute-done((bf16[1024,256]{1,0:T(8,128)(2,1)S(1)}, bf16[1024,256]{1,0:T(8,128)(2,1)}, u32[]{:S(2)}, u32[]{:S(2)}) %collective-permute-start.21) | collective-permute-done | bytes 524320 | tf_op jit(solution)/shard_map/ppermute | solution.py:350
  155.8 7.1 %plane_stats.3 = (bf16[4,2,256,256]{3,2,1,0:T(8,128)(2,1)S(1)}, f32[8,128]{1,0:T(8,128)S(1)}) custom-call(s32[5]{0:T(128)S(1)} %stack.92.ids_ref, bf16[8,5,128,256]{3,2,1,0:T(8,128)(2,1)} %all-to-all-done.1.refs_0_.refs_1_, bf16[8,5,128,256]{3,2,1,0:T(8,128)(2,1)} %all-to-all-done.1.refs_0_.refs_1_, bf16[4,256,512]{2,1,0:T(8,128)(2,1)S(1)} %pad_maximum_fusion.2.refs_2_, ...), custom_call_target="tpu_custom_call" | custom-call | tf_op jit(solution)/shard_map/plane_stats/pallas_call | solution.py:87
  163.7 5.5 %all-to-all-start.2 = ((f32[32,8,128]{2,1,0:T(8,128)}), f32[32,8,128]{2,1,0:T(8,128)S(1)}, u32[]{:S(2)}, u32[]{:S(2)}) async-start(f32[32,8,128]{2,1,0:T(8,128)} %broadcast_in_dim.23), calls=%async_computation.2 | async-start | bytes 262144 | tf_op jit(solution)/shard_map/all_to_all | solution.py:414
  179.2 5.6 %advance_all.2 = (f32[4,256,512]{2,1,0:T(8,128)}, f32[4,256,512]{2,1,0:T(8,128)}, bf16[4,256,512]{2,1,0:T(8,128)(2,1)S(1)}) custom-call(s32[5]{0:T(128)S(1)} %stack.92.ids_ref, f32[2]{0:T(128)S(1)} %pad_maximum_fusion.13.sc_ref, bf16[4,2,256,256]{3,2,1,0:T(8,128)(2,1)S(1)} %pad_maximum_fusion.3.h_ref, f32[4,256,512]{2,1,0:T(8,128)S(1)} %copy-done, ...), custom_call_target="tpu_custom_call" | custom-call | tf_op jit(solution)/shard_map/advance_all/pallas_call | solution.py:164
  189.1 10.1 %collective-permute-done.16 = bf16[2,256,256]{2,1,0:T(8,128)(2,1)} collective-permute-done((bf16[2,256,256]{2,1,0:T(8,128)(2,1)}, bf16[2,256,256]{2,1,0:T(8,128)(2,1)}, u32[]{:S(2)}, u32[]{:S(2)}) %collective-permute-start.16) | collective-permute-done | bytes 262176 | tf_op jit(solution)/shard_map/ppermute | solution.py:346
  203.2 8.8 %column_products.1 = (bf16[2048,1024]{1,0:T(8,128)(2,1)}, bf16[2048,256]{1,0:T(8,128)(2,1)}) custom-call(s32[5]{0:T(128)S(1)} %stack.92.ids_ref, bf16[2048,1024]{1,0:T(8,128)(2,1)} %g_ref.1, bf16[2048,256]{1,0:T(8,128)(2,1)S(1)} %pad_maximum_fusion.5.l_ref, bf16[4,256,512]{2,1,0:T(8,128)(2,1)S(1)} %get-tuple-element.35.k_ref), custom_call_target="tpu_custom_call" | custom-call | tf_op jit(solution)/shard_map/column_products/pallas_call | solution.py:209
  219.6 5.6 %advance_all.3 = (f32[4,256,512]{2,1,0:T(8,128)}, f32[4,256,512]{2,1,0:T(8,128)}, bf16[4,256,512]{2,1,0:T(8,128)(2,1)S(1)}) custom-call(s32[5]{0:T(128)S(1)} %stack.92.ids_ref, f32[2]{0:T(128)S(1)} %pad_maximum_fusion.14.sc_ref, bf16[4,2,256,256]{3,2,1,0:T(8,128)(2,1)S(1)} %pad_maximum_fusion.4.h_ref, f32[4,256,512]{2,1,0:T(8,128)S(1)} %copy-done.1, ...), custom_call_target="tpu_custom_call" | custom-call | tf_op jit(solution)/shard_map/advance_all/pallas_call | solution.py:164
  232.1 13.7 %collective-permute-done.32 = bf16[2,256,512]{2,1,0:T(8,128)(2,1)S(1)} collective-permute-done((bf16[2,256,512]{2,1,0:T(8,128)(2,1)S(1)}, bf16[2,256,512]{2,1,0:T(8,128)(2,1)S(1)}, u32[]{:S(2)}, u32[]{:S(2)}) %collective-permute-start.32) | collective-permute-done | bytes 524320 | tf_op jit(solution)/shard_map/ppermute | solution.py:446
  248.7 6.0 %all-to-all-done.3 = bf16[8,256,256]{2,1,0:T(8,128)(2,1)} async-done(((bf16[8,256,256]{2,1,0:T(8,128)(2,1)}), bf16[8,256,256]{2,1,0:T(8,128)(2,1)}, u32[]{:S(2)}, u32[]{:S(2)}) %all-to-all-start.3) | async-done | bytes 1048608 | tf_op jit(solution)/shard_map/all_to_all | solution.py:430
  257.1 15.5 %collective-permute-start.29 = (bf16[256,1024]{1,0:T(8,128)(2,1)S(1)}, bf16[256,1024]{1,0:T(8,128)(2,1)S(1)}, u32[]{:S(2)}, u32[]{:S(2)}) collective-permute-start(bf16[256,1024]{1,0:T(8,128)(2,1)S(1)} %pad_maximum_fusion.8), channel_id=1, source_target_pairs={{0,16},{1,17},{2,18},{3,19},{4,20},{5,21},{6,22},{7,23}} | collective-permute-start | bytes 1572872 | tf_op jit(solution)/shard_map/ppermute | solution.py:454
  274.2 5.5 %collective-permute-done.25 = bf16[256,256]{1,0:T(8,128)(2,1)S(1)} collective-permute-done((bf16[256,256]{1,0:T(8,128)(2,1)S(1)}, bf16[256,256]{1,0:T(8,128)(2,1)S(1)}, u32[]{:S(2)}, u32[]{:S(2)}) %collective-permute-start.25) | collective-permute-done | bytes 131104 | tf_op jit(solution)/shard_map/ppermute | solution.py:450
  285.2 10.4 %collective-permute-done.26 = bf16[2,256,256]{2,1,0:T(8,128)(2,1)S(1)} collective-permute-done((bf16[2,256,256]{2,1,0:T(8,128)(2,1)S(1)}, bf16[2,256,256]{2,1,0:T(8,128)(2,1)S(1)}, u32[]{:S(2)}, u32[]{:S(2)}) %collective-permute-start.26) | collective-permute-done | bytes 262176 | tf_op jit(solution)/shard_map/ppermute | solution.py:451
  295.6 7.1 %collective-permute-done.27 = bf16[2,256,256]{2,1,0:T(8,128)(2,1)S(1)} collective-permute-done((bf16[2,256,256]{2,1,0:T(8,128)(2,1)S(1)}, bf16[2,256,256]{2,1,0:T(8,128)(2,1)S(1)}, u32[]{:S(2)}, u32[]{:S(2)}) %collective-permute-start.27) | collective-permute-done | bytes 262176 | tf_op jit(solution)/shard_map/ppermute | solution.py:451
  302.8 11.1 %row_products.1 = (bf16[2048,1024]{1,0:T(8,128)(2,1)}, bf16[256,1024]{1,0:T(8,128)(2,1)S(1)}) custom-call(s32[5]{0:T(128)S(1)} %stack.92.ids_ref, bf16[2048,1024]{1,0:T(8,128)(2,1)} %get-tuple-element.36.s_ref, bf16[2048,256]{1,0:T(8,128)(2,1)S(1)} %bitcast.55, bf16[256,1024]{1,0:T(8,128)(2,1)S(1)} %broadcast_select_fusion.1.l_ref, ...), custom_call_target="tpu_custom_call" | custom-call | tf_op jit(solution)/shard_map/row_products/pallas_call | solution.py:269
  317.0 9.8 %collective-permute-done.36 = bf16[128,1024]{1,0:T(8,128)(2,1)S(1)} collective-permute-done((bf16[128,1024]{1,0:T(8,128)(2,1)S(1)}, bf16[128,1024]{1,0:T(8,128)(2,1)S(1)}, u32[]{:S(2)}, u32[]{:S(2)}) %collective-permute-start.36) | collective-permute-done | bytes 262176 | tf_op jit(solution)/shard_map/ppermute | solution.py:466
  (156 shorter events, 111.6 us)
Async XLA Ops:
  6.1 56.0 %all-to-all-start = ((bf16[8,5,128,256]{3,2,1,0:T(8,128)(2,1)}), bf16[8,5,128,256]{3,2,1,0:T(8,128)(2,1)S(1)}, u32[]{:S(2)}, u32[]{:S(2)}) async-start(bf16[8,5,128,256]{3,2,1,0:T(8,128)(2,1)} %copy-done.3), calls=%async_computation | async-start | bytes 5242880 | tf_op jit(solution)/shard_map/all_to_all | solution.py:383
  15.1 35.8 %collective-permute-start.2 = (bf16[256,512]{1,0:T(8,128)(2,1)}, bf16[256,512]{1,0:T(8,128)(2,1)}, u32[]{:S(2)}, u32[]{:S(2)}) collective-permute-start(bf16[256,512]{1,0:T(8,128)(2,1)} %pad_maximum_fusion.9), channel_id=1, source_target_pairs={{0,6},{1,7},{2,4},{3,5},{4,2},{5,3},{6,0},{7,1},{8,14},{9,15},{10,... | collective-permute-start | bytes 786440 | tf_op jit(solution)/shard_map/ppermute | solution.py:346
  18.7 50.1 %collective-permute-start.1 = (bf16[256,512]{1,0:T(8,128)(2,1)}, bf16[256,512]{1,0:T(8,128)(2,1)}, u32[]{:S(2)}, u32[]{:S(2)}) collective-permute-start(bf16[256,512]{1,0:T(8,128)(2,1)} %pad_maximum_fusion.9), channel_id=1, source_target_pairs={{0,4},{1,5},{2,6},{3,7},{4,0},{5,1},{6,2},{7,3},{8,12},{9,13},{10,... | collective-permute-start | bytes 786440 | tf_op jit(solution)/shard_map/ppermute | solution.py:346
  18.7 54.0 %collective-permute-start = (bf16[256,512]{1,0:T(8,128)(2,1)}, bf16[256,512]{1,0:T(8,128)(2,1)}, u32[]{:S(2)}, u32[]{:S(2)}) collective-permute-start(bf16[256,512]{1,0:T(8,128)(2,1)} %pad_maximum_fusion.9), channel_id=1, source_target_pairs={{0,2},{1,3},{2,0},{3,1},{4,6},{5,7},{6,4},{7,5},{8,10},{9,11},{10,... | collective-permute-start | bytes 786440 | tf_op jit(solution)/shard_map/ppermute | solution.py:346
  22.1 24.1 %collective-permute-start.3 = (bf16[2,256,256]{2,1,0:T(8,128)(2,1)}, bf16[2,256,256]{2,1,0:T(8,128)(2,1)}, u32[]{:S(2)}, u32[]{:S(2)}) collective-permute-start(bf16[2,256,256]{2,1,0:T(8,128)(2,1)} %pad_maximum_fusion.10), channel_id=1, source_target_pairs={{0,1},{8,9},{16,17},{24,25}} | collective-permute-start | bytes 786440 | tf_op jit(solution)/shard_map/ppermute | solution.py:386
  46.9 27.1 %collective-permute-start.6 = (bf16[2,256,256]{2,1,0:T(8,128)(2,1)}, bf16[2,256,256]{2,1,0:T(8,128)(2,1)}, u32[]{:S(2)}, u32[]{:S(2)}) collective-permute-start(bf16[2,256,256]{2,1,0:T(8,128)(2,1)} %broadcast_select_fusion.6), channel_id=1, source_target_pairs={{0,6},{1,7},{8,14},{9,15},{16,22},{17,23},{24,30},{25,31}} | collective-permute-start | bytes 786440 | tf_op jit(solution)/shard_map/ppermute | solution.py:350
  48.9 25.1 %collective-permute-start.5 = (bf16[2,256,256]{2,1,0:T(8,128)(2,1)}, bf16[2,256,256]{2,1,0:T(8,128)(2,1)}, u32[]{:S(2)}, u32[]{:S(2)}) collective-permute-start(bf16[2,256,256]{2,1,0:T(8,128)(2,1)} %broadcast_select_fusion.6), channel_id=1, source_target_pairs={{0,4},{1,5},{8,12},{9,13},{16,20},{17,21},{24,28},{25,29}} | collective-permute-start | bytes 786440 | tf_op jit(solution)/shard_map/ppermute | solution.py:350
  50.9 23.2 %collective-permute-start.4 = (bf16[2,256,256]{2,1,0:T(8,128)(2,1)}, bf16[2,256,256]{2,1,0:T(8,128)(2,1)}, u32[]{:S(2)}, u32[]{:S(2)}) collective-permute-start(bf16[2,256,256]{2,1,0:T(8,128)(2,1)} %broadcast_select_fusion.6), channel_id=1, source_target_pairs={{0,2},{1,3},{8,10},{9,11},{16,18},{17,19},{24,26},{25,27}} | collective-permute-start | bytes 786440 | tf_op jit(solution)/shard_map/ppermute | solution.py:350
  62.1 93.7 %all-to-all-start.1 = ((bf16[8,5,128,256]{3,2,1,0:T(8,128)(2,1)}), bf16[8,5,128,256]{3,2,1,0:T(8,128)(2,1)}, u32[]{:S(2)}, u32[]{:S(2)}) async-start(bf16[8,5,128,256]{3,2,1,0:T(8,128)(2,1)} %copy-done.2), calls=%async_computation.1 | async-start | bytes 5242880 | tf_op jit(solution)/shard_map/all_to_all | solution.py:383
  68.8 39.8 %collective-permute-start.20 = (bf16[1024,256]{1,0:T(8,128)(2,1)}, bf16[1024,256]{1,0:T(8,128)(2,1)S(1)}, u32[]{:S(2)}, u32[]{:S(2)}) collective-permute-start(bf16[1024,256]{1,0:T(8,128)(2,1)} %slice.142), channel_id=1, source_target_pairs={{0,1},{8,9},{16,17},{24,25}} | collective-permute-start | bytes 1572872 | tf_op jit(solution)/shard_map/ppermute | solution.py:391
  75.3 34.4 %collective-permute-start.9 = (bf16[256,512]{1,0:T(8,128)(2,1)}, bf16[256,512]{1,0:T(8,128)(2,1)S(1)}, u32[]{:S(2)}, u32[]{:S(2)}) collective-permute-start(bf16[256,512]{1,0:T(8,128)(2,1)} %pad_maximum_fusion.11), channel_id=1, source_target_pairs={{0,6},{1,7},{2,4},{3,5},{4,2},{5,3},{6,0},{7,1},{8,14},{9,15},{10,... | collective-permute-start | bytes 786440 | tf_op jit(solution)/shard_map/ppermute | solution.py:346
  75.4 45.4 %collective-permute-start.8 = (bf16[256,512]{1,0:T(8,128)(2,1)}, bf16[256,512]{1,0:T(8,128)(2,1)S(1)}, u32[]{:S(2)}, u32[]{:S(2)}) collective-permute-start(bf16[256,512]{1,0:T(8,128)(2,1)} %pad_maximum_fusion.11), channel_id=1, source_target_pairs={{0,4},{1,5},{2,6},{3,7},{4,0},{5,1},{6,2},{7,3},{8,12},{9,13},{10,... | collective-permute-start | bytes 786440 | tf_op jit(solution)/shard_map/ppermute | solution.py:346
  81.6 28.1 %collective-permute-start.10 = (bf16[2,256,256]{2,1,0:T(8,128)(2,1)S(1)}, bf16[2,256,256]{2,1,0:T(8,128)(2,1)S(1)}, u32[]{:S(2)}, u32[]{:S(2)}) collective-permute-start(bf16[2,256,256]{2,1,0:T(8,128)(2,1)S(1)} %get-tuple-element.56), channel_id=1, source_target_pairs={{0,2},{1,3},{2,0},{3,1},{4,6},{5,7},{6,4},{7,5},{8,10},{9,11},{10,... | collective-permute-start | bytes 786440 | tf_op jit(solution)/shard_map/ppermute | solution.py:346
  86.0 30.1 %collective-permute-start.12 = (bf16[2,256,256]{2,1,0:T(8,128)(2,1)S(1)}, bf16[2,256,256]{2,1,0:T(8,128)(2,1)S(1)}, u32[]{:S(2)}, u32[]{:S(2)}) collective-permute-start(bf16[2,256,256]{2,1,0:T(8,128)(2,1)S(1)} %get-tuple-element.57), channel_id=1, source_target_pairs={{0,6},{1,7},{2,4},{3,5},{4,2},{5,3},{6,0},{7,1},{8,14},{9,15},{10,... | collective-permute-start | bytes 786440 | tf_op jit(solution)/shard_map/ppermute | solution.py:346
  116.1 27.3 %collective-permute-start.22 = (bf16[1024,256]{1,0:T(8,128)(2,1)S(1)}, bf16[1024,256]{1,0:T(8,128)(2,1)S(1)}, u32[]{:S(2)}, u32[]{:S(2)}) collective-permute-start(bf16[1024,256]{1,0:T(8,128)(2,1)S(1)} %slice_select_fusion), channel_id=1, source_target_pairs={{0,4},{1,5},{8,12},{9,13},{16,20},{17,21},{24,28},{25,29}} | collective-permute-start | bytes 1572872 | tf_op jit(solution)/shard_map/ppermute | solution.py:350
  118.5 35.4 %collective-permute-start.21 = (bf16[1024,256]{1,0:T(8,128)(2,1)S(1)}, bf16[1024,256]{1,0:T(8,128)(2,1)}, u32[]{:S(2)}, u32[]{:S(2)}) collective-permute-start(bf16[1024,256]{1,0:T(8,128)(2,1)S(1)} %slice_select_fusion), channel_id=1, source_target_pairs={{0,2},{1,3},{8,10},{9,11},{16,18},{17,19},{24,26},{25,27}} | collective-permute-start | bytes 1572872 | tf_op jit(solution)/shard_map/ppermute | solution.py:350
  129.9 46.0 %collective-permute-start.14 = (bf16[2,2,256,256]{3,2,1,0:T(8,128)(2,1)}, bf16[2,2,256,256]{3,2,1,0:T(8,128)(2,1)}, u32[]{:S(2)}, u32[]{:S(2)}) collective-permute-start(bf16[2,2,256,256]{3,2,1,0:T(8,128)(2,1)} %pad_maximum_fusion.6), channel_id=1, source_target_pairs={{0,8},{8,0},{16,24},{24,16},{1,9},{9,1},{17,25},{25,17},{2,10},{10... | collective-permute-start | bytes 1572872 | tf_op jit(solution)/shard_map/ppermute | solution.py:373
  169.3 32.8 %collective-permute-start.24 = (bf16[1024,256]{1,0:T(8,128)(2,1)}, bf16[1024,256]{1,0:T(8,128)(2,1)}, u32[]{:S(2)}, u32[]{:S(2)}) collective-permute-start(bf16[1024,256]{1,0:T(8,128)(2,1)} %add_select_fusion), channel_id=1, source_target_pairs={{0,1},{1,0},{2,3},{3,2},{4,5},{5,4},{6,7},{7,6},{8,9},{9,8},{10,11... | collective-permute-start | bytes 1572872 | tf_op jit(solution)/shard_map/ppermute | solution.py:419
  175.9 23.3 %collective-permute-start.16 = (bf16[2,256,256]{2,1,0:T(8,128)(2,1)}, bf16[2,256,256]{2,1,0:T(8,128)(2,1)}, u32[]{:S(2)}, u32[]{:S(2)}) collective-permute-start(bf16[2,256,256]{2,1,0:T(8,128)(2,1)} %get-tuple-element.55), channel_id=1, source_target_pairs={{0,4},{1,5},{2,6},{3,7},{4,0},{5,1},{6,2},{7,3},{8,12},{9,13},{10,... | collective-permute-start | bytes 786440 | tf_op jit(solution)/shard_map/ppermute | solution.py:346
  212.0 42.7 %all-to-all-start.3 = ((bf16[8,256,256]{2,1,0:T(8,128)(2,1)}), bf16[8,256,256]{2,1,0:T(8,128)(2,1)}, u32[]{:S(2)}, u32[]{:S(2)}) async-start(bf16[8,256,256]{2,1,0:T(8,128)(2,1)} %bitcast.35), calls=%async_computation.3 | async-start | bytes 2097152 | tf_op jit(solution)/shard_map/all_to_all | solution.py:430
  230.2 42.4 %collective-permute-start.33 = (bf16[2,256,512]{2,1,0:T(8,128)(2,1)S(1)}, bf16[2,256,512]{2,1,0:T(8,128)(2,1)S(1)}, u32[]{:S(2)}, u32[]{:S(2)}) collective-permute-start(bf16[2,256,512]{2,1,0:T(8,128)(2,1)S(1)} %collective-permute-done.31), channel_id=1, source_target_pairs={{0,1},{1,0},{2,3},{3,2},{4,5},{5,4},{6,7},{7,6},{8,9},{9,8},{10,11... | collective-permute-start | bytes 1572872 | tf_op jit(solution)/shard_map/ppermute | solution.py:447
  245.7 26.9 %collective-permute-start.34 = (bf16[2,256,512]{2,1,0:T(8,128)(2,1)S(1)}, bf16[2,256,512]{2,1,0:T(8,128)(2,1)S(1)}, u32[]{:S(2)}, u32[]{:S(2)}) collective-permute-start(bf16[2,256,512]{2,1,0:T(8,128)(2,1)S(1)} %collective-permute-done.32), channel_id=1, source_target_pairs={{0,1},{1,0},{2,3},{3,2},{4,5},{5,4},{6,7},{7,6},{8,9},{9,8},{10,11... | collective-permute-start | bytes 1572872 | tf_op jit(solution)/shard_map/ppermute | solution.py:447
  257.1 26.6 %collective-permute-start.29 = (bf16[256,1024]{1,0:T(8,128)(2,1)S(1)}, bf16[256,1024]{1,0:T(8,128)(2,1)S(1)}, u32[]{:S(2)}, u32[]{:S(2)}) collective-permute-start(bf16[256,1024]{1,0:T(8,128)(2,1)S(1)} %pad_maximum_fusion.8), channel_id=1, source_target_pairs={{0,16},{1,17},{2,18},{3,19},{4,20},{5,21},{6,22},{7,23}} | collective-permute-start | bytes 1572872 | tf_op jit(solution)/shard_map/ppermute | solution.py:454
  279.8 22.9 %collective-permute-start.28 = (bf16[2,256,256]{2,1,0:T(8,128)(2,1)S(1)}, bf16[2,256,256]{2,1,0:T(8,128)(2,1)S(1)}, u32[]{:S(2)}, u32[]{:S(2)}) collective-permute-start(bf16[2,256,256]{2,1,0:T(8,128)(2,1)S(1)} %pad_maximum_fusion.12), channel_id=1, source_target_pairs={{6,0},{14,8},{22,16},{30,24}} | collective-permute-start | bytes 786440 | tf_op jit(solution)/shard_map/ppermute | solution.py:451
  (33 other events, 364.2 us)

commit v3 on v2

--- a/solution.py
+++ b/solution.py
@@ -19,6 +19,9 @@
 
 def params(*semantics):
     return pltpu.CompilerParams(dimension_semantics=semantics, vmem_limit_bytes=vmem_cap)
+
+
+light = pl.CostEstimate(flops=1, transcendentals=0, bytes_accessed=1)
 
 
 def dot(a, b, dims=((1,), (0,)), precision=None):
@@ -54,12 +57,88 @@
         ],
         out_specs=pl.BlockSpec((ds * xs, zs + 1, tile, bs), lambda i: (0, 0, i, 0)),
         out_shape=jax.ShapeDtypeStruct((ds * xs, zs + 1, count, bs), bf16),
+        cost_estimate=light,
         compiler_params=params("arbitrary"),
         name="pack_tokens",
     )(limit, tokens)
 
 
-def stats_body(x_ref, l_ref, f_ref, b_ref, o_ref, t_ref, lead_image):
+def moments_body(ids_ref, x_ref, l_ref, o_ref):
+    groups, _, count, bs = x_ref.shape
+    cols = x_ref[:, 0].reshape(groups * count, bs)
+    lead = l_ref[:, 0].reshape(groups * count, bs)
+    o_ref[0, 0] = dot(cols, cols, tn).astype(bf16)
+    o_ref[0, 1] = dot(lead, cols, tn).astype(bf16)
+    o_ref[0, 2] = dot(lead, lead, tn).astype(bf16)
+
+
+def raw_moments(ids, owned):
+    groups, slots, count, bs = owned.shape
+    zs = slots - 1
+    return pl.pallas_call(
+        moments_body,
+        grid_spec=pltpu.PrefetchScalarGridSpec(
+            num_scalar_prefetch=1,
+            grid=(zs,),
+            in_specs=[
+                pl.BlockSpec((groups, 1, count, bs), lambda k, ids: (0, ids[0] ^ k, 0, 0)),
+                pl.BlockSpec((groups, 1, count, bs), lambda k, ids: (0, zs, 0, 0)),
+            ],
+            out_specs=pl.BlockSpec((1, 3, bs, bs), lambda k, ids: (k, 0, 0, 0)),
+        ),
+        out_shape=jax.ShapeDtypeStruct((zs, 3, bs, bs), bf16),
+        cost_estimate=light,
+        compiler_params=params("arbitrary"),
+        name="raw_moments",
+    )(ids, owned, owned)
+
+
+def image_stats_body(count, ids_ref, sc_ref, *refs):
+    parts = refs[:count]
+    fac_ref, h_ref, tr_ref = refs[count:]
+    bs = fac_ref.shape[1]
+    keep = jnp.where(ids_ref[2] + ids_ref[1] > 0, 1.0, 0.0)
+    total = parts[0][...].astype(f32)
+    for part in parts[1:]:
+        total = total + part[...].astype(f32)
+    fac = fac_ref[0]
+    bn = fac[:, :bs].astype(bf16).astype(f32)
+    pn = (fac[:, bs:] * keep).astype(bf16).astype(f32)
+    mm = functools.partial(dot, precision=highest)
+    t1 = mm(total[0], bn) + mm(total[1], pn, tn)
+    t0 = mm(total[1], bn) + mm(total[2], pn)
+    own = (mm(bn, t1, tn) + mm(pn, t0, tn)) * sc_ref[0]
+    h_ref[0] = own.astype(bf16)
+    h_ref[1] = (t0 * sc_ref[0]).astype(bf16)
+    row = lax.broadcasted_iota(jnp.int32, (bs, bs), 0)
+    col = lax.broadcasted_iota(jnp.int32, (bs, bs), 1)
+    tr_ref[...] = jnp.zeros_like(tr_ref) + jnp.sum(jnp.where(row == col, own, 0.0))
+
+
+def image_stats(ids, scalars, parts, factor):
+    _, bs, wide = factor.shape
+    whole = lambda shape: pl.BlockSpec(shape, lambda i, ids: (0,) * len(shape))
+    return pl.pallas_call(
+        functools.partial(image_stats_body, len(parts)),
+        grid_spec=pltpu.PrefetchScalarGridSpec(
+            num_scalar_prefetch=1,
+            grid=(1,),
+            in_specs=[pl.BlockSpec(memory_space=pltpu.SMEM)]
+            + [whole((3, bs, bs)) for _ in parts]
+            + [pl.BlockSpec((1, bs, wide), lambda i, ids: (ids[1], 0, 0))],
+            out_specs=[whole((2, bs, bs)), whole((8, 128))],
+        ),
+        out_shape=[
+            jax.ShapeDtypeStruct((2, bs, bs), bf16),
+            jax.ShapeDtypeStruct((8, 128), f32),
+        ],
+        cost_estimate=light,
+        compiler_params=params("arbitrary"),
+        name="image_stats",
+    )(ids, scalars, *parts, factor)
+
+
+def stats_body(x_ref, l_ref, f_ref, o_ref, t_ref):
     groups, _, count, bs = x_ref.shape
     k = pl.program_id(0)
     cols = x_ref[:, 0].reshape(groups * count, bs)
@@ -67,17 +146,16 @@
 
     @pl.when(k == 0)
     def _():
-        lead_image[...] = dot(lead, b_ref[...]).astype(bf16)
         t_ref[...] = jnp.zeros_like(t_ref)
 
     image = (dot(cols, f_ref[0, :, :bs]) + dot(lead, f_ref[0, :, bs:])).astype(bf16)
     o_ref[0, 0] = dot(image, image, tn).astype(bf16)
-    o_ref[0, 1] = dot(lead_image[...], image, tn).astype(bf16)
+    o_ref[0, 1] = dot(lead, image, tn).astype(bf16)
     wide = image.astype(f32)
     t_ref[...] = t_ref[...] + jnp.sum(wide * wide)
 
 
-def stats(ids, owned, blocks, lead):
+def stats(ids, owned, blocks):
     groups, slots, count, bs = owned.shape
     zs = slots - 1
 
@@ -93,21 +171,20 @@
                 pl.BlockSpec((groups, 1, count, bs), lambda k, ids: (0, ids[0] ^ k, 0, 0)),
                 pl.BlockSpec((groups, 1, count, bs), lambda k, ids: (0, zs, 0, 0)),
                 pl.BlockSpec((1, bs, 2 * bs), lambda k, ids: (k, 0, 0)),
-                pl.BlockSpec((bs, bs), lambda k, ids: (0, 0)),
             ],
             out_specs=[
                 pl.BlockSpec((1, 2, bs, bs), lambda k, ids: (k, 0, 0, 0)),
                 pl.BlockSpec((8, 128), lambda k, ids: (0, 0)),
             ],
-            scratch_shapes=[pltpu.VMEM((groups * count, bs), bf16)],
         ),
         out_shape=[
             jax.ShapeDtypeStruct((zs, 2, bs, bs), bf16),
             jax.ShapeDtypeStruct((8, 128), f32),
         ],
+        cost_estimate=light,
         compiler_params=params("arbitrary"),
         name="plane_stats",
-    )(ids, owned, owned, blocks, lead)
+    )(ids, owned, owned, blocks)
 
 
 def advance_block(width, own, cross, fac, mom, b0, other_h, other_g, keep):
@@ -142,7 +219,7 @@
     md, ms, new_d, new_s = advance_block(
         width,
         h_ref[0, 0].astype(f32),
-        h_ref[0, 1].astype(f32),
+        dot(lead_ref[...], h_ref[0, 1], tn),
         fac_ref[0],
         mom_ref[0],
         lead_ref[...],
@@ -180,6 +257,7 @@
             jax.ShapeDtypeStruct(factor.shape, f32),
             jax.ShapeDtypeStruct(factor.shape, bf16),
         ],
+        cost_estimate=light,
         compiler_params=params("arbitrary"),
         name="advance_all",
     )(ids, scalars, stats, factor, moment, lead)
@@ -225,6 +303,7 @@
             jax.ShapeDtypeStruct((rows, wide), bf16),
             jax.ShapeDtypeStruct((rows, bs), bf16),
         ],
+        cost_estimate=light,
         compiler_params=params("arbitrary"),
         name="column_products",
     )(ids, grad, lead, kb)
@@ -235,16 +314,19 @@
     return ((ids[3] & 1) ^ (k // per)) * per + k % per
 
 
-def rows_body(ids_ref, s_ref, g_ref, l_ref, c_ref, p_ref, u_ref, acc_ref):
+def gathered_at(ids, k):
+    i = row_of(ids, k)
+    return (i % ids[4]) * 2 + i // ids[4]
+
+
+def rows_body(ids_ref, s_ref, l_ref, c_ref, p_ref, u_ref, acc_ref):
     k = pl.program_id(0)
-    bs = l_ref.shape[0]
+    bs = c_ref.shape[1]
     cd = c_ref[0, :, :bs]
     cs = c_ref[0, :, bs:]
-    lead = jnp.where(ids_ref[3] == 0, g_ref[...], s_ref[:, :bs])
-    second = jnp.concatenate([lead, s_ref[:, bs:]], axis=1)
-    third = (dot(cd, second, tn) + dot(cs, l_ref[...], tn)).astype(bf16)
+    third = (dot(cd, s_ref[:, bs:], tn) + dot(cs, l_ref[...], tn)).astype(bf16)
     fourth = dot(cd, third)
-    p_ref[...] = fourth.astype(bf16)
+    p_ref[:, bs:] = fourth.astype(bf16)
     is_first = (ids_ref[1] == 0) & (row_of(ids_ref, k) == 0)
     term = dot(cs, third) + fourth * jnp.where(is_first, 1.0, 0.0)
 
@@ -261,11 +343,12 @@
         u_ref[...] = acc_ref[...].astype(bf16)
 
 
-def rows(ids, second, gathered, lead, cb):
+def rows(ids, second, lead, cb):
     count, wide = second.shape
     blocks, bs, _ = cb.shape
+    rest = wide - bs
     spec = pl.BlockSpec((bs, wide), lambda k, ids: (row_of(ids, k), 0))
-    whole = pl.BlockSpec((bs, wide), lambda k, ids: (0, 0))
+    whole = pl.BlockSpec((bs, rest), lambda k, ids: (0, 0))
     return pl.pallas_call(
         rows_body,
         grid_spec=pltpu.PrefetchScalarGridSpec(
@@ -273,50 +356,102 @@
             grid=(blocks,),
             in_specs=[
                 spec,
-                pl.BlockSpec((bs, bs), lambda k, ids: (row_of(ids, k), 0)),
                 whole,
                 pl.BlockSpec((1, bs, 2 * bs), lambda k, ids: (k, 0, 0)),
             ],
             out_specs=[spec, whole],
-            scratch_shapes=[pltpu.VMEM((bs, wide), f32)],
+            scratch_shapes=[pltpu.VMEM((bs, rest), f32)],
         ),
         out_shape=[
             jax.ShapeDtypeStruct((count, wide), bf16),
-            jax.ShapeDtypeStruct((bs, wide), bf16),
+            jax.ShapeDtypeStruct((bs, rest), bf16),
         ],
+        cost_estimate=light,
         compiler_params=params("arbitrary"),
         name="row_products",
-    )(ids, second, gathered, lead, cb)
-
-
-def put_top_body(ids_ref, p_ref, low_ref, high_ref, o_ref):
-    half = low_ref.shape[0]
+    )(ids, second, lead, cb)
+
+
+def lead_rows_body(ids_ref, s_ref, g_ref, l_ref, c_ref, _, p_ref, u_ref):
+    blocks, bs, _ = c_ref.shape
+    total = jnp.zeros((bs, bs), f32)
+    for k in range(blocks):
+        i = row_of(ids_ref, k)
+        own = s_ref[pl.ds(pl.multiple_of(i * bs, bs), bs), :]
+        whole = g_ref[pl.ds(pl.multiple_of(gathered_at(ids_ref, k) * bs, bs), bs), :]
+        second = jnp.where(ids_ref[3] == 0, whole, own)
+        cd = c_ref[k, :, :bs]
+        cs = c_ref[k, :, bs:]
+        third = (dot(cd, second, tn) + dot(cs, l_ref[...], tn)).astype(bf16)
+        fourth = dot(cd, third)
+        p_ref[pl.ds(pl.multiple_of(i * bs, bs), bs), :] = fourth.astype(bf16)
+        is_first = (ids_ref[1] == 0) & (i == 0)
+        total = total + dot(cs, third) + fourth * jnp.where(is_first, 1.0, 0.0)
+    u_ref[...] = total.astype(bf16)
+
+
+def lead_rows_products(ids, second, gathered, lead, cb, tile):
+    count, _ = second.shape
+    blocks, bs, _ = cb.shape
+    column = pl.BlockSpec((count, bs), lambda i, ids: (0, 0))
+    square = pl.BlockSpec((bs, bs), lambda i, ids: (0, 0))
+    return pl.pallas_call(
+        lead_rows_body,
+        grid_spec=pltpu.PrefetchScalarGridSpec(
+            num_scalar_prefetch=1,
+            grid=(1,),
+            in_specs=[
+                column,
+                column,
+                square,
+                pl.BlockSpec(cb.shape, lambda i, ids: (0, 0, 0)),
+                pl.BlockSpec(memory_space=pl.ANY),
+            ],
+            out_specs=[column, square],
+        ),
+        out_shape=[
+            jax.ShapeDtypeStruct(tile.shape, bf16),
+            jax.ShapeDtypeStruct((bs, bs), bf16),
+        ],
+        input_output_aliases={5: 0},
+        cost_estimate=light,
+        compiler_params=params("arbitrary"),
+        name="lead_row_products",
+    )(ids, second, gathered, lead, cb, tile)
+
+
+def put_top_body(ids_ref, p_ref, lead_ref, rest_ref, o_ref):
+    bs = lead_ref.shape[1]
     first = ids_ref[1] == 0
 
     @pl.when(first)
     def _():
-        o_ref[:half] = low_ref[...]
-        o_ref[half:] = high_ref[...]
+        o_ref[:, :bs] = lead_ref[...]
+        o_ref[:, bs:] = rest_ref[...]
 
     @pl.when(jnp.logical_not(first))
     def _():
         o_ref[...] = p_ref[...]
 
 
-def put_top(ids, tile, low, high):
-    half, wide = low.shape
-    top = pl.BlockSpec((2 * half, wide), lambda i, ids: (0, 0))
-    part = pl.BlockSpec((half, wide), lambda i, ids: (0, 0))
+def put_top(ids, tile, lead, rest):
+    bs = lead.shape[0]
+    spec = lambda width: pl.BlockSpec((bs, width), lambda i, ids: (0, 0))
+    top = spec(tile.shape[1])
     return pl.pallas_call(
         put_top_body,
         grid_spec=pltpu.PrefetchScalarGridSpec(
-            num_scalar_prefetch=1, grid=(1,), in_specs=[top, part, part], out_specs=top
+            num_scalar_prefetch=1,
+            grid=(1,),
+            in_specs=[top, spec(bs), spec(rest.shape[1])],
+            out_specs=top,
         ),
         out_shape=jax.ShapeDtypeStruct(tile.shape, tile.dtype),
         input_output_aliases={1: 0},
+        cost_estimate=light,
         compiler_params=params("arbitrary"),
         name="put_top",
-    )(ids, tile, low, high)
+    )(ids, tile, lead, rest)
 
 
 def after(value, *earlier):
@@ -339,21 +474,16 @@
     ids = jnp.stack([z, d, s * ds, s, jnp.int32(ds)]).astype(jnp.int32)
     token_total = jnp.sum(token_counts).astype(f32)
     valid = jnp.sum(jnp.where(lax.iota(jnp.int32, ds) == d, token_counts, 0))
+    stat_scalars = (1.0 / token_total).reshape(1)
     limit = (valid - s * tok_dev).reshape(1).astype(jnp.int32)
 
     def along_z(value, k):
         pairs = [(zz * xs + xx, (zz ^ k) * xs + xx) for zz in range(zs) for xx in range(xs)]
         return lax.ppermute(value, "fsdp", pairs)
 
-    def from_plane_0(value):
-        got = [
-            lax.ppermute(value, "fsdp", [(xx, zz * xs + xx) for xx in range(xs)])
-            for zz in range(1, zs)
-        ]
-        out = got[0]
-        for g in got[1:]:
-            out = out + g
-        return jnp.where(z == 0, value, out)
+    def from_group_0(value):
+        value = jnp.where(d == 0, value, lax.ppermute(value, "dp", [(0, 2)]))
+        return jnp.where(d % 2 == 0, value, lax.ppermute(value, "dp", [(0, 1), (2, 3)]))
 
     def block_along_z(factor, *earlier):
         own = lax.dynamic_index_in_dim(factor, d, 0, keepdims=False)
@@ -362,11 +492,14 @@
         own = after(own, *earlier)
         return jnp.stack([own] + [along_z(own, k) for k in range(1, zs)])
 
-    def sum_along_z(partial):
-        total = partial[0].astype(f32)
-        for k in range(1, zs):
-            total = total + along_z(partial[k], k).astype(f32)
+    def mean_of(parts):
+        total = parts[0].astype(f32)
+        for part in parts[1:]:
+            total = total + part.astype(f32)
         return (total / token_total).astype(bf16)
+
+    def each_along_z(partial):
+        return [partial[0]] + [along_z(partial[k], k) for k in range(1, zs)]
 
     def over_dp(value):
         pair = jnp.stack([value, lax.ppermute(value, "dp", [(i, i ^ 2) for i in range(ds)])])
@@ -382,55 +515,72 @@
     def exchange(packed):
         return lax.all_to_all(packed, both, 0, 0, tiled=True, axis_index_groups=plane)
 
-    leads = jnp.stack([k_factor[0, :, :bs], c_factor[0, :, :bs]]).astype(bf16)
-    leads = jnp.where(s == 0, leads, lax.ppermute(leads, "fsdp", [(0, 1)]))
-    leads = from_plane_0(leads)
-    lead_k, lead_c = leads[0], leads[1]
-    grad_half = grad_weight.shape[0] // xs
-    grad_low = grad_weight[:grad_half, :bs]
-    grad_high = lax.ppermute(grad_weight[grad_half:, :bs], "fsdp", [(0, 1)])
-    grad_mine = jnp.where(s == 0, grad_low, grad_high)
+    load = jnp.concatenate(
+        [k_factor[0, :, :bs].astype(bf16), c_factor[0, :, :bs].astype(bf16), grad_weight[:, :bs]]
+    )
+    load_half = load.shape[0] // xs
+    load_x = lax.ppermute(load[load_half:], "fsdp", [(0, 1)])
+
+    def down_z(value, stride):
+        pairs = [
+            (zz * xs + xx, (zz + stride) * xs + xx)
+            for zz in range(0, zs, 2 * stride)
+            for xx in range(xs)
+        ]
+        return lax.ppermute(value, "fsdp", pairs)
 
     owned_k = exchange(pack(limit, acts, zs, xs, ds, bs))
-    blocks_k = block_along_z(k_factor)
-    packed_c = after(pack(limit, out_grads, zs, xs, ds, bs), owned_k)
-    owned_c = exchange(packed_c)
-    partial_k, square_k = stats(ids, owned_k, blocks_k, lead_k)
-    blocks_c = block_along_z(c_factor, owned_k)
-    stat_k = sum_along_z(partial_k)
-    grad_mine = from_plane_0(after(grad_mine, partial_k))
-    all_k = over_dp(stat_k)
+    blocks_c = block_along_z(c_factor)
+    packed_c = pack(limit, out_grads, zs, xs, ds, bs)
     gram_k = gram_part(k_factor)
     gram_c = gram_part(c_factor)
-
-    partial_c, square_c = stats(ids, owned_c, blocks_c, lead_c)
+    packed_c, owned_k, blocks_c, gram_k, gram_c = lax.optimization_barrier(
+        (packed_c, owned_k, blocks_c, gram_k, gram_c)
+    )
+    owned_c = exchange(packed_c)
+
+    raw_k = raw_moments(ids, after(owned_k, load_x))
+    sent_k = each_along_z(raw_k)
+    stride = zs // 2
+    mine = jnp.where(s == 0, load[:load_half], after(load_x, raw_k))
+    while stride > 1:
+        got = after(down_z(mine, stride), *sent_k)
+        mine = jnp.where(z % (2 * stride) == 0, mine, got)
+        stride //= 2
+    last_z = down_z(mine, 1)
+
+    stat_k, trace_k = image_stats(ids, stat_scalars, sent_k, k_factor)
+    partial_c, square_c = stats(ids, after(owned_c, trace_k), blocks_c)
     rows8 = lax.broadcasted_iota(jnp.int32, (8, 128), 0)
     sums = jnp.where(
         rows8 == 0,
-        square_k,
+        trace_k,
         jnp.where(rows8 == 1, square_c, jnp.where(rows8 == 2, gram_k, gram_c)),
     )
+    sent_c = each_along_z(partial_c)
     sums = jnp.broadcast_to(sums[None], (ds * shards, 8, 128))
     totals = jnp.sum(lax.all_to_all(sums, both, 0, 0, tiled=True), axis=0)[:, 0]
     for_k = jnp.stack([totals[1] / token_total, totals[3]])
-    for_c = jnp.stack([totals[0] / token_total, totals[2]])
-    stat_c = sum_along_z(partial_c)
-
-    grad_other = lax.ppermute(after(grad_mine, owned_c), "fsdp", flip_x)
-    grad_lead = jnp.concatenate(
-        [jnp.where(x == 0, grad_mine, grad_other), jnp.where(x == 0, grad_other, grad_mine)], axis=0
-    )
+    for_c = jnp.stack([totals[0], totals[2]])
+    all_k = over_dp(after(stat_k, partial_c))
+    mine = jnp.where(z % 2 == 0, mine, after(last_z, partial_c))
+    other = lax.ppermute(mine, "fsdp", flip_x)
+    load = jnp.concatenate([jnp.where(x == 0, mine, other), jnp.where(x == 0, other, mine)])
+    lead_k, lead_c, grad_lead = load[:bs], load[bs : 2 * bs], load[2 * bs :]
+
     scale_width = float(width)
     k_factor_new, k_moment_new, kb = advance_all(
         scale_width, ids, for_k, all_k, k_factor, k_moment, lead_k
     )
     second, term = columns(ids, grad_weight, grad_lead, kb)
     count = grad_weight.shape[0]
-    by_shard = term.reshape(shards, count // shards, bs)
-    got = lax.all_to_all(by_shard, "fsdp", 0, 0, tiled=True)
-    block_sum = jnp.sum(got.astype(f32), axis=0).astype(bf16)
-
+    kept = lax.dynamic_slice_in_dim(term, x * (count // xs), count // xs, 0)
+    passed = lax.dynamic_slice_in_dim(term, (1 - x) * (count // xs), count // xs, 0)
+    passed = lax.ppermute(passed, "fsdp", flip_x)
+
+    stat_c = mean_of([after(part, term) for part in sent_c])
     all_c = over_dp(stat_c)
+
     c_factor_new, c_moment_new, cb = advance_all(
         scale_width, ids, for_c, all_c, c_factor, c_moment, lead_c
     )
@@ -445,27 +595,32 @@
         ]
         halves.append(lax.ppermute(cb[h * (ds // 2) : (h + 1) * (ds // 2)], both, pairs))
     others = [lax.ppermute(h, "fsdp", flip_x) for h in halves]
+
+    halved = (kept.astype(f32) + passed.astype(f32)).astype(bf16).reshape(zs, bs, bs)
+    turned = [lax.dynamic_index_in_dim(halved, z ^ k, 0, keepdims=False) for k in range(zs)]
+    got = [after(g, cb) for g in each_along_z(turned)]
+
     c_rows = jnp.concatenate(halves + others, axis=0)
 
+    top_rest = from_group_0(second[:bs, bs:])
+
+    block_sum = got[0].astype(f32)
+    for g in got[1:]:
+        block_sum = block_sum + g.astype(f32)
+    block_sum = block_sum.astype(bf16)
     pair = jnp.stack([block_sum, lax.ppermute(block_sum, "fsdp", [(2 * k + 1, 2 * k) for k in range(zs)])])
     gathered = [pair] + [lax.ppermute(pair, "fsdp", [(xs * k, 0)]) for k in range(1, zs)]
     gathered = jnp.concatenate(gathered, axis=0).reshape(count, bs)
-    top = jnp.concatenate([jnp.where(s == 0, block_sum, second[:bs, :bs]), second[:bs, bs:]], axis=1)
-    over_y = lax.ppermute(top, "dp", [(0, 2)])
-    top = jnp.where(d == 0, top, over_y)
-    over_core = lax.ppermute(top, "dp", [(0, 1), (2, 3)])
-    lead_rows = jnp.where(d % 2 == 0, top, over_core)
-
-    precond, up = rows(ids, second, gathered, lead_rows, c_rows)
-    half = bs // 2
-    core = d % 2
-    mine = jnp.where(core == 0, up[:half], up[half:])
-    theirs = jnp.where(core == 0, up[half:], up[:half])
-    mine = mine.astype(f32) + lax.ppermute(theirs, "dp", [(i, i ^ 1) for i in range(ds)])
-    low = mine.astype(bf16)
-    mine = (mine + lax.ppermute(low, "dp", [(2, 0), (3, 1)])).astype(bf16)
-    high = lax.ppermute(mine, "dp", [(1, 0)])
-    precond = put_top(ids, precond, mine, high)
+    top_lead = from_group_0(jnp.where(s == 0, block_sum, second[:bs, :bs]))
+    def sum_to_group_0(value):
+        total = value.astype(f32) + lax.ppermute(value, "dp", [(2, 0), (3, 1)]).astype(f32)
+        other = lax.ppermute(total.astype(bf16), "dp", [(1, 0)])
+        return (total + other.astype(f32)).astype(bf16)
+
+    precond, up_rest = rows(ids, second, top_rest, c_rows)
+    up_rest = sum_to_group_0(up_rest)
+    precond, up_lead = lead_rows_products(ids, second, gathered, top_lead, c_rows, precond)
+    precond = put_top(ids, precond, sum_to_group_0(up_lead), up_rest)
     return (k_factor_new, c_factor_new, k_moment_new, c_moment_new, precond)
 
 

time: 335 us -> 286 us (0.85)
  the two profiles are of different devices: /device:TPU:0 before, /device:TPU:17 now
where the time goes in v3:
time: 286 us; the launch traced here: 284 us
  waiting for transfers between devices  95.1 us (33%)
  starting transfers between devices  91.7 us (32%)
  Pallas kernels  51.5 us (18%)
  local copies, waits for them, and re-layouts  21.6 us (8%)
  other arithmetic  18.5 us (6%)
  between operations  5.75 us (2%)
    ppermute x12, waiting for transfers between devices, along_z(): return lax.ppermute(value, 'fsdp', pairs)  36.3 us
    ppermute x12, starting transfers between devices, along_z(): return lax.ppermute(value, 'fsdp', pairs)  24.2 us
    ppermute x2, waiting for transfers between devices, planned(): lax.ppermute(cb[h * (ds // 2):(h + 1) * (ds // 2)], both, pairs)  20 us
    ppermute x2, waiting for transfers between devices, planned(): others = [lax.ppermute(h, 'fsdp', flip_x) for h in halves]  18 us
    ppermute x2, starting transfers between devices, down_z(): return lax.ppermute(value, 'fsdp', pairs)  13.7 us
    ppermute x2, starting transfers between devices, planned(): lax.ppermute(cb[h * (ds // 2):(h + 1) * (ds // 2)], both, pairs)  11.5 us
    pallas_call x2, Pallas kernels, advance_all(): pl.pallas_call(functools.partial(advance_body, width), grid_spec=pltpu.Pr...  11.2 us
    pallas_call x1, Pallas kernels, rows(): pl.pallas_call(rows_body, grid_spec=pltpu.PrefetchScalarGridSpec(num_scal...  10.7 us
  transfers between devices with their start and end apart: 40, of which 14 were waited for; matrix products, arithmetic and copies ran while one was open for 9% of the time, Pallas kernels for 16%

profile of v3, /device:TPU:17, one launch (start us, length us, event | category | flops | bytes accessed | tf_op | source)
XLA Modules:
  0.0 284.2 jit_solution(6761234839652170824)
XLA Ops:
  6.2 4.4 %all-to-all-start = ((bf16[8,5,128,256]{3,2,1,0:T(8,128)(2,1)}), bf16[8,5,128,256]{3,2,1,0:T(8,128)(2,1)S(1)}, u32[]{:S(2)}, u32[]{:S(2)}) async-start(bf16[8,5,128,256]{3,2,1,0:T(8,128)(2,1)} %copy-done.5), calls=%async_computation | async-start | bytes 5242880 | tf_op jit(solution)/shard_map/all_to_all | solution.py:516
  12.0 3.2 %collective-permute-start.1 = (bf16[256,512]{1,0:T(8,128)(2,1)S(1)}, bf16[256,512]{1,0:T(8,128)(2,1)}, u32[]{:S(2)}, u32[]{:S(2)}) collective-permute-start(bf16[256,512]{1,0:T(8,128)(2,1)S(1)} %pad_maximum_fusion.8), channel_id=1, source_target_pairs={{0,4},{1,5},{2,6},{3,7},{4,0},{5,1},{6,2},{7,3},{8,12},{9,13},{10,... | collective-permute-start | bytes 786440 | tf_op jit(solution)/shard_map/ppermute | solution.py:482
  31.1 3.5 %collective-permute-done.1 = bf16[256,512]{1,0:T(8,128)(2,1)} collective-permute-done((bf16[256,512]{1,0:T(8,128)(2,1)S(1)}, bf16[256,512]{1,0:T(8,128)(2,1)}, u32[]{:S(2)}, u32[]{:S(2)}) %collective-permute-start.1) | collective-permute-done | bytes 262176 | tf_op jit(solution)/shard_map/ppermute | solution.py:482
  36.7 4.8 %all-to-all-done.x_ref.l_ref = bf16[8,5,128,256]{3,2,1,0:T(8,128)(2,1)S(1)} async-done(((bf16[8,5,128,256]{3,2,1,0:T(8,128)(2,1)}), bf16[8,5,128,256]{3,2,1,0:T(8,128)(2,1)S(1)}, u32[]{:S(2)}, u32[]{:S(2)}) %all-to-all-start) | async-done | bytes 2621472 | tf_op jit(solution)/shard_map/all_to_all | solution.py:516
  41.5 3.3 %raw_moments.1 = bf16[4,3,256,256]{3,2,1,0:T(8,128)(2,1)S(1)} custom-call(s32[5]{0:T(128)S(1)} %stack.70.ids_ref, bf16[8,5,128,256]{3,2,1,0:T(8,128)(2,1)S(1)} %all-to-all-done.x_ref.l_ref, bf16[8,5,128,256]{3,2,1,0:T(8,128)(2,1)S(1)} %all-to-all-done.x_ref.l_ref), custom_call_target="tpu_custom_call" | custom-call | flops 1 | bytes 1 | tf_op jit(solution)/shard_map/raw_moments/pallas_call | solution.py:78
  46.0 4.3 %all-to-all-start.1 = ((bf16[8,5,128,256]{3,2,1,0:T(8,128)(2,1)}), bf16[8,5,128,256]{3,2,1,0:T(8,128)(2,1)S(1)}, u32[]{:S(2)}, u32[]{:S(2)}) async-start(bf16[8,5,128,256]{3,2,1,0:T(8,128)(2,1)} %copy-done.4), calls=%async_computation.1 | async-start | bytes 5242880 | tf_op jit(solution)/shard_map/all_to_all | solution.py:516
  55.4 13.2 %collective-permute-start.5 = (bf16[3,256,256]{2,1,0:T(8,128)(2,1)}, bf16[3,256,256]{2,1,0:T(8,128)(2,1)}, u32[]{:S(2)}, u32[]{:S(2)}) collective-permute-start(bf16[3,256,256]{2,1,0:T(8,128)(2,1)} %get-tuple-element.86), channel_id=1, source_target_pairs={{0,4},{1,5},{2,6},{3,7},{4,0},{5,1},{6,2},{7,3},{8,12},{9,13},{10,... | collective-permute-start | bytes 1179656 | tf_op jit(solution)/shard_map/ppermute | solution.py:482
  69.7 29.2 %collective-permute-done.5.refs_2_ = bf16[3,256,256]{2,1,0:T(8,128)(2,1)} collective-permute-done((bf16[3,256,256]{2,1,0:T(8,128)(2,1)}, bf16[3,256,256]{2,1,0:T(8,128)(2,1)}, u32[]{:S(2)}, u32[]{:S(2)}) %collective-permute-start.5) | collective-permute-done | bytes 393248 | tf_op jit(solution)/shard_map/ppermute | solution.py:482
  101.0 12.4 %collective-permute-start.10 = (bf16[1280,256]{1,0:T(8,128)(2,1)}, bf16[1280,256]{1,0:T(8,128)(2,1)}, u32[]{:S(2)}, u32[]{:S(2)}) collective-permute-start(bf16[1280,256]{1,0:T(8,128)(2,1)} %broadcast_select_fusion), channel_id=1, source_target_pairs={{0,2},{1,3},{4,6},{5,7},{8,10},{9,11},{12,14},{13,15},{16,18},{17,... | collective-permute-start | bytes 1966088 | tf_op jit(solution)/shard_map/ppermute | solution.py:530
  116.7 4.3 %image_stats.1 = (bf16[2,256,256]{2,1,0:T(8,128)(2,1)S(1)}, f32[8,128]{1,0:T(8,128)S(1)}) custom-call(s32[5]{0:T(128)S(1)} %stack.70.ids_ref, f32[1]{0:T(128)} %bitcast.4.sc_ref, bf16[3,256,256]{2,1,0:T(8,128)(2,1)S(1)} %get-tuple-element.88.refs_0_, bf16[3,256,256]{2,1,0:T(8,128)(2,1)} %collective-permute-done.4.refs_1_, ...), custom_call_target="tpu_custom_call" | custom-call | flops 1 | bytes 1 | tf_op jit(solution)/shard_map/image_stats/pallas_call | solution.py:121
  122.2 5.8 %plane_stats.1 = (bf16[4,2,256,256]{3,2,1,0:T(8,128)(2,1)S(1)}, f32[8,128]{1,0:T(8,128)S(1)}) custom-call(s32[5]{0:T(128)S(1)} %stack.70.ids_ref, bf16[8,5,128,256]{3,2,1,0:T(8,128)(2,1)S(1)} %all-to-all-done.1.refs_0_.refs_1_, bf16[8,5,128,256]{3,2,1,0:T(8,128)(2,1)S(1)} %all-to-all-done.1.refs_0_.refs_1_, bf16[4,256,512]{2,1,0:T(8,128)(2,1)S(1)} %copy-done.8), custom_call_target="tpu_custom_call" | custom-call | flops 1 | bytes 1 | tf_op jit(solution)/shard_map/plane_stats/pallas_call | solution.py:165
  132.7 4.6 %all-to-all-start.2 = ((f32[32,8,128]{2,1,0:T(8,128)}), f32[32,8,128]{2,1,0:T(8,128)S(1)}, u32[]{:S(2)}, u32[]{:S(2)}) async-start(f32[32,8,128]{2,1,0:T(8,128)} %broadcast_in_dim.23), calls=%async_computation.2 | async-start | bytes 262144 | tf_op jit(solution)/shard_map/all_to_all | solution.py:562
  142.8 6.7 %all-to-all-done.2 = f32[32,8,128]{2,1,0:T(8,128)S(1)} async-done(((f32[32,8,128]{2,1,0:T(8,128)}), f32[32,8,128]{2,1,0:T(8,128)S(1)}, u32[]{:S(2)}, u32[]{:S(2)}) %all-to-all-start.2) | async-done | bytes 131104 | tf_op jit(solution)/shard_map/all_to_all | solution.py:562
  153.7 5.6 %advance_all.2 = (f32[4,256,512]{2,1,0:T(8,128)}, f32[4,256,512]{2,1,0:T(8,128)}, bf16[4,256,512]{2,1,0:T(8,128)(2,1)S(1)}) custom-call(s32[5]{0:T(128)S(1)} %stack.70.ids_ref, f32[2]{0:T(128)S(1)} %pad_maximum_fusion.10.sc_ref, bf16[4,2,256,256]{3,2,1,0:T(8,128)(2,1)S(1)} %pad_maximum_fusion.2.h_ref, f32[4,256,512]{2,1,0:T(8,128)S(1)} %copy-done.2, ...), custom_call_target="tpu_custom_call" | custom-call | flops 1 | bytes 1 | tf_op jit(solution)/shard_map/advance_all/pallas_call | solution.py:241
  159.3 8.7 %column_products.1 = (bf16[2048,1024]{1,0:T(8,128)(2,1)}, bf16[2048,256]{1,0:T(8,128)(2,1)S(1)}) custom-call(s32[5]{0:T(128)S(1)} %stack.70.ids_ref, bf16[2048,1024]{1,0:T(8,128)(2,1)} %g_ref.1, bf16[2048,256]{1,0:T(8,128)(2,1)S(1)} %pad_maximum_fusion.l_ref, bf16[4,256,512]{2,1,0:T(8,128)(2,1)S(1)} %get-tuple-element.56.k_ref), custom_call_target="tpu_custom_call" | custom-call | flops 1 | bytes 1 | tf_op jit(solution)/shard_map/column_products/pallas_call | solution.py:287
  185.5 5.6 %advance_all.3 = (f32[4,256,512]{2,1,0:T(8,128)}, f32[4,256,512]{2,1,0:T(8,128)}, bf16[4,256,512]{2,1,0:T(8,128)(2,1)S(1)}) custom-call(s32[5]{0:T(128)S(1)} %stack.70.ids_ref, f32[2]{0:T(128)S(1)} %pad_maximum_fusion.11.sc_ref, bf16[4,2,256,256]{3,2,1,0:T(8,128)(2,1)S(1)} %pad_maximum_fusion.3.h_ref, f32[4,256,512]{2,1,0:T(8,128)S(1)} %copy-done.3, ...), custom_call_target="tpu_custom_call" | custom-call | flops 1 | bytes 1 | tf_op jit(solution)/shard_map/advance_all/pallas_call | solution.py:241
  192.9 8.9 %collective-permute-start.27 = (bf16[2,256,512]{2,1,0:T(8,128)(2,1)S(1)}, bf16[2,256,512]{2,1,0:T(8,128)(2,1)S(1)}, u32[]{:S(2)}, u32[]{:S(2)}) collective-permute-start(bf16[2,256,512]{2,1,0:T(8,128)(2,1)S(1)} %get-tuple-element.92), channel_id=1, source_target_pairs={{0,0},{1,1},{2,8},{3,9},{4,16},{5,17},{6,24},{7,25},{8,2},{9,3},{1... | collective-permute-start | bytes 1572872 | tf_op jit(solution)/shard_map/ppermute | solution.py:596
  207.4 20.0 %collective-permute-done.27 = bf16[2,256,512]{2,1,0:T(8,128)(2,1)S(1)} collective-permute-done((bf16[2,256,512]{2,1,0:T(8,128)(2,1)S(1)}, bf16[2,256,512]{2,1,0:T(8,128)(2,1)S(1)}, u32[]{:S(2)}, u32[]{:S(2)}) %collective-permute-start.27) | collective-permute-done | bytes 524320 | tf_op jit(solution)/shard_map/ppermute | solution.py:596
  232.2 8.1 %collective-permute-done.29 = bf16[2,256,512]{2,1,0:T(8,128)(2,1)S(1)} collective-permute-done((bf16[2,256,512]{2,1,0:T(8,128)(2,1)S(1)}, bf16[2,256,512]{2,1,0:T(8,128)(2,1)S(1)}, u32[]{:S(2)}, u32[]{:S(2)}) %collective-permute-start.29) | collective-permute-done | bytes 524320 | tf_op jit(solution)/shard_map/ppermute | solution.py:597
  241.7 9.9 %collective-permute-done.30 = bf16[2,256,512]{2,1,0:T(8,128)(2,1)S(1)} collective-permute-done((bf16[2,256,512]{2,1,0:T(8,128)(2,1)S(1)}, bf16[2,256,512]{2,1,0:T(8,128)(2,1)S(1)}, u32[]{:S(2)}, u32[]{:S(2)}) %collective-permute-start.30) | collective-permute-done | bytes 524320 | tf_op jit(solution)/shard_map/ppermute | solution.py:597
  251.6 10.7 %row_products.1 = (bf16[2048,1024]{1,0:T(8,128)(2,1)}, bf16[256,768]{1,0:T(8,128)(2,1)S(1)}) custom-call(s32[5]{0:T(128)S(1)} %stack.70.ids_ref, bf16[2048,1024]{1,0:T(8,128)(2,1)} %get-tuple-element.65.s_ref, bf16[256,768]{1,0:T(8,128)(2,1)S(1)} %broadcast_select_fusion.5.l_ref, bf16[8,256,512]{2,1,0:T(8,128)(2,1)S(1)} %constant_dynamic-update-slice_fusion.5.c_ref), custom_call_target="tpu_custom_call" | custom-call | flops 1 | bytes 1 | tf_op jit(solution)/shard_map/row_products/pallas_call | solution.py:352
  263.8 4.3 %lead_row_products.1 = (bf16[2048,1024]{1,0:T(8,128)(2,1)}, bf16[256,256]{1,0:T(8,128)(2,1)S(1)}) custom-call(s32[5]{0:T(128)S(1)} %stack.70.ids_ref, bf16[2048,1024]{1,0:T(8,128)(2,1)} %get-tuple-element.65.s_ref, bf16[2048,256]{1,0:T(8,128)(2,1)S(1)} %bitcast.55, ...), custom_call_target="tpu_custom_call", output_to_operand_aliasing={{0}: (5, {})} | custom-call | flops 1 | bytes 1 | tf_op jit(solution)/shard_map/lead_row_products/pallas_call | solution.py:398
  269.3 4.1 %collective-permute-done.35 = bf16[256,768]{1,0:T(8,128)(2,1)S(1)} collective-permute-done((bf16[256,768]{1,0:T(8,128)(2,1)S(1)}, bf16[256,768]{1,0:T(8,128)(2,1)S(1)}, u32[]{:S(2)}, u32[]{:S(2)}) %collective-permute-start.35) | collective-permute-done | bytes 393248 | tf_op jit(solution)/shard_map/ppermute | solution.py:616
  273.6 5.6 %collective-permute-start.36 = (bf16[256,768]{1,0:T(8,128)(2,1)S(1)}, bf16[256,768]{1,0:T(8,128)(2,1)S(1)}, u32[]{:S(2)}, u32[]{:S(2)}) collective-permute-start(bf16[256,768]{1,0:T(8,128)(2,1)S(1)} %fusion), channel_id=1, source_target_pairs={{8,0},{9,1},{10,2},{11,3},{12,4},{13,5},{14,6},{15,7}} | collective-permute-start | bytes 1179656 | tf_op jit(solution)/shard_map/ppermute | solution.py:617
  (154 shorter events, 87.1 us)
Async XLA Ops:
  6.2 35.4 %all-to-all-start = ((bf16[8,5,128,256]{3,2,1,0:T(8,128)(2,1)}), bf16[8,5,128,256]{3,2,1,0:T(8,128)(2,1)S(1)}, u32[]{:S(2)}, u32[]{:S(2)}) async-start(bf16[8,5,128,256]{3,2,1,0:T(8,128)(2,1)} %copy-done.5), calls=%async_computation | async-start | bytes 5242880 | tf_op jit(solution)/shard_map/all_to_all | solution.py:516
  11.7 19.3 %collective-permute-start.2 = (bf16[256,512]{1,0:T(8,128)(2,1)S(1)}, bf16[256,512]{1,0:T(8,128)(2,1)S(1)}, u32[]{:S(2)}, u32[]{:S(2)}) collective-permute-start(bf16[256,512]{1,0:T(8,128)(2,1)S(1)} %pad_maximum_fusion.8), channel_id=1, source_target_pairs={{0,6},{1,7},{2,4},{3,5},{4,2},{5,3},{6,0},{7,1},{8,14},{9,15},{10,... | collective-permute-start | bytes 786440 | tf_op jit(solution)/shard_map/ppermute | solution.py:482
  12.0 22.6 %collective-permute-start.1 = (bf16[256,512]{1,0:T(8,128)(2,1)S(1)}, bf16[256,512]{1,0:T(8,128)(2,1)}, u32[]{:S(2)}, u32[]{:S(2)}) collective-permute-start(bf16[256,512]{1,0:T(8,128)(2,1)S(1)} %pad_maximum_fusion.8), channel_id=1, source_target_pairs={{0,4},{1,5},{2,6},{3,7},{4,0},{5,1},{6,2},{7,3},{8,12},{9,13},{10,... | collective-permute-start | bytes 786440 | tf_op jit(solution)/shard_map/ppermute | solution.py:482
  15.2 19.4 %collective-permute-start = (bf16[256,512]{1,0:T(8,128)(2,1)S(1)}, bf16[256,512]{1,0:T(8,128)(2,1)}, u32[]{:S(2)}, u32[]{:S(2)}) collective-permute-start(bf16[256,512]{1,0:T(8,128)(2,1)S(1)} %pad_maximum_fusion.8), channel_id=1, source_target_pairs={{0,2},{1,3},{2,0},{3,1},{4,6},{5,7},{6,4},{7,5},{8,10},{9,11},{10,... | collective-permute-start | bytes 786440 | tf_op jit(solution)/shard_map/ppermute | solution.py:482
  17.2 24.4 %collective-permute-start.3 = (bf16[1280,256]{1,0:T(8,128)(2,1)}, bf16[1280,256]{1,0:T(8,128)(2,1)}, u32[]{:S(2)}, u32[]{:S(2)}) collective-permute-start(bf16[1280,256]{1,0:T(8,128)(2,1)} %slice.115), channel_id=1, source_target_pairs={{0,1},{8,9},{16,17},{24,25}} | collective-permute-start | bytes 1966088 | tf_op jit(solution)/shard_map/ppermute | solution.py:522
  46.0 75.0 %all-to-all-start.1 = ((bf16[8,5,128,256]{3,2,1,0:T(8,128)(2,1)}), bf16[8,5,128,256]{3,2,1,0:T(8,128)(2,1)S(1)}, u32[]{:S(2)}, u32[]{:S(2)}) async-start(bf16[8,5,128,256]{3,2,1,0:T(8,128)(2,1)} %copy-done.4), calls=%async_computation.1 | async-start | bytes 5242880 | tf_op jit(solution)/shard_map/all_to_all | solution.py:516
  52.6 46.3 %collective-permute-start.9 = (bf16[1280,256]{1,0:T(8,128)(2,1)}, bf16[1280,256]{1,0:T(8,128)(2,1)}, u32[]{:S(2)}, u32[]{:S(2)}) collective-permute-start(bf16[1280,256]{1,0:T(8,128)(2,1)} %fusion.1), channel_id=1, source_target_pairs={{0,4},{1,5},{8,12},{9,13},{16,20},{17,21},{24,28},{25,29}} | collective-permute-start | bytes 1966088 | tf_op jit(solution)/shard_map/ppermute | solution.py:530
  55.4 43.6 %collective-permute-start.5 = (bf16[3,256,256]{2,1,0:T(8,128)(2,1)}, bf16[3,256,256]{2,1,0:T(8,128)(2,1)}, u32[]{:S(2)}, u32[]{:S(2)}) collective-permute-start(bf16[3,256,256]{2,1,0:T(8,128)(2,1)} %get-tuple-element.86), channel_id=1, source_target_pairs={{0,4},{1,5},{2,6},{3,7},{4,0},{5,1},{6,2},{7,3},{8,12},{9,13},{10,... | collective-permute-start | bytes 1179656 | tf_op jit(solution)/shard_map/ppermute | solution.py:482
  68.6 30.4 %collective-permute-start.4 = (bf16[3,256,256]{2,1,0:T(8,128)(2,1)}, bf16[3,256,256]{2,1,0:T(8,128)(2,1)}, u32[]{:S(2)}, u32[]{:S(2)}) collective-permute-start(bf16[3,256,256]{2,1,0:T(8,128)(2,1)} %get-tuple-element.87), channel_id=1, source_target_pairs={{0,2},{1,3},{2,0},{3,1},{4,6},{5,7},{6,4},{7,5},{8,10},{9,11},{10,... | collective-permute-start | bytes 1179656 | tf_op jit(solution)/shard_map/ppermute | solution.py:482
  101.0 28.1 %collective-permute-start.10 = (bf16[1280,256]{1,0:T(8,128)(2,1)}, bf16[1280,256]{1,0:T(8,128)(2,1)}, u32[]{:S(2)}, u32[]{:S(2)}) collective-permute-start(bf16[1280,256]{1,0:T(8,128)(2,1)} %broadcast_select_fusion), channel_id=1, source_target_pairs={{0,2},{1,3},{4,6},{5,7},{8,10},{9,11},{12,14},{13,15},{16,18},{17,... | collective-permute-start | bytes 1966088 | tf_op jit(solution)/shard_map/ppermute | solution.py:530
  130.3 21.8 %collective-permute-start.11 = (bf16[1280,256]{1,0:T(8,128)(2,1)S(1)}, bf16[1280,256]{1,0:T(8,128)(2,1)S(1)}, u32[]{:S(2)}, u32[]{:S(2)}) collective-permute-start(bf16[1280,256]{1,0:T(8,128)(2,1)S(1)} %broadcast_select_fusion.1), channel_id=1, source_target_pairs={{0,1},{1,0},{2,3},{3,2},{4,5},{5,4},{6,7},{7,6},{8,9},{9,8},{10,11... | collective-permute-start | bytes 1966088 | tf_op jit(solution)/shard_map/ppermute | solution.py:567
  139.5 28.5 %collective-permute-start.14 = (bf16[2,256,256]{2,1,0:T(8,128)(2,1)}, bf16[2,256,256]{2,1,0:T(8,128)(2,1)}, u32[]{:S(2)}, u32[]{:S(2)}) collective-permute-start(bf16[2,256,256]{2,1,0:T(8,128)(2,1)} %get-tuple-element.94), channel_id=1, source_target_pairs={{0,6},{1,7},{2,4},{3,5},{4,2},{5,3},{6,0},{7,1},{8,14},{9,15},{10,... | collective-permute-start | bytes 786440 | tf_op jit(solution)/shard_map/ppermute | solution.py:482
  139.7 28.3 %collective-permute-start.13 = (bf16[2,256,256]{2,1,0:T(8,128)(2,1)}, bf16[2,256,256]{2,1,0:T(8,128)(2,1)}, u32[]{:S(2)}, u32[]{:S(2)}) collective-permute-start(bf16[2,256,256]{2,1,0:T(8,128)(2,1)} %get-tuple-element.95), channel_id=1, source_target_pairs={{0,4},{1,5},{2,6},{3,7},{4,0},{5,1},{6,2},{7,3},{8,12},{9,13},{10,... | collective-permute-start | bytes 786440 | tf_op jit(solution)/shard_map/ppermute | solution.py:482
  142.8 25.2 %collective-permute-start.12 = (bf16[2,256,256]{2,1,0:T(8,128)(2,1)}, bf16[2,256,256]{2,1,0:T(8,128)(2,1)}, u32[]{:S(2)}, u32[]{:S(2)}) collective-permute-start(bf16[2,256,256]{2,1,0:T(8,128)(2,1)} %get-tuple-element.96), channel_id=1, source_target_pairs={{0,2},{1,3},{2,0},{3,1},{4,6},{5,7},{6,4},{7,5},{8,10},{9,11},{10,... | collective-permute-start | bytes 786440 | tf_op jit(solution)/shard_map/ppermute | solution.py:482
  179.9 27.5 %collective-permute-start.32 = (bf16[256,768]{1,0:T(8,128)(2,1)S(1)}, bf16[256,768]{1,0:T(8,128)(2,1)S(1)}, u32[]{:S(2)}, u32[]{:S(2)}) collective-permute-start(bf16[256,768]{1,0:T(8,128)(2,1)S(1)} %broadcast_select_fusion.4), channel_id=1, source_target_pairs={{0,8},{16,24},{1,9},{17,25},{2,10},{18,26},{3,11},{19,27},{4,12},{... | collective-permute-start | bytes 1179656 | tf_op jit(solution)/shard_map/ppermute | solution.py:486
  192.9 34.5 %collective-permute-start.27 = (bf16[2,256,512]{2,1,0:T(8,128)(2,1)S(1)}, bf16[2,256,512]{2,1,0:T(8,128)(2,1)S(1)}, u32[]{:S(2)}, u32[]{:S(2)}) collective-permute-start(bf16[2,256,512]{2,1,0:T(8,128)(2,1)S(1)} %get-tuple-element.92), channel_id=1, source_target_pairs={{0,0},{1,1},{2,8},{3,9},{4,16},{5,17},{6,24},{7,25},{8,2},{9,3},{1... | collective-permute-start | bytes 1572872 | tf_op jit(solution)/shard_map/ppermute | solution.py:596
  202.8 26.7 %collective-permute-start.25 = (bf16[256,256]{1,0:T(8,128)(2,1)S(1)}, bf16[256,256]{1,0:T(8,128)(2,1)S(1)}, u32[]{:S(2)}, u32[]{:S(2)}) collective-permute-start(bf16[256,256]{1,0:T(8,128)(2,1)S(1)} %get-tuple-element.83), channel_id=1, source_target_pairs={{0,16},{1,17},{2,18},{3,19},{4,20},{5,21},{6,22},{7,23}} | collective-permute-start | bytes 393224 | tf_op jit(solution)/shard_map/ppermute | solution.py:485
  203.4 23.9 %collective-permute-start.21 = (bf16[256,256]{1,0:T(8,128)(2,1)S(1)}, bf16[256,256]{1,0:T(8,128)(2,1)S(1)}, u32[]{:S(2)}, u32[]{:S(2)}) collective-permute-start(bf16[256,256]{1,0:T(8,128)(2,1)S(1)} %get-tuple-element.84), channel_id=1, source_target_pairs={{1,0},{3,2},{5,4},{7,6},{9,8},{11,10},{13,12},{15,14},{17,16},{19,... | collective-permute-start | bytes 393224 | tf_op jit(solution)/shard_map/ppermute | solution.py:611
  204.7 25.4 %collective-permute-start.28 = (bf16[2,256,512]{2,1,0:T(8,128)(2,1)S(1)}, bf16[2,256,512]{2,1,0:T(8,128)(2,1)S(1)}, u32[]{:S(2)}, u32[]{:S(2)}) collective-permute-start(bf16[2,256,512]{2,1,0:T(8,128)(2,1)S(1)} %get-tuple-element.91), channel_id=1, source_target_pairs={{16,0},{17,1},{18,8},{19,9},{20,16},{21,17},{22,24},{23,25},{24,2}... | collective-permute-start | bytes 1572872 | tf_op jit(solution)/shard_map/ppermute | solution.py:596
  227.4 36.3 %collective-permute-start.24 = (bf16[2,256,256]{2,1,0:T(8,128)(2,1)S(1)}, bf16[2,256,256]{2,1,0:T(8,128)(2,1)S(1)}, u32[]{:S(2)}, u32[]{:S(2)}) collective-permute-start(bf16[2,256,256]{2,1,0:T(8,128)(2,1)S(1)} %pad_maximum_fusion.9), channel_id=1, source_target_pairs={{6,0},{14,8},{22,16},{30,24}} | collective-permute-start | bytes 786440 | tf_op jit(solution)/shard_map/ppermute | solution.py:612
  228.1 35.6 %collective-permute-start.23 = (bf16[2,256,256]{2,1,0:T(8,128)(2,1)S(1)}, bf16[2,256,256]{2,1,0:T(8,128)(2,1)S(1)}, u32[]{:S(2)}, u32[]{:S(2)}) collective-permute-start(bf16[2,256,256]{2,1,0:T(8,128)(2,1)S(1)} %pad_maximum_fusion.9), channel_id=1, source_target_pairs={{4,0},{12,8},{20,16},{28,24}} | collective-permute-start | bytes 786440 | tf_op jit(solution)/shard_map/ppermute | solution.py:612
  229.4 34.2 %collective-permute-start.22 = (bf16[2,256,256]{2,1,0:T(8,128)(2,1)S(1)}, bf16[2,256,256]{2,1,0:T(8,128)(2,1)S(1)}, u32[]{:S(2)}, u32[]{:S(2)}) collective-permute-start(bf16[2,256,256]{2,1,0:T(8,128)(2,1)S(1)} %pad_maximum_fusion.9), channel_id=1, source_target_pairs={{2,0},{10,8},{18,16},{26,24}} | collective-permute-start | bytes 786440 | tf_op jit(solution)/shard_map/ppermute | solution.py:612
  230.1 21.4 %collective-permute-start.30 = (bf16[2,256,512]{2,1,0:T(8,128)(2,1)S(1)}, bf16[2,256,512]{2,1,0:T(8,128)(2,1)S(1)}, u32[]{:S(2)}, u32[]{:S(2)}) collective-permute-start(bf16[2,256,512]{2,1,0:T(8,128)(2,1)S(1)} %collective-permute-done.28), channel_id=1, source_target_pairs={{0,1},{1,0},{2,3},{3,2},{4,5},{5,4},{6,7},{7,6},{8,9},{9,8},{10,11... | collective-permute-start | bytes 1572872 | tf_op jit(solution)/shard_map/ppermute | solution.py:597
  240.3 23.3 %collective-permute-start.26 = (bf16[256,256]{1,0:T(8,128)(2,1)S(1)}, bf16[256,256]{1,0:T(8,128)(2,1)S(1)}, u32[]{:S(2)}, u32[]{:S(2)}) collective-permute-start(bf16[256,256]{1,0:T(8,128)(2,1)S(1)} %broadcast_select_fusion.6), channel_id=1, source_target_pairs={{0,8},{16,24},{1,9},{17,25},{2,10},{18,26},{3,11},{19,27},{4,12},{... | collective-permute-start | bytes 393224 | tf_op jit(solution)/shard_map/ppermute | solution.py:486
  (31 other events, 239.7 us)

commit v4 on v3

--- a/solution.py
+++ b/solution.py
@@ -539,12 +539,12 @@
     )
     owned_c = exchange(packed_c)
 
-    raw_k = raw_moments(ids, after(owned_k, load_x))
+    raw_k = raw_moments(ids, owned_k)
     sent_k = each_along_z(raw_k)
     stride = zs // 2
-    mine = jnp.where(s == 0, load[:load_half], after(load_x, raw_k))
+    mine = jnp.where(s == 0, load[:load_half], after(load_x, *sent_k))
     while stride > 1:
-        got = after(down_z(mine, stride), *sent_k)
+        got = down_z(mine, stride)
         mine = jnp.where(z % (2 * stride) == 0, mine, got)
         stride //= 2
     last_z = down_z(mine, 1)
@@ -610,14 +610,16 @@
     block_sum = block_sum.astype(bf16)
     pair = jnp.stack([block_sum, lax.ppermute(block_sum, "fsdp", [(2 * k + 1, 2 * k) for k in range(zs)])])
     gathered = [pair] + [lax.ppermute(pair, "fsdp", [(xs * k, 0)]) for k in range(1, zs)]
-    gathered = jnp.concatenate(gathered, axis=0).reshape(count, bs)
-    top_lead = from_group_0(jnp.where(s == 0, block_sum, second[:bs, :bs]))
+    top_lead = jnp.where(s == 0, block_sum, second[:bs, :bs])
+    top_lead = from_group_0(after(top_lead, halves[0]))
     def sum_to_group_0(value):
         total = value.astype(f32) + lax.ppermute(value, "dp", [(2, 0), (3, 1)]).astype(f32)
         other = lax.ppermute(total.astype(bf16), "dp", [(1, 0)])
         return (total + other.astype(f32)).astype(bf16)
 
     precond, up_rest = rows(ids, second, top_rest, c_rows)
+    gathered = [after(g, up_rest) for g in gathered]
+    gathered = jnp.concatenate(gathered, axis=0).reshape(count, bs)
     up_rest = sum_to_group_0(up_rest)
     precond, up_lead = lead_rows_products(ids, second, gathered, top_lead, c_rows, precond)
     precond = put_top(ids, precond, sum_to_group_0(up_lead), up_rest)

time: 286 us -> 271 us (0.948)
  starting transfers between devices: 91.7 us -> 71.3 us
  waiting for transfers between devices: 95.1 us -> 98.8 us
    ppermute x2, waiting for transfers between devices: 0.01 us -> 16.6 us  [down_z(): return lax.ppermute(value, 'fsdp', pairs)]
    ppermute x12, starting transfers between devices: 24.2 us -> 12.8 us  [along_z(): return lax.ppermute(value, 'fsdp', pairs)]
    ppermute x2, starting transfers between devices: 13.7 us -> 3.42 us  [down_z(): return lax.ppermute(value, 'fsdp', pairs)]
    ppermute x12, waiting for transfers between devices: 36.3 us -> 29.6 us  [along_z(): return lax.ppermute(value, 'fsdp', pairs)]
    ppermute x2, starting transfers between devices: 6.94 us -> 10.2 us  [sum_to_group_0(): other = lax.ppermute(total.astype(bf16), 'dp', [(1, 0)])]
    unnamed x37 -> x27, local copies, waits for them, and re-layouts: 10.7 us -> 9.5 us
  transfers between devices with their start and end apart: 40 -> 40, of which waited for: 14 -> 15; matrix products, arithmetic and copies ran while one was open for 9% -> 11% of each run, Pallas kernels for 16% -> 18%
where the time goes in v4:
time: 271 us; the launch traced here: 269 us
  waiting for transfers between devices  98.8 us (36%)
  starting transfers between devices  71.3 us (26%)
  Pallas kernels  51.5 us (19%)
  local copies, waits for them, and re-layouts  21.7 us (8%)
  other arithmetic  19.9 us (7%)
  between operations  5.74 us (2%)
    ppermute x12, waiting for transfers between devices, along_z(): return lax.ppermute(value, 'fsdp', pairs)  29.6 us
    ppermute x2, waiting for transfers between devices, planned(): lax.ppermute(cb[h * (ds // 2):(h + 1) * (ds // 2)], both, pairs)  18.2 us
    ppermute x2, waiting for transfers between devices, down_z(): return lax.ppermute(value, 'fsdp', pairs)  16.6 us
    ppermute x2, waiting for transfers between devices, planned(): others = [lax.ppermute(h, 'fsdp', flip_x) for h in halves]  15.4 us
    ppermute x12, starting transfers between devices, along_z(): return lax.ppermute(value, 'fsdp', pairs)  12.8 us
    pallas_call x2, Pallas kernels, advance_all(): pl.pallas_call(functools.partial(advance_body, width), grid_spec=pltpu.Pr...  11.2 us
    pallas_call x1, Pallas kernels, rows(): pl.pallas_call(rows_body, grid_spec=pltpu.PrefetchScalarGridSpec(num_scal...  10.7 us
    ppermute x2, starting transfers between devices, planned(): lax.ppermute(cb[h * (ds // 2):(h + 1) * (ds // 2)], both, pairs)  10.4 us
  transfers between devices with their start and end apart: 40, of which 15 were waited for; matrix products, arithmetic and copies ran while one was open for 11% of the time, Pallas kernels for 18%

profile of v4, /device:TPU:17, one launch (start us, length us, event | category | flops | bytes accessed | tf_op | source)
XLA Modules:
  0.0 268.9 jit_solution(12769940382934943229)
XLA Ops:
  6.1 4.4 %all-to-all-start = ((bf16[8,5,128,256]{3,2,1,0:T(8,128)(2,1)}), bf16[8,5,128,256]{3,2,1,0:T(8,128)(2,1)S(1)}, u32[]{:S(2)}, u32[]{:S(2)}) async-start(bf16[8,5,128,256]{3,2,1,0:T(8,128)(2,1)} %copy-done.4), calls=%async_computation | async-start | bytes 5242880 | tf_op jit(solution)/shard_map/all_to_all | solution.py:516
  20.6 3.2 %multiply_reduce_fusion = (f32[]{:T(128)}, f32[]{:T(128)}, f32[]{:T(128)}, f32[]{:T(128)}) fusion(f32[4,256,512]{2,1,0:T(8,128)} %fac_ref.3, f32[4]{0:T(128)S(1)} %compare_convert_fusion, f32[4,256,512]{2,1,0:T(8,128)} %fac_ref.2), kind=kLoop, calls=%fused_computation.6 | loop fusion | flops 2621436 | bytes 4194336 | tf_op jit(solution)/shard_map/reduce_sum | solution.py:513
  26.4 4.7 %collective-permute-done.2 = bf16[256,512]{1,0:T(8,128)(2,1)S(1)} collective-permute-done((bf16[256,512]{1,0:T(8,128)(2,1)S(1)}, bf16[256,512]{1,0:T(8,128)(2,1)S(1)}, u32[]{:S(2)}, u32[]{:S(2)}) %collective-permute-start.2) | collective-permute-done | bytes 262176 | tf_op jit(solution)/shard_map/ppermute | solution.py:482
  31.0 3.5 %collective-permute-done.1 = bf16[256,512]{1,0:T(8,128)(2,1)S(1)} collective-permute-done((bf16[256,512]{1,0:T(8,128)(2,1)S(1)}, bf16[256,512]{1,0:T(8,128)(2,1)S(1)}, u32[]{:S(2)}, u32[]{:S(2)}) %collective-permute-start.1) | collective-permute-done | bytes 262176 | tf_op jit(solution)/shard_map/ppermute | solution.py:482
  36.6 4.9 %all-to-all-done.x_ref.l_ref = bf16[8,5,128,256]{3,2,1,0:T(8,128)(2,1)S(1)} async-done(((bf16[8,5,128,256]{3,2,1,0:T(8,128)(2,1)}), bf16[8,5,128,256]{3,2,1,0:T(8,128)(2,1)S(1)}, u32[]{:S(2)}, u32[]{:S(2)}) %all-to-all-start) | async-done | bytes 2621472 | tf_op jit(solution)/shard_map/all_to_all | solution.py:516
  41.5 3.3 %raw_moments.1 = bf16[4,3,256,256]{3,2,1,0:T(8,128)(2,1)S(1)} custom-call(s32[5]{0:T(128)S(1)} %stack.70.ids_ref, bf16[8,5,128,256]{3,2,1,0:T(8,128)(2,1)S(1)} %all-to-all-done.x_ref.l_ref, bf16[8,5,128,256]{3,2,1,0:T(8,128)(2,1)S(1)} %all-to-all-done.x_ref.l_ref), custom_call_target="tpu_custom_call" | custom-call | flops 1 | bytes 1 | tf_op jit(solution)/shard_map/raw_moments/pallas_call | solution.py:78
  53.2 4.9 %all-to-all-start.1 = ((bf16[8,5,128,256]{3,2,1,0:T(8,128)(2,1)}), bf16[8,5,128,256]{3,2,1,0:T(8,128)(2,1)S(1)}, u32[]{:S(2)}, u32[]{:S(2)}) async-start(bf16[8,5,128,256]{3,2,1,0:T(8,128)(2,1)} %copy-done.3), calls=%async_computation.1 | async-start | bytes 5242880 | tf_op jit(solution)/shard_map/all_to_all | solution.py:516
  58.1 14.7 %collective-permute-done.5.refs_3_ = bf16[3,256,256]{2,1,0:T(8,128)(2,1)S(1)} collective-permute-done((bf16[3,256,256]{2,1,0:T(8,128)(2,1)}, bf16[3,256,256]{2,1,0:T(8,128)(2,1)S(1)}, u32[]{:S(2)}, u32[]{:S(2)}) %collective-permute-start.5) | collective-permute-done | bytes 393248 | tf_op jit(solution)/shard_map/ppermute | solution.py:482
  72.8 6.7 %collective-permute-done.4.refs_2_ = bf16[3,256,256]{2,1,0:T(8,128)(2,1)} collective-permute-done((bf16[3,256,256]{2,1,0:T(8,128)(2,1)}, bf16[3,256,256]{2,1,0:T(8,128)(2,1)}, u32[]{:S(2)}, u32[]{:S(2)}) %collective-permute-start.4) | collective-permute-done | bytes 393248 | tf_op jit(solution)/shard_map/ppermute | solution.py:482
  83.1 16.6 %collective-permute-done.9 = bf16[1280,256]{1,0:T(8,128)(2,1)} collective-permute-done((bf16[1280,256]{1,0:T(8,128)(2,1)}, bf16[1280,256]{1,0:T(8,128)(2,1)}, u32[]{:S(2)}, u32[]{:S(2)}) %collective-permute-start.9) | collective-permute-done | bytes 655392 | tf_op jit(solution)/shard_map/ppermute | solution.py:530
  107.2 4.3 %image_stats.1 = (bf16[2,256,256]{2,1,0:T(8,128)(2,1)S(1)}, f32[8,128]{1,0:T(8,128)S(1)}) custom-call(s32[5]{0:T(128)S(1)} %stack.70.ids_ref, f32[1]{0:T(128)} %bitcast.4.sc_ref, bf16[3,256,256]{2,1,0:T(8,128)(2,1)S(1)} %get-tuple-element.94.refs_0_, bf16[3,256,256]{2,1,0:T(8,128)(2,1)} %collective-permute-done.3.refs_1_, ...), custom_call_target="tpu_custom_call" | custom-call | flops 1 | bytes 1 | tf_op jit(solution)/shard_map/image_stats/pallas_call | solution.py:121
  112.7 5.8 %plane_stats.1 = (bf16[4,2,256,256]{3,2,1,0:T(8,128)(2,1)S(1)}, f32[8,128]{1,0:T(8,128)S(1)}) custom-call(s32[5]{0:T(128)S(1)} %stack.70.ids_ref, bf16[8,5,128,256]{3,2,1,0:T(8,128)(2,1)S(1)} %all-to-all-done.1.refs_0_.refs_1_, bf16[8,5,128,256]{3,2,1,0:T(8,128)(2,1)S(1)} %all-to-all-done.1.refs_0_.refs_1_, bf16[4,256,512]{2,1,0:T(8,128)(2,1)S(1)} %copy-done.5), custom_call_target="tpu_custom_call" | custom-call | flops 1 | bytes 1 | tf_op jit(solution)/shard_map/plane_stats/pallas_call | solution.py:165
  122.4 6.6 %all-to-all-start.2 = ((f32[32,8,128]{2,1,0:T(8,128)}), f32[32,8,128]{2,1,0:T(8,128)S(1)}, u32[]{:S(2)}, u32[]{:S(2)}) async-start(f32[32,8,128]{2,1,0:T(8,128)} %broadcast_in_dim.23), calls=%async_computation.2 | async-start | bytes 262144 | tf_op jit(solution)/shard_map/all_to_all | solution.py:562
  134.5 5.7 %all-to-all-done.2 = f32[32,8,128]{2,1,0:T(8,128)S(1)} async-done(((f32[32,8,128]{2,1,0:T(8,128)}), f32[32,8,128]{2,1,0:T(8,128)S(1)}, u32[]{:S(2)}, u32[]{:S(2)}) %all-to-all-start.2) | async-done | bytes 131104 | tf_op jit(solution)/shard_map/all_to_all | solution.py:562
  144.5 5.6 %advance_all.2 = (f32[4,256,512]{2,1,0:T(8,128)}, f32[4,256,512]{2,1,0:T(8,128)}, bf16[4,256,512]{2,1,0:T(8,128)(2,1)S(1)}) custom-call(s32[5]{0:T(128)S(1)} %stack.70.ids_ref, f32[2]{0:T(128)S(1)} %pad_maximum_fusion.11.sc_ref, bf16[4,2,256,256]{3,2,1,0:T(8,128)(2,1)S(1)} %pad_maximum_fusion.2.h_ref, f32[4,256,512]{2,1,0:T(8,128)S(1)} %copy-done.1, ...), custom_call_target="tpu_custom_call" | custom-call | flops 1 | bytes 1 | tf_op jit(solution)/shard_map/advance_all/pallas_call | solution.py:241
  150.0 8.7 %column_products.1 = (bf16[2048,1024]{1,0:T(8,128)(2,1)}, bf16[2048,256]{1,0:T(8,128)(2,1)S(1)}) custom-call(s32[5]{0:T(128)S(1)} %stack.70.ids_ref, bf16[2048,1024]{1,0:T(8,128)(2,1)} %g_ref.1, bf16[2048,256]{1,0:T(8,128)(2,1)S(1)} %pad_maximum_fusion.l_ref, bf16[4,256,512]{2,1,0:T(8,128)(2,1)S(1)} %get-tuple-element.57.k_ref), custom_call_target="tpu_custom_call" | custom-call | flops 1 | bytes 1 | tf_op jit(solution)/shard_map/column_products/pallas_call | solution.py:287
  176.8 5.6 %advance_all.3 = (f32[4,256,512]{2,1,0:T(8,128)}, f32[4,256,512]{2,1,0:T(8,128)}, bf16[4,256,512]{2,1,0:T(8,128)(2,1)S(1)}) custom-call(s32[5]{0:T(128)S(1)} %stack.70.ids_ref, f32[2]{0:T(128)S(1)} %pad_maximum_fusion.12.sc_ref, bf16[4,2,256,256]{3,2,1,0:T(8,128)(2,1)S(1)} %pad_maximum_fusion.3.h_ref, f32[4,256,512]{2,1,0:T(8,128)S(1)} %copy-done.2, ...), custom_call_target="tpu_custom_call" | custom-call | flops 1 | bytes 1 | tf_op jit(solution)/shard_map/advance_all/pallas_call | solution.py:241
  182.5 7.3 %collective-permute-start.24 = (bf16[2,256,512]{2,1,0:T(8,128)(2,1)S(1)}, bf16[2,256,512]{2,1,0:T(8,128)(2,1)S(1)}, u32[]{:S(2)}, u32[]{:S(2)}) collective-permute-start(bf16[2,256,512]{2,1,0:T(8,128)(2,1)S(1)} %get-tuple-element.98), channel_id=1, source_target_pairs={{0,0},{1,1},{2,8},{3,9},{4,16},{5,17},{6,24},{7,25},{8,2},{9,3},{1... | collective-permute-start | bytes 1572872 | tf_op jit(solution)/shard_map/ppermute | solution.py:596
  196.3 18.2 %collective-permute-done.24 = bf16[2,256,512]{2,1,0:T(8,128)(2,1)S(1)} collective-permute-done((bf16[2,256,512]{2,1,0:T(8,128)(2,1)S(1)}, bf16[2,256,512]{2,1,0:T(8,128)(2,1)S(1)}, u32[]{:S(2)}, u32[]{:S(2)}) %collective-permute-start.24) | collective-permute-done | bytes 524320 | tf_op jit(solution)/shard_map/ppermute | solution.py:596
  218.9 5.5 %collective-permute-done.26 = bf16[2,256,512]{2,1,0:T(8,128)(2,1)S(1)} collective-permute-done((bf16[2,256,512]{2,1,0:T(8,128)(2,1)S(1)}, bf16[2,256,512]{2,1,0:T(8,128)(2,1)S(1)}, u32[]{:S(2)}, u32[]{:S(2)}) %collective-permute-start.26) | collective-permute-done | bytes 524320 | tf_op jit(solution)/shard_map/ppermute | solution.py:597
  225.8 9.9 %collective-permute-done.27 = bf16[2,256,512]{2,1,0:T(8,128)(2,1)S(1)} collective-permute-done((bf16[2,256,512]{2,1,0:T(8,128)(2,1)S(1)}, bf16[2,256,512]{2,1,0:T(8,128)(2,1)S(1)}, u32[]{:S(2)}, u32[]{:S(2)}) %collective-permute-start.27) | collective-permute-done | bytes 524320 | tf_op jit(solution)/shard_map/ppermute | solution.py:597
  235.7 10.7 %row_products.1 = (bf16[2048,1024]{1,0:T(8,128)(2,1)}, bf16[256,768]{1,0:T(8,128)(2,1)S(1)}) custom-call(s32[5]{0:T(128)S(1)} %stack.70.ids_ref, bf16[2048,1024]{1,0:T(8,128)(2,1)} %get-tuple-element.66.s_ref, bf16[256,768]{1,0:T(8,128)(2,1)S(1)} %broadcast_select_fusion.5.l_ref, bf16[8,256,512]{2,1,0:T(8,128)(2,1)S(1)} %constant_dynamic-update-slice_fusion.c_ref), custom_call_target="tpu_custom_call" | custom-call | flops 1 | bytes 1 | tf_op jit(solution)/shard_map/row_products/pallas_call | solution.py:352
  247.9 4.2 %lead_row_products.1 = (bf16[2048,1024]{1,0:T(8,128)(2,1)}, bf16[256,256]{1,0:T(8,128)(2,1)S(1)}) custom-call(s32[5]{0:T(128)S(1)} %stack.70.ids_ref, bf16[2048,1024]{1,0:T(8,128)(2,1)} %get-tuple-element.66.s_ref, bf16[2048,256]{1,0:T(8,128)(2,1)S(1)} %bitcast.53, ...), custom_call_target="tpu_custom_call", output_to_operand_aliasing={{0}: (5, {})} | custom-call | flops 1 | bytes 1 | tf_op jit(solution)/shard_map/lead_row_products/pallas_call | solution.py:398
  255.0 8.9 %collective-permute-start.36 = (bf16[256,768]{1,0:T(8,128)(2,1)S(1)}, bf16[256,768]{1,0:T(8,128)(2,1)S(1)}, u32[]{:S(2)}, u32[]{:S(2)}) collective-permute-start(bf16[256,768]{1,0:T(8,128)(2,1)S(1)} %fusion), channel_id=1, source_target_pairs={{8,0},{9,1},{10,2},{11,3},{12,4},{13,5},{14,6},{15,7}} | collective-permute-start | bytes 1179656 | tf_op jit(solution)/shard_map/ppermute | solution.py:617
  (144 shorter events, 89.2 us)
Async XLA Ops:
  6.1 35.4 %all-to-all-start = ((bf16[8,5,128,256]{3,2,1,0:T(8,128)(2,1)}), bf16[8,5,128,256]{3,2,1,0:T(8,128)(2,1)S(1)}, u32[]{:S(2)}, u32[]{:S(2)}) async-start(bf16[8,5,128,256]{3,2,1,0:T(8,128)(2,1)} %copy-done.4), calls=%async_computation | async-start | bytes 5242880 | tf_op jit(solution)/shard_map/all_to_all | solution.py:516
  11.7 19.3 %collective-permute-start.2 = (bf16[256,512]{1,0:T(8,128)(2,1)S(1)}, bf16[256,512]{1,0:T(8,128)(2,1)S(1)}, u32[]{:S(2)}, u32[]{:S(2)}) collective-permute-start(bf16[256,512]{1,0:T(8,128)(2,1)S(1)} %pad_maximum_fusion.9), channel_id=1, source_target_pairs={{0,6},{1,7},{2,4},{3,5},{4,2},{5,3},{6,0},{7,1},{8,14},{9,15},{10,... | collective-permute-start | bytes 786440 | tf_op jit(solution)/shard_map/ppermute | solution.py:482
  11.9 22.6 %collective-permute-start.1 = (bf16[256,512]{1,0:T(8,128)(2,1)S(1)}, bf16[256,512]{1,0:T(8,128)(2,1)S(1)}, u32[]{:S(2)}, u32[]{:S(2)}) collective-permute-start(bf16[256,512]{1,0:T(8,128)(2,1)S(1)} %pad_maximum_fusion.9), channel_id=1, source_target_pairs={{0,4},{1,5},{2,6},{3,7},{4,0},{5,1},{6,2},{7,3},{8,12},{9,13},{10,... | collective-permute-start | bytes 786440 | tf_op jit(solution)/shard_map/ppermute | solution.py:482
  15.1 19.4 %collective-permute-start = (bf16[256,512]{1,0:T(8,128)(2,1)S(1)}, bf16[256,512]{1,0:T(8,128)(2,1)}, u32[]{:S(2)}, u32[]{:S(2)}) collective-permute-start(bf16[256,512]{1,0:T(8,128)(2,1)S(1)} %pad_maximum_fusion.9), channel_id=1, source_target_pairs={{0,2},{1,3},{2,0},{3,1},{4,6},{5,7},{6,4},{7,5},{8,10},{9,11},{10,... | collective-permute-start | bytes 786440 | tf_op jit(solution)/shard_map/ppermute | solution.py:482
  17.1 41.0 %collective-permute-start.8 = (bf16[1280,256]{1,0:T(8,128)(2,1)}, bf16[1280,256]{1,0:T(8,128)(2,1)}, u32[]{:S(2)}, u32[]{:S(2)}) collective-permute-start(bf16[1280,256]{1,0:T(8,128)(2,1)} %slice.126), channel_id=1, source_target_pairs={{0,1},{8,9},{16,17},{24,25}} | collective-permute-start | bytes 1966088 | tf_op jit(solution)/shard_map/ppermute | solution.py:522
  45.9 27.0 %collective-permute-start.5 = (bf16[3,256,256]{2,1,0:T(8,128)(2,1)}, bf16[3,256,256]{2,1,0:T(8,128)(2,1)S(1)}, u32[]{:S(2)}, u32[]{:S(2)}) collective-permute-start(bf16[3,256,256]{2,1,0:T(8,128)(2,1)} %get-tuple-element.91), channel_id=1, source_target_pairs={{0,6},{1,7},{2,4},{3,5},{4,2},{5,3},{6,0},{7,1},{8,14},{9,15},{10,... | collective-permute-start | bytes 1179656 | tf_op jit(solution)/shard_map/ppermute | solution.py:482
  46.0 33.5 %collective-permute-start.4 = (bf16[3,256,256]{2,1,0:T(8,128)(2,1)}, bf16[3,256,256]{2,1,0:T(8,128)(2,1)}, u32[]{:S(2)}, u32[]{:S(2)}) collective-permute-start(bf16[3,256,256]{2,1,0:T(8,128)(2,1)} %get-tuple-element.92), channel_id=1, source_target_pairs={{0,4},{1,5},{2,6},{3,7},{4,0},{5,1},{6,2},{7,3},{8,12},{9,13},{10,... | collective-permute-start | bytes 1179656 | tf_op jit(solution)/shard_map/ppermute | solution.py:482
  49.2 30.3 %collective-permute-start.3 = (bf16[3,256,256]{2,1,0:T(8,128)(2,1)}, bf16[3,256,256]{2,1,0:T(8,128)(2,1)}, u32[]{:S(2)}, u32[]{:S(2)}) collective-permute-start(bf16[3,256,256]{2,1,0:T(8,128)(2,1)} %get-tuple-element.93), channel_id=1, source_target_pairs={{0,2},{1,3},{2,0},{3,1},{4,6},{5,7},{6,4},{7,5},{8,10},{9,11},{10,... | collective-permute-start | bytes 1179656 | tf_op jit(solution)/shard_map/ppermute | solution.py:482
  53.2 58.3 %all-to-all-start.1 = ((bf16[8,5,128,256]{3,2,1,0:T(8,128)(2,1)}), bf16[8,5,128,256]{3,2,1,0:T(8,128)(2,1)S(1)}, u32[]{:S(2)}, u32[]{:S(2)}) async-start(bf16[8,5,128,256]{3,2,1,0:T(8,128)(2,1)} %copy-done.3), calls=%async_computation.1 | async-start | bytes 5242880 | tf_op jit(solution)/shard_map/all_to_all | solution.py:516
  81.8 17.9 %collective-permute-start.9 = (bf16[1280,256]{1,0:T(8,128)(2,1)}, bf16[1280,256]{1,0:T(8,128)(2,1)}, u32[]{:S(2)}, u32[]{:S(2)}) collective-permute-start(bf16[1280,256]{1,0:T(8,128)(2,1)} %fusion.1), channel_id=1, source_target_pairs={{0,4},{1,5},{8,12},{9,13},{16,20},{17,21},{24,28},{25,29}} | collective-permute-start | bytes 1966088 | tf_op jit(solution)/shard_map/ppermute | solution.py:530
  120.8 22.0 %collective-permute-start.11 = (bf16[1280,256]{1,0:T(8,128)(2,1)S(1)}, bf16[1280,256]{1,0:T(8,128)(2,1)S(1)}, u32[]{:S(2)}, u32[]{:S(2)}) collective-permute-start(bf16[1280,256]{1,0:T(8,128)(2,1)S(1)} %broadcast_select_fusion.1), channel_id=1, source_target_pairs={{0,1},{1,0},{2,3},{3,2},{4,5},{5,4},{6,7},{7,6},{8,9},{9,8},{10,11... | collective-permute-start | bytes 1966088 | tf_op jit(solution)/shard_map/ppermute | solution.py:567
  122.4 17.8 %all-to-all-start.2 = ((f32[32,8,128]{2,1,0:T(8,128)}), f32[32,8,128]{2,1,0:T(8,128)S(1)}, u32[]{:S(2)}, u32[]{:S(2)}) async-start(f32[32,8,128]{2,1,0:T(8,128)} %broadcast_in_dim.23), calls=%async_computation.2 | async-start | bytes 262144 | tf_op jit(solution)/shard_map/all_to_all | solution.py:562
  131.2 27.6 %collective-permute-start.14 = (bf16[2,256,256]{2,1,0:T(8,128)(2,1)}, bf16[2,256,256]{2,1,0:T(8,128)(2,1)}, u32[]{:S(2)}, u32[]{:S(2)}) collective-permute-start(bf16[2,256,256]{2,1,0:T(8,128)(2,1)} %get-tuple-element.100), channel_id=1, source_target_pairs={{0,6},{1,7},{2,4},{3,5},{4,2},{5,3},{6,0},{7,1},{8,14},{9,15},{10,... | collective-permute-start | bytes 786440 | tf_op jit(solution)/shard_map/ppermute | solution.py:482
  131.4 27.3 %collective-permute-start.13 = (bf16[2,256,256]{2,1,0:T(8,128)(2,1)}, bf16[2,256,256]{2,1,0:T(8,128)(2,1)}, u32[]{:S(2)}, u32[]{:S(2)}) collective-permute-start(bf16[2,256,256]{2,1,0:T(8,128)(2,1)} %get-tuple-element.101), channel_id=1, source_target_pairs={{0,4},{1,5},{2,6},{3,7},{4,0},{5,1},{6,2},{7,3},{8,12},{9,13},{10,... | collective-permute-start | bytes 786440 | tf_op jit(solution)/shard_map/ppermute | solution.py:482
  134.5 24.2 %collective-permute-start.12 = (bf16[2,256,256]{2,1,0:T(8,128)(2,1)}, bf16[2,256,256]{2,1,0:T(8,128)(2,1)}, u32[]{:S(2)}, u32[]{:S(2)}) collective-permute-start(bf16[2,256,256]{2,1,0:T(8,128)(2,1)} %get-tuple-element.102), channel_id=1, source_target_pairs={{0,2},{1,3},{2,0},{3,1},{4,6},{5,7},{6,4},{7,5},{8,10},{9,11},{10,... | collective-permute-start | bytes 786440 | tf_op jit(solution)/shard_map/ppermute | solution.py:482
  170.1 25.2 %collective-permute-start.23 = (bf16[256,768]{1,0:T(8,128)(2,1)S(1)}, bf16[256,768]{1,0:T(8,128)(2,1)}, u32[]{:S(2)}, u32[]{:S(2)}) collective-permute-start(bf16[256,768]{1,0:T(8,128)(2,1)S(1)} %broadcast_select_fusion.4), channel_id=1, source_target_pairs={{0,8},{16,24},{1,9},{17,25},{2,10},{18,26},{3,11},{19,27},{4,12},{... | collective-permute-start | bytes 1179656 | tf_op jit(solution)/shard_map/ppermute | solution.py:486
  182.5 32.0 %collective-permute-start.24 = (bf16[2,256,512]{2,1,0:T(8,128)(2,1)S(1)}, bf16[2,256,512]{2,1,0:T(8,128)(2,1)S(1)}, u32[]{:S(2)}, u32[]{:S(2)}) collective-permute-start(bf16[2,256,512]{2,1,0:T(8,128)(2,1)S(1)} %get-tuple-element.98), channel_id=1, source_target_pairs={{0,0},{1,1},{2,8},{3,9},{4,16},{5,17},{6,24},{7,25},{8,2},{9,3},{1... | collective-permute-start | bytes 1572872 | tf_op jit(solution)/shard_map/ppermute | solution.py:596
  189.9 27.3 %collective-permute-start.25 = (bf16[2,256,512]{2,1,0:T(8,128)(2,1)S(1)}, bf16[2,256,512]{2,1,0:T(8,128)(2,1)S(1)}, u32[]{:S(2)}, u32[]{:S(2)}) collective-permute-start(bf16[2,256,512]{2,1,0:T(8,128)(2,1)S(1)} %get-tuple-element.97), channel_id=1, source_target_pairs={{16,0},{17,1},{18,8},{19,9},{20,16},{21,17},{22,24},{23,25},{24,2}... | collective-permute-start | bytes 1572872 | tf_op jit(solution)/shard_map/ppermute | solution.py:596
  193.9 20.5 %collective-permute-start.21 = (bf16[256,256]{1,0:T(8,128)(2,1)S(1)}, bf16[256,256]{1,0:T(8,128)(2,1)S(1)}, u32[]{:S(2)}, u32[]{:S(2)}) collective-permute-start(bf16[256,256]{1,0:T(8,128)(2,1)S(1)} %get-tuple-element.90), channel_id=1, source_target_pairs={{1,0},{3,2},{5,4},{7,6},{9,8},{11,10},{13,12},{15,14},{17,16},{19,... | collective-permute-start | bytes 393224 | tf_op jit(solution)/shard_map/ppermute | solution.py:611
  214.5 33.3 %collective-permute-start.30 = (bf16[2,256,256]{2,1,0:T(8,128)(2,1)S(1)}, bf16[2,256,256]{2,1,0:T(8,128)(2,1)S(1)}, u32[]{:S(2)}, u32[]{:S(2)}) collective-permute-start(bf16[2,256,256]{2,1,0:T(8,128)(2,1)S(1)} %pad_maximum_fusion.10), channel_id=1, source_target_pairs={{6,0},{14,8},{22,16},{30,24}} | collective-permute-start | bytes 786440 | tf_op jit(solution)/shard_map/ppermute | solution.py:612
  215.2 32.6 %collective-permute-start.29 = (bf16[2,256,256]{2,1,0:T(8,128)(2,1)S(1)}, bf16[2,256,256]{2,1,0:T(8,128)(2,1)S(1)}, u32[]{:S(2)}, u32[]{:S(2)}) collective-permute-start(bf16[2,256,256]{2,1,0:T(8,128)(2,1)S(1)} %pad_maximum_fusion.10), channel_id=1, source_target_pairs={{4,0},{12,8},{20,16},{28,24}} | collective-permute-start | bytes 786440 | tf_op jit(solution)/shard_map/ppermute | solution.py:612
  217.2 18.5 %collective-permute-start.27 = (bf16[2,256,512]{2,1,0:T(8,128)(2,1)S(1)}, bf16[2,256,512]{2,1,0:T(8,128)(2,1)S(1)}, u32[]{:S(2)}, u32[]{:S(2)}) collective-permute-start(bf16[2,256,512]{2,1,0:T(8,128)(2,1)S(1)} %collective-permute-done.25), channel_id=1, source_target_pairs={{0,1},{1,0},{2,3},{3,2},{4,5},{5,4},{6,7},{7,6},{8,9},{9,8},{10,11... | collective-permute-start | bytes 1572872 | tf_op jit(solution)/shard_map/ppermute | solution.py:597
  218.2 29.6 %collective-permute-start.28 = (bf16[2,256,256]{2,1,0:T(8,128)(2,1)S(1)}, bf16[2,256,256]{2,1,0:T(8,128)(2,1)S(1)}, u32[]{:S(2)}, u32[]{:S(2)}) collective-permute-start(bf16[2,256,256]{2,1,0:T(8,128)(2,1)S(1)} %pad_maximum_fusion.10), channel_id=1, source_target_pairs={{2,0},{10,8},{18,16},{26,24}} | collective-permute-start | bytes 786440 | tf_op jit(solution)/shard_map/ppermute | solution.py:612
  224.4 23.3 %collective-permute-start.32 = (bf16[256,256]{1,0:T(8,128)(2,1)S(1)}, bf16[256,256]{1,0:T(8,128)(2,1)S(1)}, u32[]{:S(2)}, u32[]{:S(2)}) collective-permute-start(bf16[256,256]{1,0:T(8,128)(2,1)S(1)} %broadcast_select_fusion.6), channel_id=1, source_target_pairs={{0,8},{16,24},{1,9},{17,25},{2,10},{18,26},{3,11},{19,27},{4,12},{... | collective-permute-start | bytes 393224 | tf_op jit(solution)/shard_map/ppermute | solution.py:486
  (28 other events, 224.3 us)

commit v5 on v4

--- a/solution.py
+++ b/solution.py
@@ -31,6 +31,22 @@
 nn = ((1,), (0,))
 tn = ((0,), (0,))
 nt = ((1,), (1,))
+
+
+def fold(full):
+    half = full.shape[0] // 2
+    low = full[half:, half:]
+    low = jnp.concatenate([low[: half // 2], low[half // 2 :]], axis=1)
+    return jnp.concatenate([full[:half], low], axis=0)
+
+
+def unfold(packed):
+    half = packed.shape[1] // 2
+    top = packed[:half]
+    low = packed[half:]
+    low = jnp.concatenate([low[:, :half], low[:, half:]], axis=0)
+    low = jnp.concatenate([top[:, half:].T, low], axis=1)
+    return jnp.concatenate([top, low], axis=0)
 
 
 def pack_body(zs, xs, ds, bs, tile, lim_ref, a_ref, o_ref):
@@ -67,9 +83,10 @@
     groups, _, count, bs = x_ref.shape
     cols = x_ref[:, 0].reshape(groups * count, bs)
     lead = l_ref[:, 0].reshape(groups * count, bs)
-    o_ref[0, 0] = dot(cols, cols, tn).astype(bf16)
-    o_ref[0, 1] = dot(lead, cols, tn).astype(bf16)
-    o_ref[0, 2] = dot(lead, lead, tn).astype(bf16)
+    fold_rows = 3 * bs // 4
+    o_ref[0, :fold_rows] = fold(dot(cols, cols, tn)).astype(bf16)
+    o_ref[0, fold_rows : fold_rows + bs] = dot(lead, cols, tn).astype(bf16)
+    o_ref[0, fold_rows + bs :] = fold(dot(lead, lead, tn)).astype(bf16)
 
 
 def raw_moments(ids, owned):
@@ -84,9 +101,9 @@
                 pl.BlockSpec((groups, 1, count, bs), lambda k, ids: (0, ids[0] ^ k, 0, 0)),
                 pl.BlockSpec((groups, 1, count, bs), lambda k, ids: (0, zs, 0, 0)),
             ],
-            out_specs=pl.BlockSpec((1, 3, bs, bs), lambda k, ids: (k, 0, 0, 0)),
+            out_specs=pl.BlockSpec((1, 5 * bs // 2, bs), lambda k, ids: (k, 0, 0)),
         ),
-        out_shape=jax.ShapeDtypeStruct((zs, 3, bs, bs), bf16),
+        out_shape=jax.ShapeDtypeStruct((zs, 5 * bs // 2, bs), bf16),
         cost_estimate=light,
         compiler_params=params("arbitrary"),
         name="raw_moments",
@@ -101,15 +118,19 @@
     total = parts[0][...].astype(f32)
     for part in parts[1:]:
         total = total + part[...].astype(f32)
+    fold_rows = 3 * bs // 4
+    own_raw = unfold(total[:fold_rows])
+    cross_raw = total[fold_rows : fold_rows + bs]
+    lead_raw = unfold(total[fold_rows + bs :])
     fac = fac_ref[0]
     bn = fac[:, :bs].astype(bf16).astype(f32)
     pn = (fac[:, bs:] * keep).astype(bf16).astype(f32)
     mm = functools.partial(dot, precision=highest)
-    t1 = mm(total[0], bn) + mm(total[1], pn, tn)
-    t0 = mm(total[1], bn) + mm(total[2], pn)
+    t1 = mm(own_raw, bn) + mm(cross_raw, pn, tn)
+    t0 = mm(cross_raw, bn) + mm(lead_raw, pn)
     own = (mm(bn, t1, tn) + mm(pn, t0, tn)) * sc_ref[0]
-    h_ref[0] = own.astype(bf16)
-    h_ref[1] = (t0 * sc_ref[0]).astype(bf16)
+    h_ref[:fold_rows] = fold(own).astype(bf16)
+    h_ref[fold_rows:] = (t0 * sc_ref[0]).astype(bf16)
     row = lax.broadcasted_iota(jnp.int32, (bs, bs), 0)
     col = lax.broadcasted_iota(jnp.int32, (bs, bs), 1)
     tr_ref[...] = jnp.zeros_like(tr_ref) + jnp.sum(jnp.where(row == col, own, 0.0))
@@ -124,12 +145,12 @@
             num_scalar_prefetch=1,
             grid=(1,),
             in_specs=[pl.BlockSpec(memory_space=pltpu.SMEM)]
-            + [whole((3, bs, bs)) for _ in parts]
+            + [whole(part.shape) for part in parts]
             + [pl.BlockSpec((1, bs, wide), lambda i, ids: (ids[1], 0, 0))],
-            out_specs=[whole((2, bs, bs)), whole((8, 128))],
+            out_specs=[whole((7 * bs // 4, bs)), whole((8, 128))],
         ),
         out_shape=[
-            jax.ShapeDtypeStruct((2, bs, bs), bf16),
+            jax.ShapeDtypeStruct((7 * bs // 4, bs), bf16),
             jax.ShapeDtypeStruct((8, 128), f32),
         ],
         cost_estimate=light,
@@ -149,8 +170,9 @@
         t_ref[...] = jnp.zeros_like(t_ref)
 
     image = (dot(cols, f_ref[0, :, :bs]) + dot(lead, f_ref[0, :, bs:])).astype(bf16)
-    o_ref[0, 0] = dot(image, image, tn).astype(bf16)
-    o_ref[0, 1] = dot(lead, image, tn).astype(bf16)
+    fold_rows = 3 * bs // 4
+    o_ref[0, :fold_rows] = fold(dot(image, image, tn)).astype(bf16)
+    o_ref[0, fold_rows:] = dot(lead, image, tn).astype(bf16)
     wide = image.astype(f32)
     t_ref[...] = t_ref[...] + jnp.sum(wide * wide)
 
@@ -173,12 +195,12 @@
                 pl.BlockSpec((1, bs, 2 * bs), lambda k, ids: (k, 0, 0)),
             ],
             out_specs=[
-                pl.BlockSpec((1, 2, bs, bs), lambda k, ids: (k, 0, 0, 0)),
+                pl.BlockSpec((1, 7 * bs // 4, bs), lambda k, ids: (k, 0, 0)),
                 pl.BlockSpec((8, 128), lambda k, ids: (0, 0)),
             ],
         ),
         out_shape=[
-            jax.ShapeDtypeStruct((zs, 2, bs, bs), bf16),
+            jax.ShapeDtypeStruct((zs, 7 * bs // 4, bs), bf16),
             jax.ShapeDtypeStruct((8, 128), f32),
         ],
         cost_estimate=light,
@@ -218,8 +240,8 @@
     keep = jnp.where(ids_ref[2] + j > 0, 1.0, 0.0)
     md, ms, new_d, new_s = advance_block(
         width,
-        h_ref[0, 0].astype(f32),
-        dot(lead_ref[...], h_ref[0, 1], tn),
+        unfold(h_ref[0, : 3 * bs // 4].astype(f32)),
+        dot(lead_ref[...], h_ref[0, 3 * bs // 4 :], tn),
         fac_ref[0],
         mom_ref[0],
         lead_ref[...],
@@ -245,7 +267,7 @@
             grid=(blocks,),
             in_specs=[
                 pl.BlockSpec(memory_space=pltpu.SMEM),
-                pl.BlockSpec((1, 2, bs, bs), lambda m, ids: (m, 0, 0, 0)),
+                pl.BlockSpec((1, 7 * bs // 4, bs), lambda m, ids: (m, 0, 0)),
                 spec,
                 spec,
                 pl.BlockSpec((bs, bs), lambda m, ids: (0, 0)),
@@ -609,9 +631,10 @@
         block_sum = block_sum + g.astype(f32)
     block_sum = block_sum.astype(bf16)
     pair = jnp.stack([block_sum, lax.ppermute(block_sum, "fsdp", [(2 * k + 1, 2 * k) for k in range(zs)])])
+    pair = after(pair, *halves)
     gathered = [pair] + [lax.ppermute(pair, "fsdp", [(xs * k, 0)]) for k in range(1, zs)]
     top_lead = jnp.where(s == 0, block_sum, second[:bs, :bs])
-    top_lead = from_group_0(after(top_lead, halves[0]))
+    top_lead = from_group_0(top_lead)
     def sum_to_group_0(value):
         total = value.astype(f32) + lax.ppermute(value, "dp", [(2, 0), (3, 1)]).astype(f32)
         other = lax.ppermute(total.astype(bf16), "dp", [(1, 0)])

time: 271 us -> 262 us (0.967)
  starting transfers between devices: 71.3 us -> 65.5 us
  waiting for transfers between devices: 98.8 us -> 94.4 us
    ppermute x12, waiting for transfers between devices: 29.6 us -> 24 us  [along_z(): return lax.ppermute(value, 'fsdp', pairs)]
    ppermute x2, starting transfers between devices: 10.2 us -> 5.36 us  [sum_to_group_0(): other = lax.ppermute(total.astype(bf16), 'dp', [(1, 0)])]
    ppermute x2, waiting for transfers between devices: 1.53 us -> 5.67 us  [sum_to_group_0(): lax.ppermute(value, 'dp', [(2, 0), (3, 1)]).astype(f32)]
    all_to_all x1, waiting for transfers between devices: 5.74 us -> 1.81 us  [planned(): totals = jnp.sum(lax.all_to_all(sums, both, 0, 0, tiled=True), axis=0)[:, 0]]
    ppermute x2, waiting for transfers between devices: 2.97 us -> 5.82 us  [over_dp(): lax.ppermute(value, 'dp', [(i, i ^ 2) for i in range(ds)])]
    unnamed x27 -> x25, local copies, waits for them, and re-layouts: 9.5 us -> 9.79 us
  transfers between devices with their start and end apart: 40 -> 40, of which waited for: 15 -> 15; matrix products, arithmetic and copies ran while one was open for 11% -> 11% of each run, Pallas kernels for 18% -> 19%
where the time goes in v5:
time: 262 us; the launch traced here: 260 us
  waiting for transfers between devices  94.4 us (36%)
  starting transfers between devices  65.5 us (25%)
  Pallas kernels  51.3 us (20%)
  local copies, waits for them, and re-layouts  21.9 us (8%)
  other arithmetic  21.1 us (8%)
  between operations  5.78 us (2%)
    ppermute x12, waiting for transfers between devices, along_z(): return lax.ppermute(value, 'fsdp', pairs)  24 us
    ppermute x2, waiting for transfers between devices, planned(): lax.ppermute(cb[h * (ds // 2):(h + 1) * (ds // 2)], both, pairs)  18 us
    ppermute x2, waiting for transfers between devices, down_z(): return lax.ppermute(value, 'fsdp', pairs)  16.6 us
    ppermute x2, waiting for transfers between devices, planned(): others = [lax.ppermute(h, 'fsdp', flip_x) for h in halves]  15 us
    ppermute x12, starting transfers between devices, along_z(): return lax.ppermute(value, 'fsdp', pairs)  12.8 us
    pallas_call x2, Pallas kernels, advance_all(): pl.pallas_call(functools.partial(advance_body, width), grid_spec=pltpu.Pr...  11.2 us
    pallas_call x1, Pallas kernels, rows(): pl.pallas_call(rows_body, grid_spec=pltpu.PrefetchScalarGridSpec(num_scal...  10.7 us
    unnamed x25, local copies, waits for them, and re-layouts  9.79 us
  transfers between devices with their start and end apart: 40, of which 15 were waited for; matrix products, arithmetic and copies ran while one was open for 11% of the time, Pallas kernels for 19%

profile of v5, /device:TPU:17, one launch (start us, length us, event | category | flops | bytes accessed | tf_op | source)
XLA Modules:
  0.0 260.0 jit_solution(213855803806547280)
XLA Ops:
  6.2 4.4 %all-to-all-start = ((bf16[8,5,128,256]{3,2,1,0:T(8,128)(2,1)}), bf16[8,5,128,256]{3,2,1,0:T(8,128)(2,1)S(1)}, u32[]{:S(2)}, u32[]{:S(2)}) async-start(bf16[8,5,128,256]{3,2,1,0:T(8,128)(2,1)} %copy-done.4), calls=%async_computation | async-start | bytes 5242880 | tf_op jit(solution)/shard_map/all_to_all | solution.py:538
  12.0 3.2 %collective-permute-start.1 = (bf16[256,512]{1,0:T(8,128)(2,1)S(1)}, bf16[256,512]{1,0:T(8,128)(2,1)S(1)}, u32[]{:S(2)}, u32[]{:S(2)}) collective-permute-start(bf16[256,512]{1,0:T(8,128)(2,1)S(1)} %pad_maximum_fusion.9), channel_id=1, source_target_pairs={{0,4},{1,5},{2,6},{3,7},{4,0},{5,1},{6,2},{7,3},{8,12},{9,13},{10,... | collective-permute-start | bytes 786440 | tf_op jit(solution)/shard_map/ppermute | solution.py:504
  20.6 3.2 %multiply_reduce_fusion = (f32[]{:T(128)}, f32[]{:T(128)}, f32[]{:T(128)}, f32[]{:T(128)}) fusion(f32[4,256,512]{2,1,0:T(8,128)} %fac_ref.3, f32[4]{0:T(128)S(1)} %compare_convert_fusion, f32[4,256,512]{2,1,0:T(8,128)} %fac_ref.2), kind=kLoop, calls=%fused_computation.4 | loop fusion | flops 2621436 | bytes 4194336 | tf_op jit(solution)/shard_map/reduce_sum | solution.py:535
  26.4 4.6 %collective-permute-done.2 = bf16[256,512]{1,0:T(8,128)(2,1)S(1)} collective-permute-done((bf16[256,512]{1,0:T(8,128)(2,1)S(1)}, bf16[256,512]{1,0:T(8,128)(2,1)S(1)}, u32[]{:S(2)}, u32[]{:S(2)}) %collective-permute-start.2) | collective-permute-done | bytes 262176 | tf_op jit(solution)/shard_map/ppermute | solution.py:504
  31.1 3.5 %collective-permute-done.1 = bf16[256,512]{1,0:T(8,128)(2,1)S(1)} collective-permute-done((bf16[256,512]{1,0:T(8,128)(2,1)S(1)}, bf16[256,512]{1,0:T(8,128)(2,1)S(1)}, u32[]{:S(2)}, u32[]{:S(2)}) %collective-permute-start.1) | collective-permute-done | bytes 262176 | tf_op jit(solution)/shard_map/ppermute | solution.py:504
  36.6 4.9 %all-to-all-done.x_ref.l_ref = bf16[8,5,128,256]{3,2,1,0:T(8,128)(2,1)S(1)} async-done(((bf16[8,5,128,256]{3,2,1,0:T(8,128)(2,1)}), bf16[8,5,128,256]{3,2,1,0:T(8,128)(2,1)S(1)}, u32[]{:S(2)}, u32[]{:S(2)}) %all-to-all-start) | async-done | bytes 2621472 | tf_op jit(solution)/shard_map/all_to_all | solution.py:538
  41.5 3.3 %raw_moments.1 = bf16[4,640,256]{2,1,0:T(8,128)(2,1)S(1)} custom-call(s32[5]{0:T(128)S(1)} %stack.70.ids_ref, bf16[8,5,128,256]{3,2,1,0:T(8,128)(2,1)S(1)} %all-to-all-done.x_ref.l_ref, bf16[8,5,128,256]{3,2,1,0:T(8,128)(2,1)S(1)} %all-to-all-done.x_ref.l_ref), custom_call_target="tpu_custom_call" | custom-call | flops 1 | bytes 1 | tf_op jit(solution)/shard_map/raw_moments/pallas_call | solution.py:95
  46.0 3.2 %collective-permute-start.4 = (bf16[640,256]{1,0:T(8,128)(2,1)}, bf16[640,256]{1,0:T(8,128)(2,1)}, u32[]{:S(2)}, u32[]{:S(2)}) collective-permute-start(bf16[640,256]{1,0:T(8,128)(2,1)} %get-tuple-element.94), channel_id=1, source_target_pairs={{0,4},{1,5},{2,6},{3,7},{4,0},{5,1},{6,2},{7,3},{8,12},{9,13},{10,... | collective-permute-start | bytes 983048 | tf_op jit(solution)/shard_map/ppermute | solution.py:504
  53.2 4.9 %all-to-all-start.1 = ((bf16[8,5,128,256]{3,2,1,0:T(8,128)(2,1)}), bf16[8,5,128,256]{3,2,1,0:T(8,128)(2,1)S(1)}, u32[]{:S(2)}, u32[]{:S(2)}) async-start(bf16[8,5,128,256]{3,2,1,0:T(8,128)(2,1)} %copy-done.3), calls=%async_computation.1 | async-start | bytes 5242880 | tf_op jit(solution)/shard_map/all_to_all | solution.py:538
  58.1 10.5 %collective-permute-done.5.refs_3_ = bf16[640,256]{1,0:T(8,128)(2,1)S(1)} collective-permute-done((bf16[640,256]{1,0:T(8,128)(2,1)}, bf16[640,256]{1,0:T(8,128)(2,1)S(1)}, u32[]{:S(2)}, u32[]{:S(2)}) %collective-permute-start.5) | collective-permute-done | bytes 327712 | tf_op jit(solution)/shard_map/ppermute | solution.py:504
  68.6 5.3 %collective-permute-done.4.refs_2_ = bf16[640,256]{1,0:T(8,128)(2,1)} collective-permute-done((bf16[640,256]{1,0:T(8,128)(2,1)}, bf16[640,256]{1,0:T(8,128)(2,1)}, u32[]{:S(2)}, u32[]{:S(2)}) %collective-permute-start.4) | collective-permute-done | bytes 327712 | tf_op jit(solution)/shard_map/ppermute | solution.py:504
  77.4 16.6 %collective-permute-done.9 = bf16[1280,256]{1,0:T(8,128)(2,1)} collective-permute-done((bf16[1280,256]{1,0:T(8,128)(2,1)}, bf16[1280,256]{1,0:T(8,128)(2,1)}, u32[]{:S(2)}, u32[]{:S(2)}) %collective-permute-start.9) | collective-permute-done | bytes 655392 | tf_op jit(solution)/shard_map/ppermute | solution.py:552
  100.5 4.2 %image_stats.1 = (bf16[448,256]{1,0:T(8,128)(2,1)S(1)}, f32[8,128]{1,0:T(8,128)S(1)}) custom-call(s32[5]{0:T(128)S(1)} %stack.70.ids_ref, f32[1]{0:T(128)} %bitcast.4.sc_ref, bf16[640,256]{1,0:T(8,128)(2,1)S(1)} %get-tuple-element.96.refs_0_, bf16[640,256]{1,0:T(8,128)(2,1)} %collective-permute-done.3.refs_1_, ...), custom_call_target="tpu_custom_call" | custom-call | flops 1 | bytes 1 | tf_op jit(solution)/shard_map/image_stats/pallas_call | solution.py:142
  105.9 5.8 %plane_stats.1 = (bf16[4,448,256]{2,1,0:T(8,128)(2,1)S(1)}, f32[8,128]{1,0:T(8,128)S(1)}) custom-call(s32[5]{0:T(128)S(1)} %stack.70.ids_ref, bf16[8,5,128,256]{3,2,1,0:T(8,128)(2,1)S(1)} %all-to-all-done.1.refs_0_.refs_1_, bf16[8,5,128,256]{3,2,1,0:T(8,128)(2,1)S(1)} %all-to-all-done.1.refs_0_.refs_1_, bf16[4,256,512]{2,1,0:T(8,128)(2,1)S(1)} %copy-done.5), custom_call_target="tpu_custom_call" | custom-call | flops 1 | bytes 1 | tf_op jit(solution)/shard_map/plane_stats/pallas_call | solution.py:187
  115.6 6.6 %all-to-all-start.2 = ((f32[32,8,128]{2,1,0:T(8,128)}), f32[32,8,128]{2,1,0:T(8,128)S(1)}, u32[]{:S(2)}, u32[]{:S(2)}) async-start(f32[32,8,128]{2,1,0:T(8,128)} %broadcast_in_dim.23), calls=%async_computation.2 | async-start | bytes 262144 | tf_op jit(solution)/shard_map/all_to_all | solution.py:584
  138.4 5.6 %advance_all.2 = (f32[4,256,512]{2,1,0:T(8,128)}, f32[4,256,512]{2,1,0:T(8,128)}, bf16[4,256,512]{2,1,0:T(8,128)(2,1)S(1)}) custom-call(s32[5]{0:T(128)S(1)} %stack.70.ids_ref, f32[2]{0:T(128)S(1)} %pad_maximum_fusion.11.sc_ref, bf16[4,448,256]{2,1,0:T(8,128)(2,1)S(1)} %pad_maximum_fusion.3.h_ref, f32[4,256,512]{2,1,0:T(8,128)S(1)} %copy-done.1, ...), custom_call_target="tpu_custom_call" | custom-call | flops 1 | bytes 1 | tf_op jit(solution)/shard_map/advance_all/pallas_call | solution.py:263
  144.0 8.6 %column_products.1 = (bf16[2048,1024]{1,0:T(8,128)(2,1)}, bf16[2048,256]{1,0:T(8,128)(2,1)S(1)}) custom-call(s32[5]{0:T(128)S(1)} %stack.70.ids_ref, bf16[2048,1024]{1,0:T(8,128)(2,1)} %g_ref.1, bf16[2048,256]{1,0:T(8,128)(2,1)S(1)} %pad_maximum_fusion.l_ref, bf16[4,256,512]{2,1,0:T(8,128)(2,1)S(1)} %get-tuple-element.57.k_ref), custom_call_target="tpu_custom_call" | custom-call | flops 1 | bytes 1 | tf_op jit(solution)/shard_map/column_products/pallas_call | solution.py:309
  169.9 5.6 %advance_all.3 = (f32[4,256,512]{2,1,0:T(8,128)}, f32[4,256,512]{2,1,0:T(8,128)}, bf16[4,256,512]{2,1,0:T(8,128)(2,1)S(1)}) custom-call(s32[5]{0:T(128)S(1)} %stack.70.ids_ref, f32[2]{0:T(128)S(1)} %pad_maximum_fusion.12.sc_ref, bf16[4,448,256]{2,1,0:T(8,128)(2,1)S(1)} %pad_maximum_fusion.4.h_ref, f32[4,256,512]{2,1,0:T(8,128)S(1)} %copy-done.2, ...), custom_call_target="tpu_custom_call" | custom-call | flops 1 | bytes 1 | tf_op jit(solution)/shard_map/advance_all/pallas_call | solution.py:263
  175.6 6.6 %collective-permute-start.23 = (bf16[2,256,512]{2,1,0:T(8,128)(2,1)S(1)}, bf16[2,256,512]{2,1,0:T(8,128)(2,1)S(1)}, u32[]{:S(2)}, u32[]{:S(2)}) collective-permute-start(bf16[2,256,512]{2,1,0:T(8,128)(2,1)S(1)} %get-tuple-element.97), channel_id=1, source_target_pairs={{16,0},{17,1},{18,8},{19,9},{20,16},{21,17},{22,24},{23,25},{24,2}... | collective-permute-start | bytes 1572872 | tf_op jit(solution)/shard_map/ppermute | solution.py:618
  188.5 15.1 %collective-permute-done.23 = bf16[2,256,512]{2,1,0:T(8,128)(2,1)S(1)} collective-permute-done((bf16[2,256,512]{2,1,0:T(8,128)(2,1)S(1)}, bf16[2,256,512]{2,1,0:T(8,128)(2,1)S(1)}, u32[]{:S(2)}, u32[]{:S(2)}) %collective-permute-start.23) | collective-permute-done | bytes 524320 | tf_op jit(solution)/shard_map/ppermute | solution.py:618
  211.8 15.0 %collective-permute-done.26 = bf16[2,256,512]{2,1,0:T(8,128)(2,1)S(1)} collective-permute-done((bf16[2,256,512]{2,1,0:T(8,128)(2,1)S(1)}, bf16[2,256,512]{2,1,0:T(8,128)(2,1)S(1)}, u32[]{:S(2)}, u32[]{:S(2)}) %collective-permute-start.26) | collective-permute-done | bytes 524320 | tf_op jit(solution)/shard_map/ppermute | solution.py:619
  227.5 10.7 %row_products.1 = (bf16[2048,1024]{1,0:T(8,128)(2,1)}, bf16[256,768]{1,0:T(8,128)(2,1)S(1)}) custom-call(s32[5]{0:T(128)S(1)} %stack.70.ids_ref, bf16[2048,1024]{1,0:T(8,128)(2,1)} %get-tuple-element.66.s_ref, bf16[256,768]{1,0:T(8,128)(2,1)S(1)} %broadcast_select_fusion.5.l_ref, bf16[8,256,512]{2,1,0:T(8,128)(2,1)S(1)} %constant_dynamic-update-slice_fusion.c_ref), custom_call_target="tpu_custom_call" | custom-call | flops 1 | bytes 1 | tf_op jit(solution)/shard_map/row_products/pallas_call | solution.py:374
  239.7 4.2 %lead_row_products.1 = (bf16[2048,1024]{1,0:T(8,128)(2,1)}, bf16[256,256]{1,0:T(8,128)(2,1)S(1)}) custom-call(s32[5]{0:T(128)S(1)} %stack.70.ids_ref, bf16[2048,1024]{1,0:T(8,128)(2,1)} %get-tuple-element.66.s_ref, bf16[2048,256]{1,0:T(8,128)(2,1)S(1)} %bitcast.53, ...), custom_call_target="tpu_custom_call", output_to_operand_aliasing={{0}: (5, {})} | custom-call | flops 1 | bytes 1 | tf_op jit(solution)/shard_map/lead_row_products/pallas_call | solution.py:420
  245.2 5.7 %collective-permute-done.35 = bf16[256,768]{1,0:T(8,128)(2,1)S(1)} collective-permute-done((bf16[256,768]{1,0:T(8,128)(2,1)S(1)}, bf16[256,768]{1,0:T(8,128)(2,1)S(1)}, u32[]{:S(2)}, u32[]{:S(2)}) %collective-permute-start.35) | collective-permute-done | bytes 393248 | tf_op jit(solution)/shard_map/ppermute | solution.py:639
  (142 shorter events, 92.8 us)
Async XLA Ops:
  6.2 35.4 %all-to-all-start = ((bf16[8,5,128,256]{3,2,1,0:T(8,128)(2,1)}), bf16[8,5,128,256]{3,2,1,0:T(8,128)(2,1)S(1)}, u32[]{:S(2)}, u32[]{:S(2)}) async-start(bf16[8,5,128,256]{3,2,1,0:T(8,128)(2,1)} %copy-done.4), calls=%async_computation | async-start | bytes 5242880 | tf_op jit(solution)/shard_map/all_to_all | solution.py:538
  11.8 19.3 %collective-permute-start.2 = (bf16[256,512]{1,0:T(8,128)(2,1)S(1)}, bf16[256,512]{1,0:T(8,128)(2,1)S(1)}, u32[]{:S(2)}, u32[]{:S(2)}) collective-permute-start(bf16[256,512]{1,0:T(8,128)(2,1)S(1)} %pad_maximum_fusion.9), channel_id=1, source_target_pairs={{0,6},{1,7},{2,4},{3,5},{4,2},{5,3},{6,0},{7,1},{8,14},{9,15},{10,... | collective-permute-start | bytes 786440 | tf_op jit(solution)/shard_map/ppermute | solution.py:504
  12.0 22.6 %collective-permute-start.1 = (bf16[256,512]{1,0:T(8,128)(2,1)S(1)}, bf16[256,512]{1,0:T(8,128)(2,1)S(1)}, u32[]{:S(2)}, u32[]{:S(2)}) collective-permute-start(bf16[256,512]{1,0:T(8,128)(2,1)S(1)} %pad_maximum_fusion.9), channel_id=1, source_target_pairs={{0,4},{1,5},{2,6},{3,7},{4,0},{5,1},{6,2},{7,3},{8,12},{9,13},{10,... | collective-permute-start | bytes 786440 | tf_op jit(solution)/shard_map/ppermute | solution.py:504
  15.2 19.4 %collective-permute-start = (bf16[256,512]{1,0:T(8,128)(2,1)S(1)}, bf16[256,512]{1,0:T(8,128)(2,1)}, u32[]{:S(2)}, u32[]{:S(2)}) collective-permute-start(bf16[256,512]{1,0:T(8,128)(2,1)S(1)} %pad_maximum_fusion.9), channel_id=1, source_target_pairs={{0,2},{1,3},{2,0},{3,1},{4,6},{5,7},{6,4},{7,5},{8,10},{9,11},{10,... | collective-permute-start | bytes 786440 | tf_op jit(solution)/shard_map/ppermute | solution.py:504
  17.2 40.9 %collective-permute-start.8 = (bf16[1280,256]{1,0:T(8,128)(2,1)}, bf16[1280,256]{1,0:T(8,128)(2,1)}, u32[]{:S(2)}, u32[]{:S(2)}) collective-permute-start(bf16[1280,256]{1,0:T(8,128)(2,1)} %slice.126), channel_id=1, source_target_pairs={{0,1},{8,9},{16,17},{24,25}} | collective-permute-start | bytes 1966088 | tf_op jit(solution)/shard_map/ppermute | solution.py:544
  45.8 22.8 %collective-permute-start.5 = (bf16[640,256]{1,0:T(8,128)(2,1)}, bf16[640,256]{1,0:T(8,128)(2,1)S(1)}, u32[]{:S(2)}, u32[]{:S(2)}) collective-permute-start(bf16[640,256]{1,0:T(8,128)(2,1)} %get-tuple-element.93), channel_id=1, source_target_pairs={{0,6},{1,7},{2,4},{3,5},{4,2},{5,3},{6,0},{7,1},{8,14},{9,15},{10,... | collective-permute-start | bytes 983048 | tf_op jit(solution)/shard_map/ppermute | solution.py:504
  46.0 27.9 %collective-permute-start.4 = (bf16[640,256]{1,0:T(8,128)(2,1)}, bf16[640,256]{1,0:T(8,128)(2,1)}, u32[]{:S(2)}, u32[]{:S(2)}) collective-permute-start(bf16[640,256]{1,0:T(8,128)(2,1)} %get-tuple-element.94), channel_id=1, source_target_pairs={{0,4},{1,5},{2,6},{3,7},{4,0},{5,1},{6,2},{7,3},{8,12},{9,13},{10,... | collective-permute-start | bytes 983048 | tf_op jit(solution)/shard_map/ppermute | solution.py:504
  49.2 24.7 %collective-permute-start.3 = (bf16[640,256]{1,0:T(8,128)(2,1)}, bf16[640,256]{1,0:T(8,128)(2,1)}, u32[]{:S(2)}, u32[]{:S(2)}) collective-permute-start(bf16[640,256]{1,0:T(8,128)(2,1)} %get-tuple-element.95), channel_id=1, source_target_pairs={{0,2},{1,3},{2,0},{3,1},{4,6},{5,7},{6,4},{7,5},{8,10},{9,11},{10,... | collective-permute-start | bytes 983048 | tf_op jit(solution)/shard_map/ppermute | solution.py:504
  53.2 51.5 %all-to-all-start.1 = ((bf16[8,5,128,256]{3,2,1,0:T(8,128)(2,1)}), bf16[8,5,128,256]{3,2,1,0:T(8,128)(2,1)S(1)}, u32[]{:S(2)}, u32[]{:S(2)}) async-start(bf16[8,5,128,256]{3,2,1,0:T(8,128)(2,1)} %copy-done.3), calls=%async_computation.1 | async-start | bytes 5242880 | tf_op jit(solution)/shard_map/all_to_all | solution.py:538
  76.1 17.9 %collective-permute-start.9 = (bf16[1280,256]{1,0:T(8,128)(2,1)}, bf16[1280,256]{1,0:T(8,128)(2,1)}, u32[]{:S(2)}, u32[]{:S(2)}) collective-permute-start(bf16[1280,256]{1,0:T(8,128)(2,1)} %fusion.1), channel_id=1, source_target_pairs={{0,4},{1,5},{8,12},{9,13},{16,20},{17,21},{24,28},{25,29}} | collective-permute-start | bytes 1966088 | tf_op jit(solution)/shard_map/ppermute | solution.py:552
  114.0 21.4 %collective-permute-start.11 = (bf16[1280,256]{1,0:T(8,128)(2,1)S(1)}, bf16[1280,256]{1,0:T(8,128)(2,1)}, u32[]{:S(2)}, u32[]{:S(2)}) collective-permute-start(bf16[1280,256]{1,0:T(8,128)(2,1)S(1)} %broadcast_select_fusion.1), channel_id=1, source_target_pairs={{0,1},{1,0},{2,3},{3,2},{4,5},{5,4},{6,7},{7,6},{8,9},{9,8},{10,11... | collective-permute-start | bytes 1966088 | tf_op jit(solution)/shard_map/ppermute | solution.py:589
  124.3 28.3 %collective-permute-start.14 = (bf16[448,256]{1,0:T(8,128)(2,1)}, bf16[448,256]{1,0:T(8,128)(2,1)}, u32[]{:S(2)}, u32[]{:S(2)}) collective-permute-start(bf16[448,256]{1,0:T(8,128)(2,1)} %get-tuple-element.100), channel_id=1, source_target_pairs={{0,6},{1,7},{2,4},{3,5},{4,2},{5,3},{6,0},{7,1},{8,14},{9,15},{10,... | collective-permute-start | bytes 688136 | tf_op jit(solution)/shard_map/ppermute | solution.py:504
  124.6 28.0 %collective-permute-start.13 = (bf16[448,256]{1,0:T(8,128)(2,1)}, bf16[448,256]{1,0:T(8,128)(2,1)}, u32[]{:S(2)}, u32[]{:S(2)}) collective-permute-start(bf16[448,256]{1,0:T(8,128)(2,1)} %get-tuple-element.101), channel_id=1, source_target_pairs={{0,4},{1,5},{2,6},{3,7},{4,0},{5,1},{6,2},{7,3},{8,12},{9,13},{10,... | collective-permute-start | bytes 688136 | tf_op jit(solution)/shard_map/ppermute | solution.py:504
  127.7 25.0 %collective-permute-start.12 = (bf16[448,256]{1,0:T(8,128)(2,1)}, bf16[448,256]{1,0:T(8,128)(2,1)}, u32[]{:S(2)}, u32[]{:S(2)}) collective-permute-start(bf16[448,256]{1,0:T(8,128)(2,1)} %get-tuple-element.102), channel_id=1, source_target_pairs={{0,2},{1,3},{2,0},{3,1},{4,6},{5,7},{6,4},{7,5},{8,10},{9,11},{10,... | collective-permute-start | bytes 688136 | tf_op jit(solution)/shard_map/ppermute | solution.py:504
  163.2 24.2 %collective-permute-start.25 = (bf16[256,768]{1,0:T(8,128)(2,1)S(1)}, bf16[256,768]{1,0:T(8,128)(2,1)}, u32[]{:S(2)}, u32[]{:S(2)}) collective-permute-start(bf16[256,768]{1,0:T(8,128)(2,1)S(1)} %broadcast_select_fusion.4), channel_id=1, source_target_pairs={{0,8},{16,24},{1,9},{17,25},{2,10},{18,26},{3,11},{19,27},{4,12},{... | collective-permute-start | bytes 1179656 | tf_op jit(solution)/shard_map/ppermute | solution.py:508
  175.6 28.0 %collective-permute-start.23 = (bf16[2,256,512]{2,1,0:T(8,128)(2,1)S(1)}, bf16[2,256,512]{2,1,0:T(8,128)(2,1)S(1)}, u32[]{:S(2)}, u32[]{:S(2)}) collective-permute-start(bf16[2,256,512]{2,1,0:T(8,128)(2,1)S(1)} %get-tuple-element.97), channel_id=1, source_target_pairs={{16,0},{17,1},{18,8},{19,9},{20,16},{21,17},{22,24},{23,25},{24,2}... | collective-permute-start | bytes 1572872 | tf_op jit(solution)/shard_map/ppermute | solution.py:618
  182.2 24.9 %collective-permute-start.22 = (bf16[2,256,512]{2,1,0:T(8,128)(2,1)S(1)}, bf16[2,256,512]{2,1,0:T(8,128)(2,1)S(1)}, u32[]{:S(2)}, u32[]{:S(2)}) collective-permute-start(bf16[2,256,512]{2,1,0:T(8,128)(2,1)S(1)} %get-tuple-element.98), channel_id=1, source_target_pairs={{0,0},{1,1},{2,8},{3,9},{4,16},{5,17},{6,24},{7,25},{8,2},{9,3},{1... | collective-permute-start | bytes 1572872 | tf_op jit(solution)/shard_map/ppermute | solution.py:618
  185.4 22.9 %collective-permute-start.31 = (bf16[256,256]{1,0:T(8,128)(2,1)S(1)}, bf16[256,256]{1,0:T(8,128)(2,1)S(1)}, u32[]{:S(2)}, u32[]{:S(2)}) collective-permute-start(bf16[256,256]{1,0:T(8,128)(2,1)S(1)} %get-tuple-element.89), channel_id=1, source_target_pairs={{0,16},{1,17},{2,18},{3,19},{4,20},{5,21},{6,22},{7,23}} | collective-permute-start | bytes 393224 | tf_op jit(solution)/shard_map/ppermute | solution.py:507
  186.1 23.5 %collective-permute-start.21 = (bf16[256,256]{1,0:T(8,128)(2,1)S(1)}, bf16[256,256]{1,0:T(8,128)(2,1)S(1)}, u32[]{:S(2)}, u32[]{:S(2)}) collective-permute-start(bf16[256,256]{1,0:T(8,128)(2,1)S(1)} %get-tuple-element.90), channel_id=1, source_target_pairs={{1,0},{3,2},{5,4},{7,6},{9,8},{11,10},{13,12},{15,14},{17,16},{19,... | collective-permute-start | bytes 393224 | tf_op jit(solution)/shard_map/ppermute | solution.py:633
  203.6 23.9 %collective-permute-start.27 = (bf16[2,256,512]{2,1,0:T(8,128)(2,1)S(1)}, bf16[2,256,512]{2,1,0:T(8,128)(2,1)S(1)}, u32[]{:S(2)}, u32[]{:S(2)}) collective-permute-start(bf16[2,256,512]{2,1,0:T(8,128)(2,1)S(1)} %collective-permute-done.23), channel_id=1, source_target_pairs={{0,1},{1,0},{2,3},{3,2},{4,5},{5,4},{6,7},{7,6},{8,9},{9,8},{10,11... | collective-permute-start | bytes 1572872 | tf_op jit(solution)/shard_map/ppermute | solution.py:619
  207.1 19.6 %collective-permute-start.26 = (bf16[2,256,512]{2,1,0:T(8,128)(2,1)S(1)}, bf16[2,256,512]{2,1,0:T(8,128)(2,1)S(1)}, u32[]{:S(2)}, u32[]{:S(2)}) collective-permute-start(bf16[2,256,512]{2,1,0:T(8,128)(2,1)S(1)} %collective-permute-done.22), channel_id=1, source_target_pairs={{0,1},{1,0},{2,3},{3,2},{4,5},{5,4},{6,7},{7,6},{8,9},{9,8},{10,11... | collective-permute-start | bytes 1572872 | tf_op jit(solution)/shard_map/ppermute | solution.py:619
  208.4 31.2 %collective-permute-start.32 = (bf16[256,256]{1,0:T(8,128)(2,1)S(1)}, bf16[256,256]{1,0:T(8,128)(2,1)S(1)}, u32[]{:S(2)}, u32[]{:S(2)}) collective-permute-start(bf16[256,256]{1,0:T(8,128)(2,1)S(1)} %broadcast_select_fusion.6), channel_id=1, source_target_pairs={{0,8},{16,24},{1,9},{17,25},{2,10},{18,26},{3,11},{19,27},{4,12},{... | collective-permute-start | bytes 393224 | tf_op jit(solution)/shard_map/ppermute | solution.py:508
  209.7 29.9 %collective-permute-start.30 = (bf16[2,256,256]{2,1,0:T(8,128)(2,1)S(1)}, bf16[2,256,256]{2,1,0:T(8,128)(2,1)S(1)}, u32[]{:S(2)}, u32[]{:S(2)}) collective-permute-start(bf16[2,256,256]{2,1,0:T(8,128)(2,1)S(1)} %pad_maximum_fusion.10), channel_id=1, source_target_pairs={{6,0},{14,8},{22,16},{30,24}} | collective-permute-start | bytes 786440 | tf_op jit(solution)/shard_map/ppermute | solution.py:635
  210.4 29.2 %collective-permute-start.29 = (bf16[2,256,256]{2,1,0:T(8,128)(2,1)S(1)}, bf16[2,256,256]{2,1,0:T(8,128)(2,1)S(1)}, u32[]{:S(2)}, u32[]{:S(2)}) collective-permute-start(bf16[2,256,256]{2,1,0:T(8,128)(2,1)S(1)} %pad_maximum_fusion.10), channel_id=1, source_target_pairs={{4,0},{12,8},{20,16},{28,24}} | collective-permute-start | bytes 786440 | tf_op jit(solution)/shard_map/ppermute | solution.py:635
  (27 other events, 230.3 us)

commit v6 on v5

--- a/solution.py
+++ b/solution.py
@@ -146,7 +146,7 @@
             grid=(1,),
             in_specs=[pl.BlockSpec(memory_space=pltpu.SMEM)]
             + [whole(part.shape) for part in parts]
-            + [pl.BlockSpec((1, bs, wide), lambda i, ids: (ids[1], 0, 0))],
+            + [pl.BlockSpec((1, bs, wide), lambda i, ids: (0, 0, 0))],
             out_specs=[whole((7 * bs // 4, bs)), whole((8, 128))],
         ),
         out_shape=[
@@ -553,11 +553,12 @@
 
     owned_k = exchange(pack(limit, acts, zs, xs, ds, bs))
     blocks_c = block_along_z(c_factor)
+    own_k = lax.dynamic_slice_in_dim(k_factor, d, 1, 0)
     packed_c = pack(limit, out_grads, zs, xs, ds, bs)
     gram_k = gram_part(k_factor)
     gram_c = gram_part(c_factor)
-    packed_c, owned_k, blocks_c, gram_k, gram_c = lax.optimization_barrier(
-        (packed_c, owned_k, blocks_c, gram_k, gram_c)
+    packed_c, owned_k, blocks_c, own_k, gram_k, gram_c = lax.optimization_barrier(
+        (packed_c, owned_k, blocks_c, own_k, gram_k, gram_c)
     )
     owned_c = exchange(packed_c)
 
@@ -571,7 +572,7 @@
         stride //= 2
     last_z = down_z(mine, 1)
 
-    stat_k, trace_k = image_stats(ids, stat_scalars, sent_k, k_factor)
+    stat_k, trace_k = image_stats(ids, stat_scalars, sent_k, own_k)
     partial_c, square_c = stats(ids, after(owned_c, trace_k), blocks_c)
     rows8 = lax.broadcasted_iota(jnp.int32, (8, 128), 0)
     sums = jnp.where(
@@ -631,7 +632,7 @@
         block_sum = block_sum + g.astype(f32)
     block_sum = block_sum.astype(bf16)
     pair = jnp.stack([block_sum, lax.ppermute(block_sum, "fsdp", [(2 * k + 1, 2 * k) for k in range(zs)])])
-    pair = after(pair, *halves)
+    pair = after(pair, halves[0])
     gathered = [pair] + [lax.ppermute(pair, "fsdp", [(xs * k, 0)]) for k in range(1, zs)]
     top_lead = jnp.where(s == 0, block_sum, second[:bs, :bs])
     top_lead = from_group_0(top_lead)

time: 262 us -> 260 us (level)
  waiting for transfers between devices: 94.4 us -> 89.3 us
  starting transfers between devices: 65.5 us -> 69.2 us
  transfers between devices with their start and end apart: 40 -> 40, of which waited for: 15 -> 15; matrix products, arithmetic and copies ran while one was open for 11% -> 12% of each run, Pallas kernels for 19% -> 19%
where the time goes in v6:
time: 260 us; the launch traced here: 258 us
  waiting for transfers between devices  89.3 us (34%)
  starting transfers between devices  69.2 us (27%)
  Pallas kernels  51.4 us (20%)
  other arithmetic  21.5 us (8%)
  local copies, waits for them, and re-layouts  21.2 us (8%)
  between operations  5.82 us (2%)
    ppermute x12, waiting for transfers between devices, along_z(): return lax.ppermute(value, 'fsdp', pairs)  22.8 us
    ppermute x2, waiting for transfers between devices, planned(): lax.ppermute(cb[h * (ds // 2):(h + 1) * (ds // 2)], both, pairs)  17.2 us
    ppermute x2, waiting for transfers between devices, down_z(): return lax.ppermute(value, 'fsdp', pairs)  16.6 us
    ppermute x2, waiting for transfers between devices, planned(): others = [lax.ppermute(h, 'fsdp', flip_x) for h in halves]  13.9 us
    ppermute x12, starting transfers between devices, along_z(): return lax.ppermute(value, 'fsdp', pairs)  13.5 us
    pallas_call x2, Pallas kernels, advance_all(): pl.pallas_call(functools.partial(advance_body, width), grid_spec=pltpu.Pr...  11.2 us
    pallas_call x1, Pallas kernels, rows(): pl.pallas_call(rows_body, grid_spec=pltpu.PrefetchScalarGridSpec(num_scal...  10.7 us
    all_to_all x2, starting transfers between devices, exchange(): lax.all_to_all(packed, both, 0, 0, tiled=True, axis_index_groups=plane)  9.3 us
  transfers between devices with their start and end apart: 40, of which 15 were waited for; matrix products, arithmetic and copies ran while one was open for 12% of the time, Pallas kernels for 19%

profile of v6, /device:TPU:17, one launch (start us, length us, event | category | flops | bytes accessed | tf_op | source)
XLA Modules:
  0.0 258.5 jit_solution(13277713029205989458)
XLA Ops:
  6.1 4.4 %all-to-all-start = ((bf16[8,5,128,256]{3,2,1,0:T(8,128)(2,1)}), bf16[8,5,128,256]{3,2,1,0:T(8,128)(2,1)S(1)}, u32[]{:S(2)}, u32[]{:S(2)}) async-start(bf16[8,5,128,256]{3,2,1,0:T(8,128)(2,1)} %copy-done.3), calls=%async_computation | async-start | bytes 5242880 | tf_op jit(solution)/shard_map/all_to_all | solution.py:538
  20.6 3.2 %multiply_reduce_fusion = (f32[]{:T(128)}, f32[]{:T(128)}, f32[]{:T(128)}, f32[]{:T(128)}) fusion(f32[4,256,512]{2,1,0:T(8,128)} %fac_ref.3, f32[4]{0:T(128)S(1)} %compare_convert_fusion, f32[4,256,512]{2,1,0:T(8,128)} %fac_ref.2), kind=kLoop, calls=%fused_computation.4 | loop fusion | flops 2621436 | bytes 4194336 | tf_op jit(solution)/shard_map/reduce_sum | solution.py:535
  27.6 3.5 %collective-permute-done.2 = bf16[256,512]{1,0:T(8,128)(2,1)} collective-permute-done((bf16[256,512]{1,0:T(8,128)(2,1)S(1)}, bf16[256,512]{1,0:T(8,128)(2,1)}, u32[]{:S(2)}, u32[]{:S(2)}) %collective-permute-start.2) | collective-permute-done | bytes 262176 | tf_op jit(solution)/shard_map/ppermute | solution.py:504
  31.1 3.5 %collective-permute-done.1 = bf16[256,512]{1,0:T(8,128)(2,1)} collective-permute-done((bf16[256,512]{1,0:T(8,128)(2,1)S(1)}, bf16[256,512]{1,0:T(8,128)(2,1)}, u32[]{:S(2)}, u32[]{:S(2)}) %collective-permute-start.1) | collective-permute-done | bytes 262176 | tf_op jit(solution)/shard_map/ppermute | solution.py:504
  36.7 4.7 %all-to-all-done.x_ref.l_ref = bf16[8,5,128,256]{3,2,1,0:T(8,128)(2,1)S(1)} async-done(((bf16[8,5,128,256]{3,2,1,0:T(8,128)(2,1)}), bf16[8,5,128,256]{3,2,1,0:T(8,128)(2,1)S(1)}, u32[]{:S(2)}, u32[]{:S(2)}) %all-to-all-start) | async-done | bytes 2621472 | tf_op jit(solution)/shard_map/all_to_all | solution.py:538
  41.5 3.3 %raw_moments.1 = bf16[4,640,256]{2,1,0:T(8,128)(2,1)S(1)} custom-call(s32[5]{0:T(128)S(1)} %stack.70.ids_ref, bf16[8,5,128,256]{3,2,1,0:T(8,128)(2,1)S(1)} %all-to-all-done.x_ref.l_ref, bf16[8,5,128,256]{3,2,1,0:T(8,128)(2,1)S(1)} %all-to-all-done.x_ref.l_ref), custom_call_target="tpu_custom_call" | custom-call | flops 1 | bytes 1 | tf_op jit(solution)/shard_map/raw_moments/pallas_call | solution.py:95
  45.9 3.2 %collective-permute-start.4 = (bf16[640,256]{1,0:T(8,128)(2,1)}, bf16[640,256]{1,0:T(8,128)(2,1)}, u32[]{:S(2)}, u32[]{:S(2)}) collective-permute-start(bf16[640,256]{1,0:T(8,128)(2,1)} %get-tuple-element.96), channel_id=1, source_target_pairs={{0,4},{1,5},{2,6},{3,7},{4,0},{5,1},{6,2},{7,3},{8,12},{9,13},{10,... | collective-permute-start | bytes 983048 | tf_op jit(solution)/shard_map/ppermute | solution.py:504
  53.2 4.9 %all-to-all-start.1 = ((bf16[8,5,128,256]{3,2,1,0:T(8,128)(2,1)}), bf16[8,5,128,256]{3,2,1,0:T(8,128)(2,1)S(1)}, u32[]{:S(2)}, u32[]{:S(2)}) async-start(bf16[8,5,128,256]{3,2,1,0:T(8,128)(2,1)} %copy-done.2), calls=%async_computation.1 | async-start | bytes 5242880 | tf_op jit(solution)/shard_map/all_to_all | solution.py:538
  58.1 10.4 %collective-permute-done.5.refs_3_ = bf16[640,256]{1,0:T(8,128)(2,1)} collective-permute-done((bf16[640,256]{1,0:T(8,128)(2,1)}, bf16[640,256]{1,0:T(8,128)(2,1)}, u32[]{:S(2)}, u32[]{:S(2)}) %collective-permute-start.5) | collective-permute-done | bytes 327712 | tf_op jit(solution)/shard_map/ppermute | solution.py:504
  68.5 5.3 %collective-permute-done.4.refs_2_ = bf16[640,256]{1,0:T(8,128)(2,1)} collective-permute-done((bf16[640,256]{1,0:T(8,128)(2,1)}, bf16[640,256]{1,0:T(8,128)(2,1)}, u32[]{:S(2)}, u32[]{:S(2)}) %collective-permute-start.4) | collective-permute-done | bytes 327712 | tf_op jit(solution)/shard_map/ppermute | solution.py:504
  77.4 16.6 %collective-permute-done.9 = bf16[1280,256]{1,0:T(8,128)(2,1)} collective-permute-done((bf16[1280,256]{1,0:T(8,128)(2,1)}, bf16[1280,256]{1,0:T(8,128)(2,1)}, u32[]{:S(2)}, u32[]{:S(2)}) %collective-permute-start.9) | collective-permute-done | bytes 655392 | tf_op jit(solution)/shard_map/ppermute | solution.py:552
  99.4 4.3 %image_stats.1 = (bf16[448,256]{1,0:T(8,128)(2,1)S(1)}, f32[8,128]{1,0:T(8,128)S(1)}) custom-call(s32[5]{0:T(128)S(1)} %stack.70.ids_ref, f32[1]{0:T(128)} %bitcast.4.sc_ref, bf16[640,256]{1,0:T(8,128)(2,1)S(1)} %get-tuple-element.98.refs_0_, bf16[640,256]{1,0:T(8,128)(2,1)} %collective-permute-done.3.refs_1_, ...), custom_call_target="tpu_custom_call" | custom-call | flops 1 | bytes 1 | tf_op jit(solution)/shard_map/image_stats/pallas_call | solution.py:142
  105.6 5.8 %plane_stats.1 = (bf16[4,448,256]{2,1,0:T(8,128)(2,1)S(1)}, f32[8,128]{1,0:T(8,128)S(1)}) custom-call(s32[5]{0:T(128)S(1)} %stack.70.ids_ref, bf16[8,5,128,256]{3,2,1,0:T(8,128)(2,1)S(1)} %all-to-all-done.1.refs_0_.refs_1_, bf16[8,5,128,256]{3,2,1,0:T(8,128)(2,1)S(1)} %all-to-all-done.1.refs_0_.refs_1_, bf16[4,256,512]{2,1,0:T(8,128)(2,1)S(1)} %copy-done.4), custom_call_target="tpu_custom_call" | custom-call | flops 1 | bytes 1 | tf_op jit(solution)/shard_map/plane_stats/pallas_call | solution.py:187
  114.3 7.7 %all-to-all-start.2 = ((f32[32,8,128]{2,1,0:T(8,128)}), f32[32,8,128]{2,1,0:T(8,128)S(1)}, u32[]{:S(2)}, u32[]{:S(2)}) async-start(f32[32,8,128]{2,1,0:T(8,128)} %broadcast_in_dim.23), calls=%async_computation.2 | async-start | bytes 262144 | tf_op jit(solution)/shard_map/all_to_all | solution.py:585
  136.9 5.6 %advance_all.2 = (f32[4,256,512]{2,1,0:T(8,128)}, f32[4,256,512]{2,1,0:T(8,128)}, bf16[4,256,512]{2,1,0:T(8,128)(2,1)S(1)}) custom-call(s32[5]{0:T(128)S(1)} %stack.70.ids_ref, f32[2]{0:T(128)S(1)} %pad_maximum_fusion.11.sc_ref, bf16[4,448,256]{2,1,0:T(8,128)(2,1)S(1)} %pad_maximum_fusion.3.h_ref, f32[4,256,512]{2,1,0:T(8,128)S(1)} %copy-done, ...), custom_call_target="tpu_custom_call" | custom-call | flops 1 | bytes 1 | tf_op jit(solution)/shard_map/advance_all/pallas_call | solution.py:263
  142.5 8.6 %column_products.1 = (bf16[2048,1024]{1,0:T(8,128)(2,1)}, bf16[2048,256]{1,0:T(8,128)(2,1)S(1)}) custom-call(s32[5]{0:T(128)S(1)} %stack.70.ids_ref, bf16[2048,1024]{1,0:T(8,128)(2,1)} %g_ref.1, bf16[2048,256]{1,0:T(8,128)(2,1)S(1)} %pad_maximum_fusion.l_ref, bf16[4,256,512]{2,1,0:T(8,128)(2,1)S(1)} %get-tuple-element.59.k_ref), custom_call_target="tpu_custom_call" | custom-call | flops 1 | bytes 1 | tf_op jit(solution)/shard_map/column_products/pallas_call | solution.py:309
  169.0 5.6 %advance_all.3 = (f32[4,256,512]{2,1,0:T(8,128)}, f32[4,256,512]{2,1,0:T(8,128)}, bf16[4,256,512]{2,1,0:T(8,128)(2,1)S(1)}) custom-call(s32[5]{0:T(128)S(1)} %stack.70.ids_ref, f32[2]{0:T(128)S(1)} %pad_maximum_fusion.12.sc_ref, bf16[4,448,256]{2,1,0:T(8,128)(2,1)S(1)} %pad_maximum_fusion.4.h_ref, f32[4,256,512]{2,1,0:T(8,128)S(1)} %copy-done.1, ...), custom_call_target="tpu_custom_call" | custom-call | flops 1 | bytes 1 | tf_op jit(solution)/shard_map/advance_all/pallas_call | solution.py:263
  174.7 7.1 %collective-permute-start.25 = (bf16[2,256,512]{2,1,0:T(8,128)(2,1)S(1)}, bf16[2,256,512]{2,1,0:T(8,128)(2,1)S(1)}, u32[]{:S(2)}, u32[]{:S(2)}) collective-permute-start(bf16[2,256,512]{2,1,0:T(8,128)(2,1)S(1)} %get-tuple-element.99), channel_id=1, source_target_pairs={{16,0},{17,1},{18,8},{19,9},{20,16},{21,17},{22,24},{23,25},{24,2}... | collective-permute-start | bytes 1572872 | tf_op jit(solution)/shard_map/ppermute | solution.py:619
  187.7 14.7 %collective-permute-done.25 = bf16[2,256,512]{2,1,0:T(8,128)(2,1)S(1)} collective-permute-done((bf16[2,256,512]{2,1,0:T(8,128)(2,1)S(1)}, bf16[2,256,512]{2,1,0:T(8,128)(2,1)S(1)}, u32[]{:S(2)}, u32[]{:S(2)}) %collective-permute-start.25) | collective-permute-done | bytes 524320 | tf_op jit(solution)/shard_map/ppermute | solution.py:619
  211.3 13.9 %collective-permute-done.26 = bf16[2,256,512]{2,1,0:T(8,128)(2,1)S(1)} collective-permute-done((bf16[2,256,512]{2,1,0:T(8,128)(2,1)S(1)}, bf16[2,256,512]{2,1,0:T(8,128)(2,1)S(1)}, u32[]{:S(2)}, u32[]{:S(2)}) %collective-permute-start.26) | collective-permute-done | bytes 524320 | tf_op jit(solution)/shard_map/ppermute | solution.py:620
  226.0 10.7 %row_products.1 = (bf16[2048,1024]{1,0:T(8,128)(2,1)}, bf16[256,768]{1,0:T(8,128)(2,1)S(1)}) custom-call(s32[5]{0:T(128)S(1)} %stack.70.ids_ref, bf16[2048,1024]{1,0:T(8,128)(2,1)} %get-tuple-element.68.s_ref, bf16[256,768]{1,0:T(8,128)(2,1)S(1)} %broadcast_select_fusion.5.l_ref, bf16[8,256,512]{2,1,0:T(8,128)(2,1)S(1)} %constant_dynamic-update-slice_fusion.c_ref), custom_call_target="tpu_custom_call" | custom-call | flops 1 | bytes 1 | tf_op jit(solution)/shard_map/row_products/pallas_call | solution.py:374
  238.2 4.2 %lead_row_products.1 = (bf16[2048,1024]{1,0:T(8,128)(2,1)}, bf16[256,256]{1,0:T(8,128)(2,1)S(1)}) custom-call(s32[5]{0:T(128)S(1)} %stack.70.ids_ref, bf16[2048,1024]{1,0:T(8,128)(2,1)} %get-tuple-element.68.s_ref, bf16[2048,256]{1,0:T(8,128)(2,1)S(1)} %bitcast.53, ...), custom_call_target="tpu_custom_call", output_to_operand_aliasing={{0}: (5, {})} | custom-call | flops 1 | bytes 1 | tf_op jit(solution)/shard_map/lead_row_products/pallas_call | solution.py:420
  243.7 5.6 %collective-permute-done.35 = bf16[256,768]{1,0:T(8,128)(2,1)S(1)} collective-permute-done((bf16[256,768]{1,0:T(8,128)(2,1)S(1)}, bf16[256,768]{1,0:T(8,128)(2,1)S(1)}, u32[]{:S(2)}, u32[]{:S(2)}) %collective-permute-start.35) | collective-permute-done | bytes 393248 | tf_op jit(solution)/shard_map/ppermute | solution.py:640
  249.3 3.3 %collective-permute-start.36 = (bf16[256,768]{1,0:T(8,128)(2,1)S(1)}, bf16[256,768]{1,0:T(8,128)(2,1)S(1)}, u32[]{:S(2)}, u32[]{:S(2)}) collective-permute-start(bf16[256,768]{1,0:T(8,128)(2,1)S(1)} %fusion), channel_id=1, source_target_pairs={{8,0},{9,1},{10,2},{11,3},{12,4},{13,5},{14,6},{15,7}} | collective-permute-start | bytes 1179656 | tf_op jit(solution)/shard_map/ppermute | solution.py:641
  (143 shorter events, 92.5 us)
Async XLA Ops:
  6.1 35.4 %all-to-all-start = ((bf16[8,5,128,256]{3,2,1,0:T(8,128)(2,1)}), bf16[8,5,128,256]{3,2,1,0:T(8,128)(2,1)S(1)}, u32[]{:S(2)}, u32[]{:S(2)}) async-start(bf16[8,5,128,256]{3,2,1,0:T(8,128)(2,1)} %copy-done.3), calls=%async_computation | async-start | bytes 5242880 | tf_op jit(solution)/shard_map/all_to_all | solution.py:538
  11.7 19.3 %collective-permute-start.2 = (bf16[256,512]{1,0:T(8,128)(2,1)S(1)}, bf16[256,512]{1,0:T(8,128)(2,1)}, u32[]{:S(2)}, u32[]{:S(2)}) collective-permute-start(bf16[256,512]{1,0:T(8,128)(2,1)S(1)} %pad_maximum_fusion.9), channel_id=1, source_target_pairs={{0,6},{1,7},{2,4},{3,5},{4,2},{5,3},{6,0},{7,1},{8,14},{9,15},{10,... | collective-permute-start | bytes 786440 | tf_op jit(solution)/shard_map/ppermute | solution.py:504
  11.9 22.6 %collective-permute-start.1 = (bf16[256,512]{1,0:T(8,128)(2,1)S(1)}, bf16[256,512]{1,0:T(8,128)(2,1)}, u32[]{:S(2)}, u32[]{:S(2)}) collective-permute-start(bf16[256,512]{1,0:T(8,128)(2,1)S(1)} %pad_maximum_fusion.9), channel_id=1, source_target_pairs={{0,4},{1,5},{2,6},{3,7},{4,0},{5,1},{6,2},{7,3},{8,12},{9,13},{10,... | collective-permute-start | bytes 786440 | tf_op jit(solution)/shard_map/ppermute | solution.py:504
  15.2 19.4 %collective-permute-start = (bf16[256,512]{1,0:T(8,128)(2,1)S(1)}, bf16[256,512]{1,0:T(8,128)(2,1)}, u32[]{:S(2)}, u32[]{:S(2)}) collective-permute-start(bf16[256,512]{1,0:T(8,128)(2,1)S(1)} %pad_maximum_fusion.9), channel_id=1, source_target_pairs={{0,2},{1,3},{2,0},{3,1},{4,6},{5,7},{6,4},{7,5},{8,10},{9,11},{10,... | collective-permute-start | bytes 786440 | tf_op jit(solution)/shard_map/ppermute | solution.py:504
  17.1 41.0 %collective-permute-start.8 = (bf16[1280,256]{1,0:T(8,128)(2,1)}, bf16[1280,256]{1,0:T(8,128)(2,1)}, u32[]{:S(2)}, u32[]{:S(2)}) collective-permute-start(bf16[1280,256]{1,0:T(8,128)(2,1)} %slice.126), channel_id=1, source_target_pairs={{0,1},{8,9},{16,17},{24,25}} | collective-permute-start | bytes 1966088 | tf_op jit(solution)/shard_map/ppermute | solution.py:544
  45.8 22.8 %collective-permute-start.5 = (bf16[640,256]{1,0:T(8,128)(2,1)}, bf16[640,256]{1,0:T(8,128)(2,1)}, u32[]{:S(2)}, u32[]{:S(2)}) collective-permute-start(bf16[640,256]{1,0:T(8,128)(2,1)} %get-tuple-element.95), channel_id=1, source_target_pairs={{0,6},{1,7},{2,4},{3,5},{4,2},{5,3},{6,0},{7,1},{8,14},{9,15},{10,... | collective-permute-start | bytes 983048 | tf_op jit(solution)/shard_map/ppermute | solution.py:504
  45.9 27.9 %collective-permute-start.4 = (bf16[640,256]{1,0:T(8,128)(2,1)}, bf16[640,256]{1,0:T(8,128)(2,1)}, u32[]{:S(2)}, u32[]{:S(2)}) collective-permute-start(bf16[640,256]{1,0:T(8,128)(2,1)} %get-tuple-element.96), channel_id=1, source_target_pairs={{0,4},{1,5},{2,6},{3,7},{4,0},{5,1},{6,2},{7,3},{8,12},{9,13},{10,... | collective-permute-start | bytes 983048 | tf_op jit(solution)/shard_map/ppermute | solution.py:504
  49.2 24.7 %collective-permute-start.3 = (bf16[640,256]{1,0:T(8,128)(2,1)}, bf16[640,256]{1,0:T(8,128)(2,1)}, u32[]{:S(2)}, u32[]{:S(2)}) collective-permute-start(bf16[640,256]{1,0:T(8,128)(2,1)} %get-tuple-element.97), channel_id=1, source_target_pairs={{0,2},{1,3},{2,0},{3,1},{4,6},{5,7},{6,4},{7,5},{8,10},{9,11},{10,... | collective-permute-start | bytes 983048 | tf_op jit(solution)/shard_map/ppermute | solution.py:504
  53.2 51.2 %all-to-all-start.1 = ((bf16[8,5,128,256]{3,2,1,0:T(8,128)(2,1)}), bf16[8,5,128,256]{3,2,1,0:T(8,128)(2,1)S(1)}, u32[]{:S(2)}, u32[]{:S(2)}) async-start(bf16[8,5,128,256]{3,2,1,0:T(8,128)(2,1)} %copy-done.2), calls=%async_computation.1 | async-start | bytes 5242880 | tf_op jit(solution)/shard_map/all_to_all | solution.py:538
  76.1 17.9 %collective-permute-start.9 = (bf16[1280,256]{1,0:T(8,128)(2,1)}, bf16[1280,256]{1,0:T(8,128)(2,1)}, u32[]{:S(2)}, u32[]{:S(2)}) collective-permute-start(bf16[1280,256]{1,0:T(8,128)(2,1)} %fusion.1), channel_id=1, source_target_pairs={{0,4},{1,5},{8,12},{9,13},{16,20},{17,21},{24,28},{25,29}} | collective-permute-start | bytes 1966088 | tf_op jit(solution)/shard_map/ppermute | solution.py:552
  112.7 21.5 %collective-permute-start.11 = (bf16[1280,256]{1,0:T(8,128)(2,1)S(1)}, bf16[1280,256]{1,0:T(8,128)(2,1)}, u32[]{:S(2)}, u32[]{:S(2)}) collective-permute-start(bf16[1280,256]{1,0:T(8,128)(2,1)S(1)} %broadcast_select_fusion.1), channel_id=1, source_target_pairs={{0,1},{1,0},{2,3},{3,2},{4,5},{5,4},{6,7},{7,6},{8,9},{9,8},{10,11... | collective-permute-start | bytes 1966088 | tf_op jit(solution)/shard_map/ppermute | solution.py:590
  124.1 27.1 %collective-permute-start.14 = (bf16[448,256]{1,0:T(8,128)(2,1)}, bf16[448,256]{1,0:T(8,128)(2,1)S(1)}, u32[]{:S(2)}, u32[]{:S(2)}) collective-permute-start(bf16[448,256]{1,0:T(8,128)(2,1)} %get-tuple-element.102), channel_id=1, source_target_pairs={{0,6},{1,7},{2,4},{3,5},{4,2},{5,3},{6,0},{7,1},{8,14},{9,15},{10,... | collective-permute-start | bytes 688136 | tf_op jit(solution)/shard_map/ppermute | solution.py:504
  124.3 26.8 %collective-permute-start.13 = (bf16[448,256]{1,0:T(8,128)(2,1)}, bf16[448,256]{1,0:T(8,128)(2,1)}, u32[]{:S(2)}, u32[]{:S(2)}) collective-permute-start(bf16[448,256]{1,0:T(8,128)(2,1)} %get-tuple-element.103), channel_id=1, source_target_pairs={{0,4},{1,5},{2,6},{3,7},{4,0},{5,1},{6,2},{7,3},{8,12},{9,13},{10,... | collective-permute-start | bytes 688136 | tf_op jit(solution)/shard_map/ppermute | solution.py:504
  127.4 23.7 %collective-permute-start.12 = (bf16[448,256]{1,0:T(8,128)(2,1)}, bf16[448,256]{1,0:T(8,128)(2,1)}, u32[]{:S(2)}, u32[]{:S(2)}) collective-permute-start(bf16[448,256]{1,0:T(8,128)(2,1)} %get-tuple-element.104), channel_id=1, source_target_pairs={{0,2},{1,3},{2,0},{3,1},{4,6},{5,7},{6,4},{7,5},{8,10},{9,11},{10,... | collective-permute-start | bytes 688136 | tf_op jit(solution)/shard_map/ppermute | solution.py:504
  161.6 25.1 %collective-permute-start.24 = (bf16[256,768]{1,0:T(8,128)(2,1)S(1)}, bf16[256,768]{1,0:T(8,128)(2,1)}, u32[]{:S(2)}, u32[]{:S(2)}) collective-permute-start(bf16[256,768]{1,0:T(8,128)(2,1)S(1)} %broadcast_select_fusion.4), channel_id=1, source_target_pairs={{0,8},{16,24},{1,9},{17,25},{2,10},{18,26},{3,11},{19,27},{4,12},{... | collective-permute-start | bytes 1179656 | tf_op jit(solution)/shard_map/ppermute | solution.py:508
  174.7 27.8 %collective-permute-start.25 = (bf16[2,256,512]{2,1,0:T(8,128)(2,1)S(1)}, bf16[2,256,512]{2,1,0:T(8,128)(2,1)S(1)}, u32[]{:S(2)}, u32[]{:S(2)}) collective-permute-start(bf16[2,256,512]{2,1,0:T(8,128)(2,1)S(1)} %get-tuple-element.99), channel_id=1, source_target_pairs={{16,0},{17,1},{18,8},{19,9},{20,16},{21,17},{22,24},{23,25},{24,2}... | collective-permute-start | bytes 1572872 | tf_op jit(solution)/shard_map/ppermute | solution.py:619
  181.7 24.8 %collective-permute-start.22 = (bf16[2,256,512]{2,1,0:T(8,128)(2,1)S(1)}, bf16[2,256,512]{2,1,0:T(8,128)(2,1)S(1)}, u32[]{:S(2)}, u32[]{:S(2)}) collective-permute-start(bf16[2,256,512]{2,1,0:T(8,128)(2,1)S(1)} %get-tuple-element.100), channel_id=1, source_target_pairs={{0,0},{1,1},{2,8},{3,9},{4,16},{5,17},{6,24},{7,25},{8,2},{9,3},{1... | collective-permute-start | bytes 1572872 | tf_op jit(solution)/shard_map/ppermute | solution.py:619
  184.7 23.1 %collective-permute-start.31 = (bf16[256,256]{1,0:T(8,128)(2,1)S(1)}, bf16[256,256]{1,0:T(8,128)(2,1)S(1)}, u32[]{:S(2)}, u32[]{:S(2)}) collective-permute-start(bf16[256,256]{1,0:T(8,128)(2,1)S(1)} %get-tuple-element.91), channel_id=1, source_target_pairs={{0,16},{1,17},{2,18},{3,19},{4,20},{5,21},{6,22},{7,23}} | collective-permute-start | bytes 393224 | tf_op jit(solution)/shard_map/ppermute | solution.py:507
  185.4 23.8 %collective-permute-start.21 = (bf16[256,256]{1,0:T(8,128)(2,1)S(1)}, bf16[256,256]{1,0:T(8,128)(2,1)S(1)}, u32[]{:S(2)}, u32[]{:S(2)}) collective-permute-start(bf16[256,256]{1,0:T(8,128)(2,1)S(1)} %get-tuple-element.92), channel_id=1, source_target_pairs={{1,0},{3,2},{5,4},{7,6},{9,8},{11,10},{13,12},{15,14},{17,16},{19,... | collective-permute-start | bytes 393224 | tf_op jit(solution)/shard_map/ppermute | solution.py:634
  202.4 23.5 %collective-permute-start.27 = (bf16[2,256,512]{2,1,0:T(8,128)(2,1)S(1)}, bf16[2,256,512]{2,1,0:T(8,128)(2,1)S(1)}, u32[]{:S(2)}, u32[]{:S(2)}) collective-permute-start(bf16[2,256,512]{2,1,0:T(8,128)(2,1)S(1)} %collective-permute-done.25), channel_id=1, source_target_pairs={{0,1},{1,0},{2,3},{3,2},{4,5},{5,4},{6,7},{7,6},{8,9},{9,8},{10,11... | collective-permute-start | bytes 1572872 | tf_op jit(solution)/shard_map/ppermute | solution.py:620
  206.6 18.6 %collective-permute-start.26 = (bf16[2,256,512]{2,1,0:T(8,128)(2,1)S(1)}, bf16[2,256,512]{2,1,0:T(8,128)(2,1)S(1)}, u32[]{:S(2)}, u32[]{:S(2)}) collective-permute-start(bf16[2,256,512]{2,1,0:T(8,128)(2,1)S(1)} %collective-permute-done.22), channel_id=1, source_target_pairs={{0,1},{1,0},{2,3},{3,2},{4,5},{5,4},{6,7},{7,6},{8,9},{9,8},{10,11... | collective-permute-start | bytes 1572872 | tf_op jit(solution)/shard_map/ppermute | solution.py:620
  207.9 30.1 %collective-permute-start.32 = (bf16[256,256]{1,0:T(8,128)(2,1)S(1)}, bf16[256,256]{1,0:T(8,128)(2,1)S(1)}, u32[]{:S(2)}, u32[]{:S(2)}) collective-permute-start(bf16[256,256]{1,0:T(8,128)(2,1)S(1)} %broadcast_select_fusion.6), channel_id=1, source_target_pairs={{0,8},{16,24},{1,9},{17,25},{2,10},{18,26},{3,11},{19,27},{4,12},{... | collective-permute-start | bytes 393224 | tf_op jit(solution)/shard_map/ppermute | solution.py:508
  209.2 28.8 %collective-permute-start.30 = (bf16[2,256,256]{2,1,0:T(8,128)(2,1)S(1)}, bf16[2,256,256]{2,1,0:T(8,128)(2,1)S(1)}, u32[]{:S(2)}, u32[]{:S(2)}) collective-permute-start(bf16[2,256,256]{2,1,0:T(8,128)(2,1)S(1)} %pad_maximum_fusion.10), channel_id=1, source_target_pairs={{6,0},{14,8},{22,16},{30,24}} | collective-permute-start | bytes 786440 | tf_op jit(solution)/shard_map/ppermute | solution.py:636
  209.9 28.1 %collective-permute-start.29 = (bf16[2,256,256]{2,1,0:T(8,128)(2,1)S(1)}, bf16[2,256,256]{2,1,0:T(8,128)(2,1)S(1)}, u32[]{:S(2)}, u32[]{:S(2)}) collective-permute-start(bf16[2,256,256]{2,1,0:T(8,128)(2,1)S(1)} %pad_maximum_fusion.10), channel_id=1, source_target_pairs={{4,0},{12,8},{20,16},{28,24}} | collective-permute-start | bytes 786440 | tf_op jit(solution)/shard_map/ppermute | solution.py:636
  (27 other events, 223.5 us)

commit v7 on v6

--- a/solution.py
+++ b/solution.py
@@ -49,9 +49,10 @@
     return jnp.concatenate([top, low], axis=0)
 
 
-def pack_body(zs, xs, ds, bs, tile, lim_ref, a_ref, o_ref):
-    rows = pl.program_id(0) * tile + lax.broadcasted_iota(jnp.int32, (tile, bs), 0)
-    keep = jnp.where(rows < lim_ref[0], 1.0, 0.0).astype(bf16)
+def pack_body(zs, xs, ds, bs, tile, count_ref, a_ref, o_ref):
+    start = (lax.axis_index("fsdp") * pl.num_programs(0) + pl.program_id(0)) * tile
+    rows = start + lax.broadcasted_iota(jnp.int32, (tile, bs), 0)
+    keep = jnp.where(rows < count_ref[lax.axis_index("dp")], 1.0, 0.0).astype(bf16)
     lead = a_ref[:, :bs] * keep
     for d in range(ds):
         for x in range(xs):
@@ -61,7 +62,7 @@
             o_ref[d * xs + x, zs] = lead
 
 
-def pack(limit, tokens, zs, xs, ds, bs):
+def pack(token_counts, tokens, zs, xs, ds, bs):
     count, width = tokens.shape
     tile = 32
     return pl.pallas_call(
@@ -76,7 +77,7 @@
         cost_estimate=light,
         compiler_params=params("arbitrary"),
         name="pack_tokens",
-    )(limit, tokens)
+    )(token_counts, tokens)
 
 
 def moments_body(ids_ref, x_ref, l_ref, o_ref):
@@ -347,10 +348,11 @@
     cd = c_ref[0, :, :bs]
     cs = c_ref[0, :, bs:]
     third = (dot(cd, s_ref[:, bs:], tn) + dot(cs, l_ref[...], tn)).astype(bf16)
-    fourth = dot(cd, third)
+    pair = dot(jnp.concatenate([cd, cs], axis=0), third)
+    fourth = pair[:bs]
     p_ref[:, bs:] = fourth.astype(bf16)
     is_first = (ids_ref[1] == 0) & (row_of(ids_ref, k) == 0)
-    term = dot(cs, third) + fourth * jnp.where(is_first, 1.0, 0.0)
+    term = pair[bs:] + fourth * jnp.where(is_first, 1.0, 0.0)
 
     @pl.when(k == 0)
     def _():
@@ -405,10 +407,11 @@
         cd = c_ref[k, :, :bs]
         cs = c_ref[k, :, bs:]
         third = (dot(cd, second, tn) + dot(cs, l_ref[...], tn)).astype(bf16)
-        fourth = dot(cd, third)
+        pair = dot(jnp.concatenate([cd, cs], axis=0), third)
+        fourth = pair[:bs]
         p_ref[pl.ds(pl.multiple_of(i * bs, bs), bs), :] = fourth.astype(bf16)
         is_first = (ids_ref[1] == 0) & (i == 0)
-        total = total + dot(cs, third) + fourth * jnp.where(is_first, 1.0, 0.0)
+        total = total + pair[bs:] + fourth * jnp.where(is_first, 1.0, 0.0)
     u_ref[...] = total.astype(bf16)
 
 
@@ -495,9 +498,7 @@
     flip_x = [(i, i ^ 1) for i in range(shards)]
     ids = jnp.stack([z, d, s * ds, s, jnp.int32(ds)]).astype(jnp.int32)
     token_total = jnp.sum(token_counts).astype(f32)
-    valid = jnp.sum(jnp.where(lax.iota(jnp.int32, ds) == d, token_counts, 0))
     stat_scalars = (1.0 / token_total).reshape(1)
-    limit = (valid - s * tok_dev).reshape(1).astype(jnp.int32)
 
     def along_z(value, k):
         pairs = [(zz * xs + xx, (zz ^ k) * xs + xx) for zz in range(zs) for xx in range(xs)]
@@ -551,10 +552,10 @@
         ]
         return lax.ppermute(value, "fsdp", pairs)
 
-    owned_k = exchange(pack(limit, acts, zs, xs, ds, bs))
+    owned_k = exchange(pack(token_counts, acts, zs, xs, ds, bs))
     blocks_c = block_along_z(c_factor)
     own_k = lax.dynamic_slice_in_dim(k_factor, d, 1, 0)
-    packed_c = pack(limit, out_grads, zs, xs, ds, bs)
+    packed_c = pack(token_counts, out_grads, zs, xs, ds, bs)
     gram_k = gram_part(k_factor)
     gram_c = gram_part(c_factor)
     packed_c, owned_k, blocks_c, own_k, gram_k, gram_c = lax.optimization_barrier(

time: 260 us -> 260 us (level)
  starting transfers between devices: 69.2 us -> 66.3 us
    unnamed x25 -> x29, local copies, waits for them, and re-layouts: 7.98 us -> 8.61 us
  transfers between devices with their start and end apart: 40 -> 40, of which waited for: 15 -> 15; matrix products, arithmetic and copies ran while one was open for 12% -> 13% of each run, Pallas kernels for 19% -> 19%
where the time goes in v7:
time: 260 us; the launch traced here: 258 us
  waiting for transfers between devices  90.2 us (35%)
  starting transfers between devices  66.3 us (26%)
  Pallas kernels  52.7 us (20%)
  local copies, waits for them, and re-layouts  22.6 us (9%)
  other arithmetic  21.7 us (8%)
  between operations  4.98 us (2%)
    ppermute x12, waiting for transfers between devices, along_z(): return lax.ppermute(value, 'fsdp', pairs)  22.3 us
    ppermute x2, waiting for transfers between devices, planned(): lax.ppermute(cb[h * (ds // 2):(h + 1) * (ds // 2)], both, pairs)  17.9 us
    ppermute x2, waiting for transfers between devices, down_z(): return lax.ppermute(value, 'fsdp', pairs)  16.6 us
    ppermute x2, waiting for transfers between devices, planned(): others = [lax.ppermute(h, 'fsdp', flip_x) for h in halves]  14.6 us
    ppermute x12, starting transfers between devices, along_z(): return lax.ppermute(value, 'fsdp', pairs)  12.8 us
    pallas_call x2, Pallas kernels, advance_all(): pl.pallas_call(functools.partial(advance_body, width), grid_spec=pltpu.Pr...  11.2 us
    pallas_call x1, Pallas kernels, rows(): pl.pallas_call(rows_body, grid_spec=pltpu.PrefetchScalarGridSpec(num_scal...  10.7 us
    all_to_all x2, starting transfers between devices, exchange(): lax.all_to_all(packed, both, 0, 0, tiled=True, axis_index_groups=plane)  9.3 us
  transfers between devices with their start and end apart: 40, of which 15 were waited for; matrix products, arithmetic and copies ran while one was open for 13% of the time, Pallas kernels for 19%

profile of v7, /device:TPU:17, one launch (start us, length us, event | category | flops | bytes accessed | tf_op | source)
XLA Modules:
  0.0 258.5 jit_solution(14622205137251668251)
XLA Ops:
  5.4 4.4 %all-to-all-start = ((bf16[8,5,128,256]{3,2,1,0:T(8,128)(2,1)}), bf16[8,5,128,256]{3,2,1,0:T(8,128)(2,1)S(1)}, u32[]{:S(2)}, u32[]{:S(2)}) async-start(bf16[8,5,128,256]{3,2,1,0:T(8,128)(2,1)} %copy-done.3), calls=%async_computation | async-start | bytes 5242880 | tf_op jit(solution)/shard_map/all_to_all | solution.py:539
  12.9 3.2 %collective-permute-start.1 = (bf16[256,512]{1,0:T(8,128)(2,1)S(1)}, bf16[256,512]{1,0:T(8,128)(2,1)}, u32[]{:S(2)}, u32[]{:S(2)}) collective-permute-start(bf16[256,512]{1,0:T(8,128)(2,1)S(1)} %pad_maximum_fusion.9), channel_id=1, source_target_pairs={{0,4},{1,5},{2,6},{3,7},{4,0},{5,1},{6,2},{7,3},{8,12},{9,13},{10,... | collective-permute-start | bytes 786440 | tf_op jit(solution)/shard_map/ppermute | solution.py:505
  22.1 3.2 %multiply_reduce_fusion = (f32[]{:T(128)}, f32[]{:T(128)}, f32[]{:T(128)}, f32[]{:T(128)}) fusion(f32[4,256,512]{2,1,0:T(8,128)} %fac_ref.3, f32[4]{0:T(128)S(1)} %compare_convert_fusion, f32[4,256,512]{2,1,0:T(8,128)} %fac_ref.2), kind=kLoop, calls=%fused_computation.4 | loop fusion | flops 2621436 | bytes 4194336 | tf_op jit(solution)/shard_map/reduce_sum | solution.py:536
  28.9 3.1 %collective-permute-done.2 = bf16[256,512]{1,0:T(8,128)(2,1)} collective-permute-done((bf16[256,512]{1,0:T(8,128)(2,1)S(1)}, bf16[256,512]{1,0:T(8,128)(2,1)}, u32[]{:S(2)}, u32[]{:S(2)}) %collective-permute-start.2) | collective-permute-done | bytes 262176 | tf_op jit(solution)/shard_map/ppermute | solution.py:505
  32.0 3.5 %collective-permute-done.1 = bf16[256,512]{1,0:T(8,128)(2,1)} collective-permute-done((bf16[256,512]{1,0:T(8,128)(2,1)S(1)}, bf16[256,512]{1,0:T(8,128)(2,1)}, u32[]{:S(2)}, u32[]{:S(2)}) %collective-permute-start.1) | collective-permute-done | bytes 262176 | tf_op jit(solution)/shard_map/ppermute | solution.py:505
  40.8 3.3 %raw_moments.1 = bf16[4,640,256]{2,1,0:T(8,128)(2,1)S(1)} custom-call(s32[5]{0:T(128)S(1)} %stack.70.ids_ref, bf16[8,5,128,256]{3,2,1,0:T(8,128)(2,1)S(1)} %all-to-all-done.x_ref.l_ref, bf16[8,5,128,256]{3,2,1,0:T(8,128)(2,1)S(1)} %all-to-all-done.x_ref.l_ref), custom_call_target="tpu_custom_call" | custom-call | flops 1 | bytes 1 | tf_op jit(solution)/shard_map/raw_moments/pallas_call | solution.py:96
  45.2 3.2 %collective-permute-start.4 = (bf16[640,256]{1,0:T(8,128)(2,1)}, bf16[640,256]{1,0:T(8,128)(2,1)}, u32[]{:S(2)}, u32[]{:S(2)}) collective-permute-start(bf16[640,256]{1,0:T(8,128)(2,1)} %get-tuple-element.94), channel_id=1, source_target_pairs={{0,4},{1,5},{2,6},{3,7},{4,0},{5,1},{6,2},{7,3},{8,12},{9,13},{10,... | collective-permute-start | bytes 983048 | tf_op jit(solution)/shard_map/ppermute | solution.py:505
  52.5 4.9 %all-to-all-start.1 = ((bf16[8,5,128,256]{3,2,1,0:T(8,128)(2,1)}), bf16[8,5,128,256]{3,2,1,0:T(8,128)(2,1)S(1)}, u32[]{:S(2)}, u32[]{:S(2)}) async-start(bf16[8,5,128,256]{3,2,1,0:T(8,128)(2,1)} %copy-done.2), calls=%async_computation.1 | async-start | bytes 5242880 | tf_op jit(solution)/shard_map/all_to_all | solution.py:539
  57.4 10.4 %collective-permute-done.5.refs_3_ = bf16[640,256]{1,0:T(8,128)(2,1)} collective-permute-done((bf16[640,256]{1,0:T(8,128)(2,1)}, bf16[640,256]{1,0:T(8,128)(2,1)}, u32[]{:S(2)}, u32[]{:S(2)}) %collective-permute-start.5) | collective-permute-done | bytes 327712 | tf_op jit(solution)/shard_map/ppermute | solution.py:505
  67.9 5.3 %collective-permute-done.4.refs_2_ = bf16[640,256]{1,0:T(8,128)(2,1)} collective-permute-done((bf16[640,256]{1,0:T(8,128)(2,1)}, bf16[640,256]{1,0:T(8,128)(2,1)}, u32[]{:S(2)}, u32[]{:S(2)}) %collective-permute-start.4) | collective-permute-done | bytes 327712 | tf_op jit(solution)/shard_map/ppermute | solution.py:505
  76.7 16.6 %collective-permute-done.9 = bf16[1280,256]{1,0:T(8,128)(2,1)} collective-permute-done((bf16[1280,256]{1,0:T(8,128)(2,1)}, bf16[1280,256]{1,0:T(8,128)(2,1)}, u32[]{:S(2)}, u32[]{:S(2)}) %collective-permute-start.9) | collective-permute-done | bytes 655392 | tf_op jit(solution)/shard_map/ppermute | solution.py:553
  99.3 4.3 %image_stats.1 = (bf16[448,256]{1,0:T(8,128)(2,1)S(1)}, f32[8,128]{1,0:T(8,128)S(1)}) custom-call(s32[5]{0:T(128)S(1)} %stack.70.ids_ref, f32[1]{0:T(128)} %bitcast.4.sc_ref, bf16[640,256]{1,0:T(8,128)(2,1)S(1)} %get-tuple-element.96.refs_0_, bf16[640,256]{1,0:T(8,128)(2,1)} %collective-permute-done.3.refs_1_, ...), custom_call_target="tpu_custom_call" | custom-call | flops 1 | bytes 1 | tf_op jit(solution)/shard_map/image_stats/pallas_call | solution.py:143
  105.5 5.8 %plane_stats.1 = (bf16[4,448,256]{2,1,0:T(8,128)(2,1)S(1)}, f32[8,128]{1,0:T(8,128)S(1)}) custom-call(s32[5]{0:T(128)S(1)} %stack.70.ids_ref, bf16[8,5,128,256]{3,2,1,0:T(8,128)(2,1)S(1)} %all-to-all-done.1.refs_0_.refs_1_, bf16[8,5,128,256]{3,2,1,0:T(8,128)(2,1)S(1)} %all-to-all-done.1.refs_0_.refs_1_, bf16[4,256,512]{2,1,0:T(8,128)(2,1)S(1)} %copy-done.4), custom_call_target="tpu_custom_call" | custom-call | flops 1 | bytes 1 | tf_op jit(solution)/shard_map/plane_stats/pallas_call | solution.py:188
  113.6 7.6 %all-to-all-start.2 = ((f32[32,8,128]{2,1,0:T(8,128)}), f32[32,8,128]{2,1,0:T(8,128)S(1)}, u32[]{:S(2)}, u32[]{:S(2)}) async-start(f32[32,8,128]{2,1,0:T(8,128)} %broadcast_in_dim.18), calls=%async_computation.2 | async-start | bytes 262144 | tf_op jit(solution)/shard_map/all_to_all | solution.py:586
  136.9 5.6 %advance_all.2 = (f32[4,256,512]{2,1,0:T(8,128)}, f32[4,256,512]{2,1,0:T(8,128)}, bf16[4,256,512]{2,1,0:T(8,128)(2,1)S(1)}) custom-call(s32[5]{0:T(128)S(1)} %stack.70.ids_ref, f32[2]{0:T(128)S(1)} %pad_maximum_fusion.11.sc_ref, bf16[4,448,256]{2,1,0:T(8,128)(2,1)S(1)} %pad_maximum_fusion.3.h_ref, f32[4,256,512]{2,1,0:T(8,128)S(1)} %copy-done, ...), custom_call_target="tpu_custom_call" | custom-call | flops 1 | bytes 1 | tf_op jit(solution)/shard_map/advance_all/pallas_call | solution.py:264
  142.5 8.7 %column_products.1 = (bf16[2048,1024]{1,0:T(8,128)(2,1)}, bf16[2048,256]{1,0:T(8,128)(2,1)S(1)}) custom-call(s32[5]{0:T(128)S(1)} %stack.70.ids_ref, bf16[2048,1024]{1,0:T(8,128)(2,1)} %g_ref.1, bf16[2048,256]{1,0:T(8,128)(2,1)S(1)} %pad_maximum_fusion.l_ref, bf16[4,256,512]{2,1,0:T(8,128)(2,1)S(1)} %get-tuple-element.59.k_ref), custom_call_target="tpu_custom_call" | custom-call | flops 1 | bytes 1 | tf_op jit(solution)/shard_map/column_products/pallas_call | solution.py:310
  168.3 5.6 %advance_all.3 = (f32[4,256,512]{2,1,0:T(8,128)}, f32[4,256,512]{2,1,0:T(8,128)}, bf16[4,256,512]{2,1,0:T(8,128)(2,1)S(1)}) custom-call(s32[5]{0:T(128)S(1)} %stack.70.ids_ref, f32[2]{0:T(128)S(1)} %pad_maximum_fusion.12.sc_ref, bf16[4,448,256]{2,1,0:T(8,128)(2,1)S(1)} %pad_maximum_fusion.4.h_ref, f32[4,256,512]{2,1,0:T(8,128)S(1)} %copy-done.1, ...), custom_call_target="tpu_custom_call" | custom-call | flops 1 | bytes 1 | tf_op jit(solution)/shard_map/advance_all/pallas_call | solution.py:264
  174.0 7.1 %collective-permute-start.25 = (bf16[2,256,512]{2,1,0:T(8,128)(2,1)S(1)}, bf16[2,256,512]{2,1,0:T(8,128)(2,1)S(1)}, u32[]{:S(2)}, u32[]{:S(2)}) collective-permute-start(bf16[2,256,512]{2,1,0:T(8,128)(2,1)S(1)} %get-tuple-element.97), channel_id=1, source_target_pairs={{16,0},{17,1},{18,8},{19,9},{20,16},{21,17},{22,24},{23,25},{24,2}... | collective-permute-start | bytes 1572872 | tf_op jit(solution)/shard_map/ppermute | solution.py:620
  187.1 14.9 %collective-permute-done.25 = bf16[2,256,512]{2,1,0:T(8,128)(2,1)S(1)} collective-permute-done((bf16[2,256,512]{2,1,0:T(8,128)(2,1)S(1)}, bf16[2,256,512]{2,1,0:T(8,128)(2,1)S(1)}, u32[]{:S(2)}, u32[]{:S(2)}) %collective-permute-start.25) | collective-permute-done | bytes 524320 | tf_op jit(solution)/shard_map/ppermute | solution.py:620
  210.6 14.6 %collective-permute-done.26 = bf16[2,256,512]{2,1,0:T(8,128)(2,1)S(1)} collective-permute-done((bf16[2,256,512]{2,1,0:T(8,128)(2,1)S(1)}, bf16[2,256,512]{2,1,0:T(8,128)(2,1)S(1)}, u32[]{:S(2)}, u32[]{:S(2)}) %collective-permute-start.26) | collective-permute-done | bytes 524320 | tf_op jit(solution)/shard_map/ppermute | solution.py:621
  226.0 10.7 %row_products.1 = (bf16[2048,1024]{1,0:T(8,128)(2,1)}, bf16[256,768]{1,0:T(8,128)(2,1)S(1)}) custom-call(s32[5]{0:T(128)S(1)} %stack.70.ids_ref, bf16[2048,1024]{1,0:T(8,128)(2,1)} %get-tuple-element.68.s_ref, bf16[256,768]{1,0:T(8,128)(2,1)S(1)} %broadcast_select_fusion.5.l_ref, bf16[8,256,512]{2,1,0:T(8,128)(2,1)S(1)} %constant_dynamic-update-slice_fusion.c_ref), custom_call_target="tpu_custom_call" | custom-call | flops 1 | bytes 1 | tf_op jit(solution)/shard_map/row_products/pallas_call | solution.py:376
  238.2 4.2 %lead_row_products.1 = (bf16[2048,1024]{1,0:T(8,128)(2,1)}, bf16[256,256]{1,0:T(8,128)(2,1)S(1)}) custom-call(s32[5]{0:T(128)S(1)} %stack.70.ids_ref, bf16[2048,1024]{1,0:T(8,128)(2,1)} %get-tuple-element.68.s_ref, bf16[2048,256]{1,0:T(8,128)(2,1)S(1)} %bitcast.52, ...), custom_call_target="tpu_custom_call", output_to_operand_aliasing={{0}: (5, {})} | custom-call | flops 1 | bytes 1 | tf_op jit(solution)/shard_map/lead_row_products/pallas_call | solution.py:423
  243.7 5.6 %collective-permute-done.35 = bf16[256,768]{1,0:T(8,128)(2,1)S(1)} collective-permute-done((bf16[256,768]{1,0:T(8,128)(2,1)S(1)}, bf16[256,768]{1,0:T(8,128)(2,1)S(1)}, u32[]{:S(2)}, u32[]{:S(2)}) %collective-permute-start.35) | collective-permute-done | bytes 393248 | tf_op jit(solution)/shard_map/ppermute | solution.py:641
  249.4 3.2 %collective-permute-start.36 = (bf16[256,768]{1,0:T(8,128)(2,1)S(1)}, bf16[256,768]{1,0:T(8,128)(2,1)S(1)}, u32[]{:S(2)}, u32[]{:S(2)}) collective-permute-start(bf16[256,768]{1,0:T(8,128)(2,1)S(1)} %fusion), channel_id=1, source_target_pairs={{8,0},{9,1},{10,2},{11,3},{12,4},{13,5},{14,6},{15,7}} | collective-permute-start | bytes 1179656 | tf_op jit(solution)/shard_map/ppermute | solution.py:642
  (147 shorter events, 94.5 us)
Async XLA Ops:
  5.4 35.4 %all-to-all-start = ((bf16[8,5,128,256]{3,2,1,0:T(8,128)(2,1)}), bf16[8,5,128,256]{3,2,1,0:T(8,128)(2,1)S(1)}, u32[]{:S(2)}, u32[]{:S(2)}) async-start(bf16[8,5,128,256]{3,2,1,0:T(8,128)(2,1)} %copy-done.3), calls=%async_computation | async-start | bytes 5242880 | tf_op jit(solution)/shard_map/all_to_all | solution.py:539
  12.7 19.3 %collective-permute-start.2 = (bf16[256,512]{1,0:T(8,128)(2,1)S(1)}, bf16[256,512]{1,0:T(8,128)(2,1)}, u32[]{:S(2)}, u32[]{:S(2)}) collective-permute-start(bf16[256,512]{1,0:T(8,128)(2,1)S(1)} %pad_maximum_fusion.9), channel_id=1, source_target_pairs={{0,6},{1,7},{2,4},{3,5},{4,2},{5,3},{6,0},{7,1},{8,14},{9,15},{10,... | collective-permute-start | bytes 786440 | tf_op jit(solution)/shard_map/ppermute | solution.py:505
  12.9 22.6 %collective-permute-start.1 = (bf16[256,512]{1,0:T(8,128)(2,1)S(1)}, bf16[256,512]{1,0:T(8,128)(2,1)}, u32[]{:S(2)}, u32[]{:S(2)}) collective-permute-start(bf16[256,512]{1,0:T(8,128)(2,1)S(1)} %pad_maximum_fusion.9), channel_id=1, source_target_pairs={{0,4},{1,5},{2,6},{3,7},{4,0},{5,1},{6,2},{7,3},{8,12},{9,13},{10,... | collective-permute-start | bytes 786440 | tf_op jit(solution)/shard_map/ppermute | solution.py:505
  16.1 19.4 %collective-permute-start = (bf16[256,512]{1,0:T(8,128)(2,1)S(1)}, bf16[256,512]{1,0:T(8,128)(2,1)}, u32[]{:S(2)}, u32[]{:S(2)}) collective-permute-start(bf16[256,512]{1,0:T(8,128)(2,1)S(1)} %pad_maximum_fusion.9), channel_id=1, source_target_pairs={{0,2},{1,3},{2,0},{3,1},{4,6},{5,7},{6,4},{7,5},{8,10},{9,11},{10,... | collective-permute-start | bytes 786440 | tf_op jit(solution)/shard_map/ppermute | solution.py:505
  18.1 39.3 %collective-permute-start.8 = (bf16[1280,256]{1,0:T(8,128)(2,1)}, bf16[1280,256]{1,0:T(8,128)(2,1)}, u32[]{:S(2)}, u32[]{:S(2)}) collective-permute-start(bf16[1280,256]{1,0:T(8,128)(2,1)} %slice.126), channel_id=1, source_target_pairs={{0,1},{8,9},{16,17},{24,25}} | collective-permute-start | bytes 1966088 | tf_op jit(solution)/shard_map/ppermute | solution.py:545
  45.1 22.8 %collective-permute-start.5 = (bf16[640,256]{1,0:T(8,128)(2,1)}, bf16[640,256]{1,0:T(8,128)(2,1)}, u32[]{:S(2)}, u32[]{:S(2)}) collective-permute-start(bf16[640,256]{1,0:T(8,128)(2,1)} %get-tuple-element.93), channel_id=1, source_target_pairs={{0,6},{1,7},{2,4},{3,5},{4,2},{5,3},{6,0},{7,1},{8,14},{9,15},{10,... | collective-permute-start | bytes 983048 | tf_op jit(solution)/shard_map/ppermute | solution.py:505
  45.2 27.9 %collective-permute-start.4 = (bf16[640,256]{1,0:T(8,128)(2,1)}, bf16[640,256]{1,0:T(8,128)(2,1)}, u32[]{:S(2)}, u32[]{:S(2)}) collective-permute-start(bf16[640,256]{1,0:T(8,128)(2,1)} %get-tuple-element.94), channel_id=1, source_target_pairs={{0,4},{1,5},{2,6},{3,7},{4,0},{5,1},{6,2},{7,3},{8,12},{9,13},{10,... | collective-permute-start | bytes 983048 | tf_op jit(solution)/shard_map/ppermute | solution.py:505
  48.5 24.7 %collective-permute-start.3 = (bf16[640,256]{1,0:T(8,128)(2,1)}, bf16[640,256]{1,0:T(8,128)(2,1)}, u32[]{:S(2)}, u32[]{:S(2)}) collective-permute-start(bf16[640,256]{1,0:T(8,128)(2,1)} %get-tuple-element.95), channel_id=1, source_target_pairs={{0,2},{1,3},{2,0},{3,1},{4,6},{5,7},{6,4},{7,5},{8,10},{9,11},{10,... | collective-permute-start | bytes 983048 | tf_op jit(solution)/shard_map/ppermute | solution.py:505
  52.5 51.8 %all-to-all-start.1 = ((bf16[8,5,128,256]{3,2,1,0:T(8,128)(2,1)}), bf16[8,5,128,256]{3,2,1,0:T(8,128)(2,1)S(1)}, u32[]{:S(2)}, u32[]{:S(2)}) async-start(bf16[8,5,128,256]{3,2,1,0:T(8,128)(2,1)} %copy-done.2), calls=%async_computation.1 | async-start | bytes 5242880 | tf_op jit(solution)/shard_map/all_to_all | solution.py:539
  112.6 21.5 %collective-permute-start.11 = (bf16[1280,256]{1,0:T(8,128)(2,1)S(1)}, bf16[1280,256]{1,0:T(8,128)(2,1)}, u32[]{:S(2)}, u32[]{:S(2)}) collective-permute-start(bf16[1280,256]{1,0:T(8,128)(2,1)S(1)} %broadcast_select_fusion.1), channel_id=1, source_target_pairs={{0,1},{1,0},{2,3},{3,2},{4,5},{5,4},{6,7},{7,6},{8,9},{9,8},{10,11... | collective-permute-start | bytes 1966088 | tf_op jit(solution)/shard_map/ppermute | solution.py:591
  113.6 18.5 %all-to-all-start.2 = ((f32[32,8,128]{2,1,0:T(8,128)}), f32[32,8,128]{2,1,0:T(8,128)S(1)}, u32[]{:S(2)}, u32[]{:S(2)}) async-start(f32[32,8,128]{2,1,0:T(8,128)} %broadcast_in_dim.18), calls=%async_computation.2 | async-start | bytes 262144 | tf_op jit(solution)/shard_map/all_to_all | solution.py:586
  123.4 27.8 %collective-permute-start.14 = (bf16[448,256]{1,0:T(8,128)(2,1)}, bf16[448,256]{1,0:T(8,128)(2,1)S(1)}, u32[]{:S(2)}, u32[]{:S(2)}) collective-permute-start(bf16[448,256]{1,0:T(8,128)(2,1)} %get-tuple-element.100), channel_id=1, source_target_pairs={{0,6},{1,7},{2,4},{3,5},{4,2},{5,3},{6,0},{7,1},{8,14},{9,15},{10,... | collective-permute-start | bytes 688136 | tf_op jit(solution)/shard_map/ppermute | solution.py:505
  123.7 27.5 %collective-permute-start.13 = (bf16[448,256]{1,0:T(8,128)(2,1)}, bf16[448,256]{1,0:T(8,128)(2,1)}, u32[]{:S(2)}, u32[]{:S(2)}) collective-permute-start(bf16[448,256]{1,0:T(8,128)(2,1)} %get-tuple-element.101), channel_id=1, source_target_pairs={{0,4},{1,5},{2,6},{3,7},{4,0},{5,1},{6,2},{7,3},{8,12},{9,13},{10,... | collective-permute-start | bytes 688136 | tf_op jit(solution)/shard_map/ppermute | solution.py:505
  126.7 24.4 %collective-permute-start.12 = (bf16[448,256]{1,0:T(8,128)(2,1)}, bf16[448,256]{1,0:T(8,128)(2,1)}, u32[]{:S(2)}, u32[]{:S(2)}) collective-permute-start(bf16[448,256]{1,0:T(8,128)(2,1)} %get-tuple-element.102), channel_id=1, source_target_pairs={{0,2},{1,3},{2,0},{3,1},{4,6},{5,7},{6,4},{7,5},{8,10},{9,11},{10,... | collective-permute-start | bytes 688136 | tf_op jit(solution)/shard_map/ppermute | solution.py:505
  161.6 24.4 %collective-permute-start.24 = (bf16[256,768]{1,0:T(8,128)(2,1)S(1)}, bf16[256,768]{1,0:T(8,128)(2,1)}, u32[]{:S(2)}, u32[]{:S(2)}) collective-permute-start(bf16[256,768]{1,0:T(8,128)(2,1)S(1)} %broadcast_select_fusion.4), channel_id=1, source_target_pairs={{0,8},{16,24},{1,9},{17,25},{2,10},{18,26},{3,11},{19,27},{4,12},{... | collective-permute-start | bytes 1179656 | tf_op jit(solution)/shard_map/ppermute | solution.py:509
  174.0 28.0 %collective-permute-start.25 = (bf16[2,256,512]{2,1,0:T(8,128)(2,1)S(1)}, bf16[2,256,512]{2,1,0:T(8,128)(2,1)S(1)}, u32[]{:S(2)}, u32[]{:S(2)}) collective-permute-start(bf16[2,256,512]{2,1,0:T(8,128)(2,1)S(1)} %get-tuple-element.97), channel_id=1, source_target_pairs={{16,0},{17,1},{18,8},{19,9},{20,16},{21,17},{22,24},{23,25},{24,2}... | collective-permute-start | bytes 1572872 | tf_op jit(solution)/shard_map/ppermute | solution.py:620
  181.1 24.8 %collective-permute-start.22 = (bf16[2,256,512]{2,1,0:T(8,128)(2,1)S(1)}, bf16[2,256,512]{2,1,0:T(8,128)(2,1)S(1)}, u32[]{:S(2)}, u32[]{:S(2)}) collective-permute-start(bf16[2,256,512]{2,1,0:T(8,128)(2,1)S(1)} %get-tuple-element.98), channel_id=1, source_target_pairs={{0,0},{1,1},{2,8},{3,9},{4,16},{5,17},{6,24},{7,25},{8,2},{9,3},{1... | collective-permute-start | bytes 1572872 | tf_op jit(solution)/shard_map/ppermute | solution.py:620
  184.0 23.1 %collective-permute-start.31 = (bf16[256,256]{1,0:T(8,128)(2,1)S(1)}, bf16[256,256]{1,0:T(8,128)(2,1)S(1)}, u32[]{:S(2)}, u32[]{:S(2)}) collective-permute-start(bf16[256,256]{1,0:T(8,128)(2,1)S(1)} %get-tuple-element.89), channel_id=1, source_target_pairs={{0,16},{1,17},{2,18},{3,19},{4,20},{5,21},{6,22},{7,23}} | collective-permute-start | bytes 393224 | tf_op jit(solution)/shard_map/ppermute | solution.py:508
  184.7 23.8 %collective-permute-start.21 = (bf16[256,256]{1,0:T(8,128)(2,1)S(1)}, bf16[256,256]{1,0:T(8,128)(2,1)S(1)}, u32[]{:S(2)}, u32[]{:S(2)}) collective-permute-start(bf16[256,256]{1,0:T(8,128)(2,1)S(1)} %get-tuple-element.90), channel_id=1, source_target_pairs={{1,0},{3,2},{5,4},{7,6},{9,8},{11,10},{13,12},{15,14},{17,16},{19,... | collective-permute-start | bytes 393224 | tf_op jit(solution)/shard_map/ppermute | solution.py:635
  201.9 24.0 %collective-permute-start.27 = (bf16[2,256,512]{2,1,0:T(8,128)(2,1)S(1)}, bf16[2,256,512]{2,1,0:T(8,128)(2,1)S(1)}, u32[]{:S(2)}, u32[]{:S(2)}) collective-permute-start(bf16[2,256,512]{2,1,0:T(8,128)(2,1)S(1)} %collective-permute-done.25), channel_id=1, source_target_pairs={{0,1},{1,0},{2,3},{3,2},{4,5},{5,4},{6,7},{7,6},{8,9},{9,8},{10,11... | collective-permute-start | bytes 1572872 | tf_op jit(solution)/shard_map/ppermute | solution.py:621
  205.9 19.3 %collective-permute-start.26 = (bf16[2,256,512]{2,1,0:T(8,128)(2,1)S(1)}, bf16[2,256,512]{2,1,0:T(8,128)(2,1)S(1)}, u32[]{:S(2)}, u32[]{:S(2)}) collective-permute-start(bf16[2,256,512]{2,1,0:T(8,128)(2,1)S(1)} %collective-permute-done.22), channel_id=1, source_target_pairs={{0,1},{1,0},{2,3},{3,2},{4,5},{5,4},{6,7},{7,6},{8,9},{9,8},{10,11... | collective-permute-start | bytes 1572872 | tf_op jit(solution)/shard_map/ppermute | solution.py:621
  207.2 30.8 %collective-permute-start.32 = (bf16[256,256]{1,0:T(8,128)(2,1)S(1)}, bf16[256,256]{1,0:T(8,128)(2,1)S(1)}, u32[]{:S(2)}, u32[]{:S(2)}) collective-permute-start(bf16[256,256]{1,0:T(8,128)(2,1)S(1)} %broadcast_select_fusion.6), channel_id=1, source_target_pairs={{0,8},{16,24},{1,9},{17,25},{2,10},{18,26},{3,11},{19,27},{4,12},{... | collective-permute-start | bytes 393224 | tf_op jit(solution)/shard_map/ppermute | solution.py:509
  208.5 29.5 %collective-permute-start.30 = (bf16[2,256,256]{2,1,0:T(8,128)(2,1)S(1)}, bf16[2,256,256]{2,1,0:T(8,128)(2,1)S(1)}, u32[]{:S(2)}, u32[]{:S(2)}) collective-permute-start(bf16[2,256,256]{2,1,0:T(8,128)(2,1)S(1)} %pad_maximum_fusion.10), channel_id=1, source_target_pairs={{6,0},{14,8},{22,16},{30,24}} | collective-permute-start | bytes 786440 | tf_op jit(solution)/shard_map/ppermute | solution.py:637
  209.2 28.8 %collective-permute-start.29 = (bf16[2,256,256]{2,1,0:T(8,128)(2,1)S(1)}, bf16[2,256,256]{2,1,0:T(8,128)(2,1)S(1)}, u32[]{:S(2)}, u32[]{:S(2)}) collective-permute-start(bf16[2,256,256]{2,1,0:T(8,128)(2,1)S(1)} %pad_maximum_fusion.10), channel_id=1, source_target_pairs={{4,0},{12,8},{20,16},{28,24}} | collective-permute-start | bytes 786440 | tf_op jit(solution)/shard_map/ppermute | solution.py:637
  (29 other events, 233.2 us)
